TPU v7x, 512 devices: a whole 4x4x16 slice. The times are simulated.
512 devices in a mesh: user: 128 (over z, y, core), ad: 4 (over x).
Axes of the slice: x: 4, y: 4, z: 16, core: 2. Of those that a mesh axis runs over, the one named last changes fastest.
Arguments:
- user_embedding: bfloat16 [32768, 128], P('user'), may hold values from -6 to 6
- user_scale: float32 [32768], P('user'), may hold values from 0.5 to 2
- user_mass: float32 [32768], P('user'), may hold values from 0.2 to 5
- ad_embedding: bfloat16 [16384, 128], P('ad'), may hold values from -6 to 6
- ad_scale: float32 [16384], P('ad'), may hold values from 0.5 to 2
- listing_view_demand: float32 [16384], P('ad'), may hold values from 0.2 to 5
- listing_unplaced_penalty: float32 [16384], P('ad'), may hold values from -2 to 2
- campaign_dual_vector_initial: float32 [16384], P(('ad', 'user')), may hold values from -6 to 6
- eligible: int32 [128, 4, 4], P('user', 'ad'), may hold values from 0 to 3, as said below
- counts: int32 [128, 4], P('user', 'ad'), may hold values from 1 to 4, as said below
Outputs:
- closing_viewer_scaling: float32 [32768], P('user')
- campaign_dual_vector_after: float32 [16384], P(('ad', 'user'))
Inputs may be any that keep to these rules, and one draw needn't show every extreme that they name: The used entries of one list eligible[b, j, :] are distinct, and so are all 4 entries. `counts`: some pair (b, j) uses all 4 slots.
All inputs are finite; a program needn't handle non-finite values.
Results may differ from a plain program's by a relative error of at most 0.0003.
Values sent between devices are 32-bit elements; how exact they have to be, the bound alone decides.
No kernel may reach another device: no remote copies, remote signals or barrier semaphores. Data moves between devices by JAX's collectives and lax.ppermute only.
A program may use at most 64 MiB of HBM per device.

v0:
```python
import math

import jax
import jax.numpy as jnp
from jax import lax
from jax.sharding import PartitionSpec as P

ADS_IN_PART = 1024
KMAX = 4
ITERS = 2


regularizer_epsilon = 0.1
very_low = -1e30


def joined(value, axis, combine):
    everything = jax.tree.map(lambda part: lax.all_gather(part, axis), value)
    first = jax.tree.map(lambda part: part[0], everything)

    def hop(k, so_far):
        return combine(so_far, jax.tree.map(lambda part: part[k], everything))

    return lax.fori_loop(1, lax.axis_size(axis), hop, first)


def pair_combine(first, second):
    ongoing_largest = jnp.maximum(first[0], second[0])
    return (
        ongoing_largest,
        first[1] * jnp.exp(first[0] - ongoing_largest)
        + second[1] * jnp.exp(second[0] - ongoing_largest),
    )


def on_device(
    user_embedding,
    user_scale,
    user_mass,
    ad_embedding,
    ad_scale,
    listing_view_demand,
    listing_unplaced_penalty,
    campaign_dual_vector_initial,
    eligible,
    counts,
):
    row_count = user_embedding.shape[0]
    group_ads = ad_embedding.shape[0]
    local_quantity = campaign_dual_vector_initial.shape[0]
    inverse_root = 1.0 / math.sqrt(user_embedding.shape[1])
    partition_sequence = eligible[0, 0]
    active_count = counts[0, 0]
    log_weight_share = jnp.log(user_mass)
    stacked_factors = lax.all_gather(campaign_dual_vector_initial, "user", axis=0, tiled=True)
    local_starting_position = lax.axis_index("user") * local_quantity
    closing_viewer_scaling = jnp.zeros((row_count,), jnp.float32)
    campaign_dual_vector_after = campaign_dual_vector_initial
    for sweep in range(ITERS):
        source_largest_entry = jnp.full((row_count,), very_low, jnp.float32)
        source_exponent_accum = jnp.zeros((row_count,), jnp.float32)
        col_peak = jnp.full((group_ads,), very_low, jnp.float32)
        col_total = jnp.zeros((group_ads,), jnp.float32)
        tile_blocks = []
        for partition_index in range(KMAX):
            tile_offset = partition_sequence[partition_index] * ADS_IN_PART
            ad_rows = lax.dynamic_slice_in_dim(ad_embedding, tile_offset, ADS_IN_PART, 0)
            ad_rowscale = lax.dynamic_slice_in_dim(ad_scale, tile_offset, ADS_IN_PART, 0)
            product = lax.dot_general(
                user_embedding,
                ad_rows,
                (((1,), (1,)), ((), ())),
                preferred_element_type=jnp.float32,
            )
            shipping_price = -(user_scale[:, None] * ad_rowscale[None, :]) * (
                product * inverse_root
            )
            tile_blocks.append(shipping_price)
            target_side_scaling = lax.dynamic_slice_in_dim(
                stacked_factors, partition_sequence[partition_index] * ADS_IN_PART, ADS_IN_PART, 0
            )
            affinity_table_entries = (
                target_side_scaling[None, :] - shipping_price
            ) / regularizer_epsilon
            tile_peak = jnp.max(affinity_table_entries, axis=1)
            tile_total = jnp.sum(jnp.exp(affinity_table_entries - tile_peak[:, None]), axis=1)
            new_peak, new_total = pair_combine(
                (source_largest_entry, source_exponent_accum), (tile_peak, tile_total)
            )
            active = partition_index < active_count
            source_largest_entry = jnp.where(active, new_peak, source_largest_entry)
            source_exponent_accum = jnp.where(active, new_total, source_exponent_accum)
        source_largest_entry, source_exponent_accum = joined(
            (source_largest_entry, source_exponent_accum), "ad", pair_combine
        )
        closing_viewer_scaling = regularizer_epsilon * log_weight_share - regularizer_epsilon * (
            source_largest_entry + jnp.log(source_exponent_accum)
        )
        for partition_index in range(KMAX):
            column_affinity_table_entries = (
                closing_viewer_scaling[:, None] - tile_blocks[partition_index]
            ) / regularizer_epsilon
            column_tile_peak = jnp.max(column_affinity_table_entries, axis=0)
            column_tile_total = jnp.sum(
                jnp.exp(column_affinity_table_entries - column_tile_peak[None, :]), axis=0
            )
            tile_peak = column_tile_peak
            tile_total = column_tile_total
            active = partition_index < active_count
            tile_peak = jnp.where(active, tile_peak, very_low)
            tile_total = jnp.where(active, tile_total, 0.0)
            offset = partition_sequence[partition_index] * ADS_IN_PART
            col_peak = lax.dynamic_update_slice_in_dim(col_peak, tile_peak, offset, 0)
            col_total = lax.dynamic_update_slice_in_dim(col_total, tile_total, offset, 0)
        ongoing_largest, ongoing_accumulation = joined((col_peak, col_total), "user", pair_combine)
        fallback_affinity_level = -listing_unplaced_penalty / regularizer_epsilon
        ongoing_largest, ongoing_accumulation = pair_combine(
            (ongoing_largest, ongoing_accumulation),
            (fallback_affinity_level, jnp.ones_like(fallback_affinity_level)),
        )
        stacked_factors = regularizer_epsilon * jnp.log(
            listing_view_demand
        ) - regularizer_epsilon * (ongoing_largest + jnp.log(ongoing_accumulation))
        campaign_dual_vector_after = lax.dynamic_slice_in_dim(
            stacked_factors, local_starting_position, local_quantity, 0
        )
    return (closing_viewer_scaling, campaign_dual_vector_after)


def solution(mesh):
    in_specs = (
        P("user", None),
        P("user"),
        P("user"),
        P("ad", None),
        P("ad"),
        P("ad"),
        P("ad"),
        P(("ad", "user")),
        P("user", "ad", None),
        P("user", "ad"),
    )
    out_specs = (P("user"), P(("ad", "user")))
    return jax.shard_map(
        on_device, mesh=mesh, in_specs=in_specs, out_specs=out_specs, check_vma=False
    )
```

profile of v0, /device:TPU:1, one launch (start us, length us, event | category | flops | bytes accessed | tf_op | source)
XLA Modules:
  0.0 1386.3 jit_solution(9052609408661725676)
XLA Ops:
  7.3 1.5 fusion.45
  12.0 1.3 dynamic-slice
  14.8 498.1 %all-reduce = f32[4096]{0:T(1024)S(1)} all-reduce(f32[4096]{0:T(1024)S(1)} %dynamic-update-slice), channel_id=1, replica_groups=mesh['user'=128,'ad'=4] {'user'}, use_global_device_ids=true, to_apply=%add | all-reduce | flops 4096 | bytes 32768
  513.6 1.3 fusion.11
  517.5 7.7 all-gather
  525.2 5.2 all-gather.1
  532.1 1.1 exponential_reduce_fusion.8
  534.1 2.2 exponential_reduce_fusion.9
  537.1 137.6 %all-gather.13.cloned.1.call-done = f32[128,1,4096]{2,1,0:T(1,128)} async-done(((f32[1,1,4096]{2,1,0:T(1,128)}), f32[128,1,4096]{2,1,0:T(1,128)}) %all-gather.13.cloned.1.call-update) | async-done | bytes 2097168 | tf_op jit(solution)/shard_map/all_gather | solution.py:18
  674.6 4.5 copy.31
  679.2 134.7 %all-gather.15.cloned.1.call-done = f32[128,1,4096]{2,1,0:T(1,128)} async-done(((f32[1,1,4096]{2,1,0:T(1,128)}), f32[128,1,4096]{2,1,0:T(1,128)}) %all-gather.15.cloned.1.call-update) | async-done | bytes 2097168 | tf_op jit(solution)/shard_map/all_gather | solution.py:18
  813.9 4.6 copy.30
  818.5 132.9 %while.69 = (s32[]{:T(128)}, f32[4096]{0:T(1024)S(1)}, f32[4096]{0:T(1024)S(1)}, f32[128,4096]{1,0:T(8,128)}, f32[128,4096]{1,0:T(8,128)}, /*index=5*/s32[]{:T(128)}, s32[]{:T(128)}, s32[]{:T(128)}) while((s32[]{:T(128)}, f32[4096]{0:T(1024)S(1)}, f32[4096]{0:T(1024)S(1)}, f32[128,4096]{1,0:T(8,128)}, f32[128,4096]{1,0:T(8,128)}, ...), condition=%wide.region_19.20_spmd, body=%wide.region_18.19_spmd.sunk | while | flops 24581 | bytes 163971 | solution.py:24
  820.6 1.0 constant_dynamic-slice_fusion.13
  821.6 1.0 constant_dynamic-slice_fusion.13
  822.7 1.0 constant_dynamic-slice_fusion.13
  825.8 1.0 constant_dynamic-slice_fusion.13
  826.9 1.0 constant_dynamic-slice_fusion.13
  827.9 1.0 constant_dynamic-slice_fusion.13
  830.0 1.0 constant_dynamic-slice_fusion.13
  831.1 1.0 constant_dynamic-slice_fusion.13
  832.1 1.0 constant_dynamic-slice_fusion.13
  833.2 1.0 constant_dynamic-slice_fusion.13
  835.2 1.0 constant_dynamic-slice_fusion.13
  836.3 1.0 constant_dynamic-slice_fusion.13
  837.3 1.0 constant_dynamic-slice_fusion.13
  838.4 1.0 constant_dynamic-slice_fusion.13
  840.5 1.0 constant_dynamic-slice_fusion.13
  841.5 1.0 constant_dynamic-slice_fusion.13
  842.6 1.0 constant_dynamic-slice_fusion.13
  845.7 1.0 constant_dynamic-slice_fusion.13
  846.8 1.0 constant_dynamic-slice_fusion.13
  847.8 1.0 constant_dynamic-slice_fusion.13
  849.9 1.0 constant_dynamic-slice_fusion.13
  850.9 1.0 constant_dynamic-slice_fusion.13
  852.0 1.0 constant_dynamic-slice_fusion.13
  853.0 1.0 constant_dynamic-slice_fusion.13
  855.1 1.0 constant_dynamic-slice_fusion.13
  856.2 1.0 constant_dynamic-slice_fusion.13
  857.2 1.0 constant_dynamic-slice_fusion.13
  858.3 1.0 constant_dynamic-slice_fusion.13
  860.4 1.0 constant_dynamic-slice_fusion.13
  861.4 1.0 constant_dynamic-slice_fusion.13
  862.4 1.0 constant_dynamic-slice_fusion.13
  865.6 1.0 constant_dynamic-slice_fusion.13
  866.6 1.0 constant_dynamic-slice_fusion.13
  867.7 1.0 constant_dynamic-slice_fusion.13
  869.8 1.0 constant_dynamic-slice_fusion.13
  870.8 1.0 constant_dynamic-slice_fusion.13
  871.9 1.0 constant_dynamic-slice_fusion.13
  872.9 1.0 constant_dynamic-slice_fusion.13
  875.0 1.0 constant_dynamic-slice_fusion.13
  876.1 1.0 constant_dynamic-slice_fusion.13
  877.1 1.0 constant_dynamic-slice_fusion.13
  878.1 1.0 constant_dynamic-slice_fusion.13
  880.2 1.0 constant_dynamic-slice_fusion.13
  954.2 7.6 all-gather.4
  961.8 5.4 all-gather.5
  969.0 1.1 exponential_reduce_fusion
  972.3 138.3 %all-gather.17.cloned.1.call-done = f32[128,1,4096]{2,1,0:T(1,128)} async-done(((f32[1,1,4096]{2,1,0:T(1,128)}), f32[128,1,4096]{2,1,0:T(1,128)}) %all-gather.17.cloned.1.call-update) | async-done | bytes 2097168 | tf_op jit(solution)/shard_map/all_gather | solution.py:18
  1110.6 3.2 copy.29
  1113.8 135.8 %all-gather.19.cloned.1.call-done = f32[128,1,4096]{2,1,0:T(1,128)} async-done(((f32[1,1,4096]{2,1,0:T(1,128)}), f32[128,1,4096]{2,1,0:T(1,128)}) %all-gather.19.cloned.1.call-update) | async-done | bytes 2097168 | tf_op jit(solution)/shard_map/all_gather | solution.py:18
  1249.7 4.6 copy.28
  1254.3 124.8 %while.71 = (s32[]{:T(128)}, f32[4096]{0:T(1024)S(1)}, f32[4096]{0:T(1024)S(1)}, f32[128,4096]{1,0:T(8,128)S(1)}, f32[128,4096]{1,0:T(8,128)}, /*index=5*/s32[]{:T(128)}, s32[]{:T(128)}, s32[]{:T(128)}) while((s32[]{:T(128)}, f32[4096]{0:T(1024)S(1)}, f32[4096]{0:T(1024)S(1)}, f32[128,4096]{1,0:T(8,128)S(1)}, f32[128,4096]{1,0:T(8,128)}, ...), condition=%wide.region_39.40_spmd, body=%wide.region_38.39_spmd.sunk | while | flops 24581 | bytes 163971 | solution.py:24
  (603 shorter events, 222.9 us)
Async XLA Ops:
  7.2 506.5 %copy-start = (bf16[4096,128]{1,0:T(8,128)(2,1)S(1)}, bf16[4096,128]{1,0:T(8,128)(2,1)}, u32[]{:S(2)}) copy-start(bf16[4096,128]{1,0:T(8,128)(2,1)} %param.21) | copy-start | bytes 3145732
  7.2 508.0 %copy-start.17 = (bf16[256,128]{1,0:T(8,128)(2,1)S(1)}, bf16[256,128]{1,0:T(8,128)(2,1)}, u32[]{:S(2)}) copy-start(bf16[256,128]{1,0:T(8,128)(2,1)} %param.18) | copy-start | bytes 196612
  7.2 508.0 %copy-start.18 = (f32[256]{0:T(256)S(1)}, f32[256]{0:T(256)}, u32[]{:S(2)}) copy-start(f32[256]{0:T(256)} %param.19) | copy-start | bytes 3076
  7.2 667.4 %all-gather.13.cloned.1.call-start = ((), (), s32[]{:S(2)}) async-start(), calls=%async_computation | async-start | bytes 2113536 | tf_op jit(solution)/shard_map/all_gather | solution.py:18
  515.7 1.5 copy-start.1
  516.4 14.1 %copy-start.5 = (f32[256,1024]{0,1:T(8,128)}, f32[256,1024]{0,1:T(8,128)S(1)}, u32[]{:S(2)}) copy-start(f32[256,1024]{0,1:T(8,128)S(1)} %get-tuple-element.644) | copy-start | bytes 3145732
  516.4 14.2 %copy-start.16 = (f32[256]{0:T(256)S(1)}, f32[256]{0:T(256)}, u32[]{:S(2)}) copy-start(f32[256]{0:T(256)} %param.20) | copy-start | bytes 3076
  530.6 1.2 copy-start.2
  530.6 1.5 copy-start.6
  533.3 0.6 copy-start.12
  534.0 279.9 %all-gather.15.cloned.1.call-start = ((), (), s32[]{:S(2)}) async-start(), calls=%async_computation.1 | async-start | bytes 2113536 | tf_op jit(solution)/shard_map/all_gather | solution.py:18
  536.4 0.6 copy-start.13
  537.0 573.6 %all-gather.17.cloned.1.call-start = ((), (), s32[]{:S(2)}) async-start(), calls=%async_computation.2 | async-start | bytes 2113536 | tf_op jit(solution)/shard_map/all_gather | solution.py:18
  813.9 4.6 slice-start.1
  813.9 4.6 slice-start.3
  813.9 137.5 %copy-start.9 = (f32[4096]{0:T(1024)S(1)}, f32[4096]{0:T(1024)}, u32[]{:S(2)}) copy-start(f32[4096]{0:T(1024)} %param.24) | copy-start | bytes 49156
  813.9 137.5 %copy-start.15 = (f32[4096]{0:T(1024)S(1)}, f32[4096]{0:T(1024)}, u32[]{:S(2)}) copy-start(f32[4096]{0:T(1024)} %param.23) | copy-start | bytes 49156
  951.4 1.2 copy-start.3
  951.5 1.7 copy-start.7
  967.4 1.2 copy-start.4
  967.4 1.5 copy-start.8
  967.4 2.6 copy-start.14
  971.0 0.6 copy-start.11
  971.6 278.1 %all-gather.19.cloned.1.call-start = ((), (), s32[]{:S(2)}) async-start(), calls=%async_computation.3 | async-start | bytes 2113536 | tf_op jit(solution)/shard_map/all_gather | solution.py:18
  971.7 0.6 copy-start.10
  1249.7 4.6 slice-start
  1249.7 4.6 slice-start.2
Sparse Core Ops, SparseCore 0:
  534.1 140.5 all-gather.12
  677.8 136.0 all-gather.14
  971.7 138.8 all-gather.16
  1113.6 136.0 all-gather.18
where the time goes:
time: 1390 us
  waiting for transfers between devices  546 us (39%)
  blocking collectives  524 us (38%)
  local copies, waits for them, and re-layouts  272 us (20%)
  between operations  18.3 us (1%)
  other arithmetic  15.7 us (1%)
    all_gather x4, waiting for transfers between devices, joined(): everything = jax.tree.map(lambda part: lax.all_gather(part, axis), value)  546 us
    unnamed x1, blocking collectives  498 us
    dynamic_slice x260, local copies, waits for them, and re-layouts, hop(): return combine(so_far, jax.tree.map(lambda part: part[k], everything))  245 us
  transfers between devices with their start and end apart: 4, of which 4 were waited for; matrix products, arithmetic and copies ran while one was open for 1% of the time, Pallas kernels for 0%

commit v1 on v0

v1 whole, which is shorter than its diff:
```python
import functools
import math

import jax
import jax.numpy as jnp
from jax import lax
from jax.experimental import pallas as pl
from jax.experimental.pallas import tpu as pltpu
from jax.sharding import Mesh
from jax.sharding import PartitionSpec as P

ADS_IN_PART = 1024
AB_J = 4
KMAX = 4
UBS = 256
NZ, NY, NC, NX = 16, 4, 2, 4
NS = NY * NC
NROW = NS * NX
SHARD = 32
USERS_HERE = NS * UBS
ADS_HERE = NZ * SHARD
PART_HERE = ADS_HERE // AB_J
ROWS = UBS + 8

regularizer_epsilon = 0.1
very_low = -1e30
LOG2E = math.log2(math.e)
TO_BITS = LOG2E / regularizer_epsilon
FROM_BITS = regularizer_epsilon / LOG2E
COL_SHIFT = 64.0
ROW_SHIFT = 100.0

VMEM_LIMIT = 40 * 1024 * 1024


def as_columns(row):
    return jnp.broadcast_to(row, (128, row.shape[1])).T


def tile_kernel(msg, ads, ad_weight, pot, tile, row_lse):
    weight = as_columns(ad_weight[...])
    pots = as_columns(pot[...])

    def block(s, carry):
        users = msg[s, :UBS, :].astype(jnp.bfloat16)
        scale = jnp.concatenate([msg[s, UBS : UBS + 1, :], msg[s, UBS + 1 : UBS + 2, :]], axis=1)
        at = pl.ds(pl.multiple_of(s * UBS, UBS), UBS)
        peaks, totals = [], []
        for q in range(AB_J):
            rows = slice(q * PART_HERE, (q + 1) * PART_HERE)
            product = lax.dot_general(
                ads[rows, :], users, (((1,), (1,)), ((), ())), preferred_element_type=jnp.float32
            )
            bias = msg[s, UBS + 4 + q : UBS + 5 + q, :]
            bias = jnp.concatenate([bias, bias], axis=1)
            wide = jnp.concatenate([weight[rows], weight[rows]], axis=1)
            values = product * wide * scale + bias
            tile[rows, at] = values
            values = values + jnp.concatenate([pots[rows], pots[rows]], axis=1)
            peak = jnp.max(values, axis=0, keepdims=True)
            peaks.append(peak)
            totals.append(jnp.sum(jnp.exp2(values - peak), axis=0, keepdims=True))
        peak = functools.reduce(jnp.maximum, peaks)
        total = sum(t * jnp.exp2(p - peak) for p, t in zip(peaks, totals))
        lse = peak + jnp.log2(total)
        row_lse[:, :, at] = jnp.broadcast_to(lse[None], (NROW, 1, UBS))
        return carry

    lax.fori_loop(0, NS, block, 0)


def column_sums(tile, row_pot, pots):
    sums = []
    for q in range(AB_J):
        rows = slice(q * PART_HERE, (q + 1) * PART_HERE)
        total = jnp.zeros((PART_HERE, 128), jnp.float32)
        for t in range(USERS_HERE // 128):
            lanes = slice(t * 128, (t + 1) * 128)
            total = total + jnp.exp2(tile[rows, lanes] + row_pot[:, lanes] + pots[rows])
        sums.append(jnp.sum(total.T, axis=0, keepdims=True))
    return jnp.concatenate(sums, axis=1)


def log_mass_of(msg):
    return jnp.concatenate(
        [msg[s, UBS + 2 + h : UBS + 3 + h, :] for s in range(NS) for h in range(2)], axis=1
    )


def first_column_kernel(tile, parts, mass, pot, row_pot_out, col_out):
    peak = jnp.max(parts[...], axis=0)
    total = jnp.sum(jnp.exp2(parts[...] - peak[None]), axis=0)
    row_pot = mass[...] - (peak + jnp.log2(total))
    row_pot_out[...] = row_pot
    sums = column_sums(tile, row_pot + COL_SHIFT, as_columns(pot[...]))
    col_out[...] = jnp.broadcast_to(sums[None], (NZ, 1, ADS_HERE))


def column_update(log_sum, fallback, log_demand):
    peak = jnp.maximum(log_sum, fallback)
    return log_demand - (peak + jnp.log2(jnp.exp2(log_sum - peak) + jnp.exp2(fallback - peak)))


def second_row_kernel(tile, parts, row_pot, pot, fallback, log_demand, pot_out, row_out):
    sums = jnp.sum(parts[...], axis=0)
    new_pot = column_update(
        jnp.log2(sums) - COL_SHIFT - pot[...], fallback[...], log_demand[...]
    )
    pot_out[...] = new_pot
    pots = as_columns(new_pot)
    for t in range(USERS_HERE // 128):
        lanes = slice(t * 128, (t + 1) * 128)
        shift = row_pot[:, lanes] + ROW_SHIFT
        total = jnp.zeros((8, 128), jnp.float32)
        for q in range(AB_J):
            rows = slice(q * PART_HERE, (q + 1) * PART_HERE)
            terms = jnp.exp2(tile[rows, lanes] + shift + pots[rows])
            total = total + jnp.sum(terms.reshape(PART_HERE // 8, 8, 128), axis=0)
        total = jnp.sum(total, axis=0, keepdims=True)
        row_out[:, :, lanes] = jnp.broadcast_to(total[None], (NROW, 1, 128))


def second_column_kernel(own, tile, parts, row_pot, mass, pot, user_out, col_out):
    sums = jnp.sum(parts[...], axis=0)
    new = row_pot[...] + (mass[...] + ROW_SHIFT - jnp.log2(sums))
    col_out[...] = column_sums(tile, new, as_columns(pot[...]))
    picked = jnp.zeros((1, UBS), jnp.float32)
    for s in range(NS):
        picked = jnp.where(own[0] == s, new[:, s * UBS : (s + 1) * UBS], picked)
    user_out[...] = picked * FROM_BITS


def last_kernel(parts, pot, fallback, log_demand, out):
    sums = jnp.sum(parts[...], axis=0)
    out[...] = (
        column_update(jnp.log2(sums) - pot[...], fallback[...], log_demand[...]) * FROM_BITS
    )


def call(kernel, out_shape, *operands, scalars=0):
    vmem = pl.BlockSpec(memory_space=pltpu.VMEM)
    smem = pl.BlockSpec(memory_space=pltpu.SMEM)
    return pl.pallas_call(
        kernel,
        out_shape=[jax.ShapeDtypeStruct(s, jnp.float32) for s in out_shape],
        in_specs=[smem] * scalars + [vmem] * (len(operands) - scalars),
        out_specs=[vmem] * len(out_shape),
        compiler_params=pltpu.CompilerParams(vmem_limit_bytes=VMEM_LIMIT),
    )(*operands)


def to_all(value, axes, count):
    return lax.all_to_all(
        jnp.broadcast_to(value[None], (count,) + value.shape), axes, 0, 0, tiled=True
    )


def on_device(
    user_embedding,
    user_scale,
    user_mass,
    ad_embedding,
    ad_scale,
    listing_view_demand,
    listing_unplaced_penalty,
    campaign_dual_vector_initial,
    eligible,
    counts,
):
    inverse_root = 1.0 / math.sqrt(user_embedding.shape[1])
    mine = lax.axis_index("y") * NC + lax.axis_index("c")

    used = jnp.arange(KMAX) < counts[0, 0]
    active = jnp.any(
        (eligible[0, 0][None, :] == jnp.arange(AB_J)[:, None]) & used[None, :], axis=1
    )
    bias = jnp.where(active, 0.0, very_low).astype(jnp.float32)
    message = jnp.concatenate(
        [
            user_embedding.astype(jnp.float32),
            user_scale.reshape(2, 128),
            jnp.log2(user_mass).reshape(2, 128),
            jnp.broadcast_to(bias[:, None], (AB_J, 128)),
        ]
    )
    messages = to_all(message, ("y", "c"), NS)
    pot = to_all(campaign_dual_vector_initial * TO_BITS, "z", NZ).reshape(1, ADS_HERE)

    def of_here(array):
        shape = array.shape[1:]
        picked = lax.dynamic_index_in_dim(
            array.reshape((NZ, NS, SHARD) + shape), mine, 1, keepdims=False
        )
        return picked.reshape((ADS_HERE,) + shape)

    ads = of_here(ad_embedding)
    weight = (of_here(ad_scale) * (inverse_root * TO_BITS)).reshape(1, ADS_HERE)
    fallback = (of_here(listing_unplaced_penalty) * -TO_BITS).reshape(1, ADS_HERE)
    log_demand = jnp.log2(of_here(listing_view_demand)).reshape(1, ADS_HERE)
    mass = messages[:, UBS + 2 : UBS + 4, :].reshape(1, USERS_HERE)

    row_axes = ("y", "c", "x")
    tile, row_parts = call(
        tile_kernel,
        [(ADS_HERE, USERS_HERE), (NROW, 1, USERS_HERE)],
        messages, ads, weight, pot,
    )
    row_parts = lax.all_to_all(row_parts, row_axes, 0, 0, tiled=True)
    row_pot, col_parts = call(
        first_column_kernel,
        [(1, USERS_HERE), (NZ, 1, ADS_HERE)],
        tile, row_parts, mass, pot,
    )
    col_parts = lax.all_to_all(col_parts, "z", 0, 0, tiled=True)
    pot, row_parts = call(
        second_row_kernel,
        [(1, ADS_HERE), (NROW, 1, USERS_HERE)],
        tile, col_parts, row_pot, pot, fallback, log_demand,
    )
    row_parts = lax.all_to_all(row_parts, row_axes, 0, 0, tiled=True)
    users, col_parts = call(
        second_column_kernel,
        [(1, UBS), (1, ADS_HERE)],
        mine.reshape(1), tile, row_parts, row_pot, mass, pot,
        scalars=1,
    )
    col_parts = lax.all_to_all(col_parts.reshape(NZ, 1, SHARD), "z", 0, 0, tiled=True)

    def of_mine(row):
        return lax.dynamic_slice_in_dim(row, lax.axis_index("z") * SHARD, SHARD, 1)

    (last,) = call(
        last_kernel, [(1, SHARD)],
        col_parts, of_mine(pot), of_mine(fallback), of_mine(log_demand),
    )
    return users.reshape(UBS), last.reshape(SHARD)


def solution(mesh):
    fine = Mesh(mesh.devices.reshape(NZ, NY, NC, NX), ("z", "y", "c", "x"))
    user = ("z", "y", "c")
    in_specs = (
        P(user, None),
        P(user),
        P(user),
        P("x", None),
        P("x"),
        P("x"),
        P("x"),
        P(("x",) + user),
        P(user, "x", None),
        P(user, "x"),
    )
    out_specs = (P(user), P(("x",) + user))
    return jax.shard_map(
        on_device, mesh=fine, in_specs=in_specs, out_specs=out_specs, check_vma=False
    )
```

time: 1390 us -> 130 us (0.09)
  blocking collectives: 524 us -> 0 us
  waiting for transfers between devices: 546 us -> 60.4 us
  local copies, waits for them, and re-layouts: 272 us -> 12.4 us
  starting transfers between devices: 0.16 us -> 40.7 us
  between operations: 18.3 us -> 1.41 us
    all_gather x4 -> x0, waiting for transfers between devices: 546 us -> none  [joined(): everything = jax.tree.map(lambda part: lax.all_gather(part, axis), value)]
    unnamed x1 -> x0, blocking collectives: 498 us -> none
    dynamic_slice x263 -> x4, local copies, waits for them, and re-layouts: 246 us -> 0.23 us  [the longest x3 0.23 us: of_mine(): return lax.dynamic_slice_in_dim(row, lax.axis_index('z') * SHARD, SHARD, 1)]
    all_to_all x0 -> x6, waiting for transfers between devices: none -> 60.4 us  [the longest x2 21.4 us: to_all(): lax.all_to_all(jnp.broadcast_to(value[None], (count,) + value.shape), axe...]
    all_to_all x0 -> x6, starting transfers between devices: none -> 40.7 us  [the longest x2 22.4 us: to_all(): lax.all_to_all(jnp.broadcast_to(value[None], (count,) + value.shape), axe...]
    all_gather x4 -> x0, blocking collectives: 26 us -> none  [joined(): everything = jax.tree.map(lambda part: lax.all_gather(part, axis), value)]
    unnamed x53 -> x16, local copies, waits for them, and re-layouts: 24.5 us -> 8.52 us
  transfers between devices with their start and end apart: 4 -> 6, of which waited for: 4 -> 6; matrix products, arithmetic and copies ran while one was open for 1% -> 5% of each run, Pallas kernels for 0% -> 0%
where the time goes in v1:
time: 130 us
  waiting for transfers between devices  60.4 us (46%)
  starting transfers between devices  40.7 us (31%)
  local copies, waits for them, and re-layouts  12.4 us (10%)
  Pallas kernels  9.06 us (7%)
  other arithmetic  5.68 us (4%)
  between operations  1.41 us (1%)
    all_to_all x2, starting transfers between devices, to_all(): lax.all_to_all(jnp.broadcast_to(value[None], (count,) + value.shape), axe...  22.4 us
    all_to_all x2, waiting for transfers between devices, to_all(): lax.all_to_all(jnp.broadcast_to(value[None], (count,) + value.shape), axe...  21.4 us
    all_to_all x2, waiting for transfers between devices, on_device(): row_parts = lax.all_to_all(row_parts, row_axes, 0, 0, tiled=True)  17.5 us
    all_to_all x2, starting transfers between devices, on_device(): row_parts = lax.all_to_all(row_parts, row_axes, 0, 0, tiled=True)  11.3 us
    all_to_all x1, waiting for transfers between devices, on_device(): lax.all_to_all(col_parts.reshape(NZ, 1, SHARD), 'z', 0, 0, tiled=True)  11.1 us
    all_to_all x1, waiting for transfers between devices, on_device(): col_parts = lax.all_to_all(col_parts, 'z', 0, 0, tiled=True)  10.4 us
    pallas_call x5, Pallas kernels, call(): pl.pallas_call(kernel, out_shape=[jax.ShapeDtypeStruct(s, jnp.float32) fo...  9.06 us
    unnamed x16, local copies, waits for them, and re-layouts  8.52 us
  transfers between devices with their start and end apart: 6, of which 6 were waited for; matrix products, arithmetic and copies ran while one was open for 5% of the time, Pallas kernels for 0%

profile of v1, /device:TPU:1, one launch (start us, length us, event | category | flops | bytes accessed | tf_op | source)
XLA Modules:
  0.0 129.6 jit_solution(13132643680685128833)
XLA Ops:
  0.6 0.0 copy-start
  0.6 0.7 broadcast_multiply_fusion
  1.4 0.6 broadcast_in_dim.32
  2.0 15.7 %all-to-all-start.1 = ((f32[16,1,32]{2,1,0:T(1,128)}), f32[16,1,32]{2,1,0:T(1,128)S(1)}, u32[]{:S(2)}, u32[]{:S(2)}) async-start(f32[16,1,32]{2,1,0:T(1,128)} %broadcast_in_dim.32), calls=%async_computation.1 | async-start | bytes 16384 | tf_op jit(solution)/shard_map/all_to_all | solution.py:153
  18.4 0.8 fusion.1
  19.2 0.7 multiply_bitcast_fusion
  19.9 0.9 convert_element_type.3
  20.7 0.1 pad.3.clone
  20.8 0.8 maximum_maximum_fusion
  21.6 7.4 %all-to-all-done.1 = f32[16,1,32]{2,1,0:T(1,128)S(1)} async-done(((f32[16,1,32]{2,1,0:T(1,128)}), f32[16,1,32]{2,1,0:T(1,128)S(1)}, u32[]{:S(2)}, u32[]{:S(2)}) %all-to-all-start.1) | async-done | bytes 2080 | tf_op jit(solution)/shard_map/all_to_all | solution.py:153
  29.0 1.0 broadcast_in_dim.17
  30.0 0.0 copy-start.5
  30.0 6.7 %all-to-all-start = ((f32[8,264,128]{2,1,0:T(8,128)}), f32[8,264,128]{2,1,0:T(8,128)S(1)}, u32[]{:S(2)}, u32[]{:S(2)}) async-start(f32[8,264,128]{2,1,0:T(8,128)} %broadcast_in_dim.17), calls=%async_computation | async-start | bytes 2162688 | tf_op jit(solution)/shard_map/all_to_all | solution.py:153
  36.7 0.0 copy-done.5
  36.7 0.1 reshape.121
  36.9 0.1 mul.52.ad_weight
  36.9 0.0 copy-done
  36.9 0.5 broadcast.68
  37.5 0.6 reduce.20
  38.0 0.1 reshape.122.pot
  38.1 14.1 %all-to-all-done.msg = f32[8,264,128]{2,1,0:T(8,128)S(1)} async-done(((f32[8,264,128]{2,1,0:T(8,128)}), f32[8,264,128]{2,1,0:T(8,128)S(1)}, u32[]{:S(2)}, u32[]{:S(2)}) %all-to-all-start) | async-done | bytes 1081376 | tf_op jit(solution)/shard_map/all_to_all | solution.py:153
  52.2 4.0 %shard_map.113 = (f32[512,2048]{1,0:T(8,128)S(1)}, f32[32,1,2048]{2,1,0:T(1,128)}) custom-call(f32[8,264,128]{2,1,0:T(8,128)S(1)} %all-to-all-done.msg, bf16[512,128]{1,0:T(8,128)(2,1)S(1)} %bitcast.21, f32[1,512]{1,0:T(1,128)S(1)} %mul.52.ad_weight, f32[1,512]{1,0:T(1,128)S(1)} %reshape.122.pot), custom_call_target="tpu_custom_call" | custom-call | tf_op jit(solution)/shard_map/pallas_call | solution.py:143
  56.1 0.0 copy-start.1
  56.1 1.9 %copy-done.1 = f32[512,2048]{1,0:T(8,128)} copy-done((f32[512,2048]{1,0:T(8,128)}, f32[512,2048]{1,0:T(8,128)S(1)}, u32[]{:S(2)}) %copy-start.1) | copy-done | bytes 4194328
  58.1 5.9 %all-to-all-start.2 = ((f32[32,1,2048]{2,1,0:T(1,128)}), f32[32,1,2048]{2,1,0:T(1,128)S(1)}, u32[]{:S(2)}, u32[]{:S(2)}) async-start(f32[32,1,2048]{2,1,0:T(1,128)} %get-tuple-element.11), calls=%async_computation.2 | async-start | bytes 524288 | tf_op jit(solution)/shard_map/all_to_all | solution.py:208
  64.0 8.9 %all-to-all-done.2.parts = f32[32,1,2048]{2,1,0:T(1,128)S(1)} async-done(((f32[32,1,2048]{2,1,0:T(1,128)}), f32[32,1,2048]{2,1,0:T(1,128)S(1)}, u32[]{:S(2)}, u32[]{:S(2)}) %all-to-all-start.2) | async-done | bytes 262176 | tf_op jit(solution)/shard_map/all_to_all | solution.py:208
  72.9 0.0 copy-start.2
  72.9 2.2 %copy-done.2 = f32[512,2048]{1,0:T(8,128)S(1)} copy-done((f32[512,2048]{1,0:T(8,128)S(1)}, f32[512,2048]{1,0:T(8,128)}, u32[]{:S(2)}) %copy-start.2) | copy-done | bytes 4194328
  75.1 0.0 copy-start.6
  75.1 0.0 copy-start.7
  75.1 1.5 %shard_map.114 = (f32[1,2048]{1,0:T(1,128)S(1)}, f32[16,1,512]{2,1,0:T(1,128)}) custom-call(f32[512,2048]{1,0:T(8,128)S(1)} %copy-done.2, f32[32,1,2048]{2,1,0:T(1,128)S(1)} %all-to-all-done.2.parts, f32[1,2048]{1,0:T(1,128)S(1)} %bitcast.22, f32[1,512]{1,0:T(1,128)S(1)} %reshape.122.pot), custom_call_target="tpu_custom_call" | custom-call | tf_op jit(solution)/shard_map/pallas_call | solution.py:143
  76.6 3.5 %all-to-all-start.3 = ((f32[16,1,512]{2,1,0:T(1,128)}), f32[16,1,512]{2,1,0:T(1,128)S(1)}, u32[]{:S(2)}, u32[]{:S(2)}) async-start(f32[16,1,512]{2,1,0:T(1,128)} %get-tuple-element.12), calls=%async_computation.3 | async-start | bytes 65536 | tf_op jit(solution)/shard_map/all_to_all | solution.py:214
  80.1 0.0 copy-done.6
  80.1 0.1 reshape.125
  80.2 0.0 copy-done.7
  80.2 0.1 reshape.124
  80.3 0.6 fusion.2
  80.9 0.1 log2.46.log_demand
  81.0 0.1 mul.57.fallback
  81.1 10.4 %all-to-all-done.3.parts = f32[16,1,512]{2,1,0:T(1,128)S(1)} async-done(((f32[16,1,512]{2,1,0:T(1,128)}), f32[16,1,512]{2,1,0:T(1,128)S(1)}, u32[]{:S(2)}, u32[]{:S(2)}) %all-to-all-start.3) | async-done | bytes 32800 | tf_op jit(solution)/shard_map/all_to_all | solution.py:214
  91.5 0.0 copy-start.3
  91.5 2.2 %copy-done.3 = f32[512,2048]{1,0:T(8,128)S(1)} copy-done((f32[512,2048]{1,0:T(8,128)S(1)}, f32[512,2048]{1,0:T(8,128)}, u32[]{:S(2)}) %copy-start.3) | copy-done | bytes 4194328
  93.7 1.7 %shard_map.115 = (f32[1,512]{1,0:T(1,128)S(1)}, f32[32,1,2048]{2,1,0:T(1,128)}) custom-call(f32[512,2048]{1,0:T(8,128)S(1)} %copy-done.3, f32[16,1,512]{2,1,0:T(1,128)S(1)} %all-to-all-done.3.parts, f32[1,2048]{1,0:T(1,128)S(1)} %get-tuple-element.13.row_pot, f32[1,512]{1,0:T(1,128)S(1)} %reshape.122.pot, f32[1,512]{1,0:T(1,128)S(1)} %mul.57.fallback, ...), custom_call_target="tpu_custom_call" | custom-call | tf_op jit(solution)/shard_map/pallas_call | solution.py:143
  95.4 5.4 %all-to-all-start.4 = ((f32[32,1,2048]{2,1,0:T(1,128)}), f32[32,1,2048]{2,1,0:T(1,128)S(1)}, u32[]{:S(2)}, u32[]{:S(2)}) async-start(f32[32,1,2048]{2,1,0:T(1,128)} %get-tuple-element.14), calls=%async_computation.4 | async-start | bytes 524288 | tf_op jit(solution)/shard_map/all_to_all | solution.py:220
  100.8 0.1 log2.47
  100.8 0.1 mul.59
  100.9 0.1 dynamic-slice_bitcast_fusion.log_demand
  101.0 0.1 dynamic-slice_bitcast_fusion.1.fallback
  101.1 8.6 %all-to-all-done.4.parts = f32[32,1,2048]{2,1,0:T(1,128)S(1)} async-done(((f32[32,1,2048]{2,1,0:T(1,128)}), f32[32,1,2048]{2,1,0:T(1,128)S(1)}, u32[]{:S(2)}, u32[]{:S(2)}) %all-to-all-start.4) | async-done | bytes 262176 | tf_op jit(solution)/shard_map/all_to_all | solution.py:220
  109.7 0.0 copy-start.4
  109.7 2.2 %copy-done.4 = f32[512,2048]{1,0:T(8,128)S(1)} copy-done((f32[512,2048]{1,0:T(8,128)S(1)}, f32[512,2048]{1,0:T(8,128)}, u32[]{:S(2)}) %copy-start.4) | copy-done | bytes 4194328
  111.8 1.3 %shard_map.116 = (f32[1,256]{1,0:T(1,128)}, f32[1,512]{1,0:T(1,128)S(1)}) custom-call(s32[1]{0:T(128)} %bitcast.own, f32[512,2048]{1,0:T(8,128)S(1)} %copy-done.4, f32[32,1,2048]{2,1,0:T(1,128)S(1)} %all-to-all-done.4.parts, f32[1,2048]{1,0:T(1,128)S(1)} %get-tuple-element.13.row_pot, f32[1,2048]{1,0:T(1,128)S(1)} %bitcast.23, ...), custom_call_target="tpu_custom_call" | custom-call | tf_op jit(solution)/shard_map/pallas_call | solution.py:143
  113.2 0.6 reduce.23
  113.7 0.7 reshape.127
  114.4 3.4 %all-to-all-start.5 = ((f32[16,1,32]{2,1,0:T(1,128)}), f32[16,1,32]{2,1,0:T(1,128)S(1)}, u32[]{:S(2)}, u32[]{:S(2)}) async-start(f32[16,1,32]{2,1,0:T(1,128)} %reshape.127), calls=%async_computation.5 | async-start | bytes 16384 | tf_op jit(solution)/shard_map/all_to_all | solution.py:227
  117.8 0.1 constant_dynamic-slice_fusion.pot
  117.9 11.1 %all-to-all-done.5.parts = f32[16,1,32]{2,1,0:T(1,128)S(1)} async-done(((f32[16,1,32]{2,1,0:T(1,128)}), f32[16,1,32]{2,1,0:T(1,128)S(1)}, u32[]{:S(2)}, u32[]{:S(2)}) %all-to-all-start.5) | async-done | bytes 2080 | tf_op jit(solution)/shard_map/all_to_all | solution.py:227
  129.0 0.6 shard_map.117
  (5 shorter events, 0.1 us)
Async XLA Ops:
  0.6 36.3 %copy-start = (bf16[4096,128]{1,0:T(8,128)(2,1)S(1)}, bf16[4096,128]{1,0:T(8,128)(2,1)}, u32[]{:S(2)}) copy-start(bf16[4096,128]{1,0:T(8,128)(2,1)} %param.13) | copy-start | bytes 3145732
  2.0 27.0 %all-to-all-start.1 = ((f32[16,1,32]{2,1,0:T(1,128)}), f32[16,1,32]{2,1,0:T(1,128)S(1)}, u32[]{:S(2)}, u32[]{:S(2)}) async-start(f32[16,1,32]{2,1,0:T(1,128)} %broadcast_in_dim.32), calls=%async_computation.1 | async-start | bytes 16384 | tf_op jit(solution)/shard_map/all_to_all | solution.py:153
  30.0 6.7 %copy-start.5 = (f32[4096]{0:T(1024)S(1)}, f32[4096]{0:T(1024)}, u32[]{:S(2)}) copy-start(f32[4096]{0:T(1024)} %param.14) | copy-start | bytes 49156
  30.0 22.2 %all-to-all-start = ((f32[8,264,128]{2,1,0:T(8,128)}), f32[8,264,128]{2,1,0:T(8,128)S(1)}, u32[]{:S(2)}, u32[]{:S(2)}) async-start(f32[8,264,128]{2,1,0:T(8,128)} %broadcast_in_dim.17), calls=%async_computation | async-start | bytes 2162688 | tf_op jit(solution)/shard_map/all_to_all | solution.py:153
  56.1 1.9 %copy-start.1 = (f32[512,2048]{1,0:T(8,128)}, f32[512,2048]{1,0:T(8,128)S(1)}, u32[]{:S(2)}) copy-start(f32[512,2048]{1,0:T(8,128)S(1)} %get-tuple-element.10.tile) | copy-start | bytes 12582916
  58.1 14.8 %all-to-all-start.2 = ((f32[32,1,2048]{2,1,0:T(1,128)}), f32[32,1,2048]{2,1,0:T(1,128)S(1)}, u32[]{:S(2)}, u32[]{:S(2)}) async-start(f32[32,1,2048]{2,1,0:T(1,128)} %get-tuple-element.11), calls=%async_computation.2 | async-start | bytes 524288 | tf_op jit(solution)/shard_map/all_to_all | solution.py:208
  72.9 2.2 %copy-start.2 = (f32[512,2048]{1,0:T(8,128)S(1)}, f32[512,2048]{1,0:T(8,128)}, u32[]{:S(2)}) copy-start(f32[512,2048]{1,0:T(8,128)} %copy-done.1) | copy-start | bytes 12582916
  75.1 5.0 %copy-start.6 = (f32[4096]{0:T(1024)S(1)}, f32[4096]{0:T(1024)}, u32[]{:S(2)}) copy-start(f32[4096]{0:T(1024)} %param.15) | copy-start | bytes 49156
  75.1 5.1 %copy-start.7 = (f32[4096]{0:T(1024)S(1)}, f32[4096]{0:T(1024)}, u32[]{:S(2)}) copy-start(f32[4096]{0:T(1024)} %param.16) | copy-start | bytes 49156
  76.6 14.8 %all-to-all-start.3 = ((f32[16,1,512]{2,1,0:T(1,128)}), f32[16,1,512]{2,1,0:T(1,128)S(1)}, u32[]{:S(2)}, u32[]{:S(2)}) async-start(f32[16,1,512]{2,1,0:T(1,128)} %get-tuple-element.12), calls=%async_computation.3 | async-start | bytes 65536 | tf_op jit(solution)/shard_map/all_to_all | solution.py:214
  91.5 2.2 %copy-start.3 = (f32[512,2048]{1,0:T(8,128)S(1)}, f32[512,2048]{1,0:T(8,128)}, u32[]{:S(2)}) copy-start(f32[512,2048]{1,0:T(8,128)} %copy-done.1) | copy-start | bytes 12582916
  95.4 14.3 %all-to-all-start.4 = ((f32[32,1,2048]{2,1,0:T(1,128)}), f32[32,1,2048]{2,1,0:T(1,128)S(1)}, u32[]{:S(2)}, u32[]{:S(2)}) async-start(f32[32,1,2048]{2,1,0:T(1,128)} %get-tuple-element.14), calls=%async_computation.4 | async-start | bytes 524288 | tf_op jit(solution)/shard_map/all_to_all | solution.py:220
  109.7 2.2 %copy-start.4 = (f32[512,2048]{1,0:T(8,128)S(1)}, f32[512,2048]{1,0:T(8,128)}, u32[]{:S(2)}) copy-start(f32[512,2048]{1,0:T(8,128)} %copy-done.1) | copy-start | bytes 12582916
  114.4 14.6 %all-to-all-start.5 = ((f32[16,1,32]{2,1,0:T(1,128)}), f32[16,1,32]{2,1,0:T(1,128)S(1)}, u32[]{:S(2)}, u32[]{:S(2)}) async-start(f32[16,1,32]{2,1,0:T(1,128)} %reshape.127), calls=%async_computation.5 | async-start | bytes 16384 | tf_op jit(solution)/shard_map/all_to_all | solution.py:227

commit v2 on v1

--- a/solution.py
+++ b/solution.py
@@ -37,36 +37,64 @@
     return jnp.broadcast_to(row, (128, row.shape[1])).T
 
 
-def tile_kernel(msg, ads, ad_weight, pot, tile, row_lse):
+def message_kernel(eligible, counts, embedding, scale, mass, out):
+    out[:UBS, :] = embedding[...].astype(jnp.float32)
+    out[UBS : UBS + 2, :] = scale[...]
+    out[UBS + 2 : UBS + 4, :] = jnp.log2(mass[...])
+    for q in range(AB_J):
+        bias = jnp.float32(very_low)
+        for k in range(KMAX):
+            hit = jnp.logical_and(k < counts[0, 0], eligible[0, 0, k] == q)
+            bias = jnp.where(hit, jnp.float32(0.0), bias)
+        out[UBS + 4 + q : UBS + 5 + q, :] = jnp.full((1, 128), bias, jnp.float32)
+
+
+def tile_kernel(
+    mine, msg0, msg1, msg2, msg3, ads, ad_weight, pot_parts, fallback, log_demand,
+    tile, row_lse, log_mass, pot,
+):
+    del fallback, log_demand
     weight = as_columns(ad_weight[...])
-    pots = as_columns(pot[...])
-
-    def block(s, carry):
-        users = msg[s, :UBS, :].astype(jnp.bfloat16)
-        scale = jnp.concatenate([msg[s, UBS : UBS + 1, :], msg[s, UBS + 1 : UBS + 2, :]], axis=1)
-        at = pl.ds(pl.multiple_of(s * UBS, UBS), UBS)
-        peaks, totals = [], []
-        for q in range(AB_J):
-            rows = slice(q * PART_HERE, (q + 1) * PART_HERE)
-            product = lax.dot_general(
-                ads[rows, :], users, (((1,), (1,)), ((), ())), preferred_element_type=jnp.float32
+    pots = jnp.concatenate(
+        [jnp.sum(pot_parts[4 * q : 4 * q + 4], axis=0) for q in range(AB_J)], axis=1
+    )
+    pot[...] = pots
+    pots = as_columns(pots)
+    for back, msg in enumerate((msg0, msg1, msg2, msg3)):
+        first = lax.rem(mine[0] + (NY - back), NY) * NC
+
+        def block(c, carry, msg=msg, first=first):
+            users = msg[c, :UBS, :].astype(jnp.bfloat16)
+            scale = jnp.concatenate(
+                [msg[c, UBS : UBS + 1, :], msg[c, UBS + 1 : UBS + 2, :]], axis=1
             )
-            bias = msg[s, UBS + 4 + q : UBS + 5 + q, :]
-            bias = jnp.concatenate([bias, bias], axis=1)
-            wide = jnp.concatenate([weight[rows], weight[rows]], axis=1)
-            values = product * wide * scale + bias
-            tile[rows, at] = values
-            values = values + jnp.concatenate([pots[rows], pots[rows]], axis=1)
-            peak = jnp.max(values, axis=0, keepdims=True)
-            peaks.append(peak)
-            totals.append(jnp.sum(jnp.exp2(values - peak), axis=0, keepdims=True))
-        peak = functools.reduce(jnp.maximum, peaks)
-        total = sum(t * jnp.exp2(p - peak) for p, t in zip(peaks, totals))
-        lse = peak + jnp.log2(total)
-        row_lse[:, :, at] = jnp.broadcast_to(lse[None], (NROW, 1, UBS))
-        return carry
-
-    lax.fori_loop(0, NS, block, 0)
+            at = pl.ds(pl.multiple_of((first + c) * UBS, UBS), UBS)
+            log_mass[:, at] = jnp.concatenate(
+                [msg[c, UBS + 2 : UBS + 3, :], msg[c, UBS + 3 : UBS + 4, :]], axis=1
+            )
+            peaks, totals = [], []
+            for q in range(AB_J):
+                rows = slice(q * PART_HERE, (q + 1) * PART_HERE)
+                product = lax.dot_general(
+                    ads[rows, :], users, (((1,), (1,)), ((), ())),
+                    preferred_element_type=jnp.float32,
+                )
+                bias = msg[c, UBS + 4 + q : UBS + 5 + q, :]
+                bias = jnp.concatenate([bias, bias], axis=1)
+                wide = jnp.concatenate([weight[rows], weight[rows]], axis=1)
+                values = product * wide * scale + bias
+                tile[rows, at] = values
+                values = values + jnp.concatenate([pots[rows], pots[rows]], axis=1)
+                peak = jnp.max(values, axis=0, keepdims=True)
+                peaks.append(peak)
+                totals.append(jnp.sum(jnp.exp2(values - peak), axis=0, keepdims=True))
+            peak = functools.reduce(jnp.maximum, peaks)
+            total = sum(t * jnp.exp2(p - peak) for p, t in zip(peaks, totals))
+            lse = peak + jnp.log2(total)
+            row_lse[:, :, at] = jnp.broadcast_to(lse[None], (NROW, 1, UBS))
+            return carry
+
+        lax.fori_loop(0, NC, block, 0)
 
 
 def column_sums(tile, row_pot, pots):
@@ -79,12 +107,6 @@
             total = total + jnp.exp2(tile[rows, lanes] + row_pot[:, lanes] + pots[rows])
         sums.append(jnp.sum(total.T, axis=0, keepdims=True))
     return jnp.concatenate(sums, axis=1)
-
-
-def log_mass_of(msg):
-    return jnp.concatenate(
-        [msg[s, UBS + 2 + h : UBS + 3 + h, :] for s in range(NS) for h in range(2)], axis=1
-    )
 
 
 def first_column_kernel(tile, parts, mass, pot, row_pot_out, col_out):
@@ -123,18 +145,20 @@
 def second_column_kernel(own, tile, parts, row_pot, mass, pot, user_out, col_out):
     sums = jnp.sum(parts[...], axis=0)
     new = row_pot[...] + (mass[...] + ROW_SHIFT - jnp.log2(sums))
-    col_out[...] = column_sums(tile, new, as_columns(pot[...]))
+    sums = column_sums(tile, new, as_columns(pot[...]))
+    col_out[...] = jnp.broadcast_to(sums[None], (NZ, 1, ADS_HERE))
     picked = jnp.zeros((1, UBS), jnp.float32)
     for s in range(NS):
         picked = jnp.where(own[0] == s, new[:, s * UBS : (s + 1) * UBS], picked)
     user_out[...] = picked * FROM_BITS
 
 
-def last_kernel(parts, pot, fallback, log_demand, out):
+def last_kernel(own, parts, pot, fallback, log_demand, out):
     sums = jnp.sum(parts[...], axis=0)
-    out[...] = (
-        column_update(jnp.log2(sums) - pot[...], fallback[...], log_demand[...]) * FROM_BITS
-    )
+    new = column_update(jnp.log2(sums) - pot[...], fallback[...], log_demand[...]) * FROM_BITS
+    new = jnp.broadcast_to(new, (8, ADS_HERE))
+    turned = pltpu.roll(new, lax.rem(ADS_HERE - own[0] * SHARD, ADS_HERE), 1)
+    out[...] = turned[:1, :SHARD]
 
 
 def call(kernel, out_shape, *operands, scalars=0):
@@ -147,12 +171,6 @@
         out_specs=[vmem] * len(out_shape),
         compiler_params=pltpu.CompilerParams(vmem_limit_bytes=VMEM_LIMIT),
     )(*operands)
-
-
-def to_all(value, axes, count):
-    return lax.all_to_all(
-        jnp.broadcast_to(value[None], (count,) + value.shape), axes, 0, 0, tiled=True
-    )
 
 
 def on_device(
@@ -168,23 +186,28 @@
     counts,
 ):
     inverse_root = 1.0 / math.sqrt(user_embedding.shape[1])
-    mine = lax.axis_index("y") * NC + lax.axis_index("c")
-
-    used = jnp.arange(KMAX) < counts[0, 0]
-    active = jnp.any(
-        (eligible[0, 0][None, :] == jnp.arange(AB_J)[:, None]) & used[None, :], axis=1
-    )
-    bias = jnp.where(active, 0.0, very_low).astype(jnp.float32)
-    message = jnp.concatenate(
-        [
-            user_embedding.astype(jnp.float32),
-            user_scale.reshape(2, 128),
-            jnp.log2(user_mass).reshape(2, 128),
-            jnp.broadcast_to(bias[:, None], (AB_J, 128)),
-        ]
-    )
-    messages = to_all(message, ("y", "c"), NS)
-    pot = to_all(campaign_dual_vector_initial * TO_BITS, "z", NZ).reshape(1, ADS_HERE)
+    y, z = lax.axis_index("y"), lax.axis_index("z")
+    mine = y * NC + lax.axis_index("c")
+
+    pot_part = lax.dynamic_update_slice(
+        jnp.zeros((128,), jnp.float32),
+        campaign_dual_vector_initial * TO_BITS,
+        (lax.rem(z, AB_J) * SHARD,),
+    )
+    pot_parts = lax.all_to_all(
+        jnp.broadcast_to(pot_part, (NZ, 1, 128)), "z", 0, 0, tiled=True
+    )
+
+    (message,) = call(
+        message_kernel,
+        [(ROWS, 128)],
+        eligible, counts, user_embedding, user_scale.reshape(2, 128), user_mass.reshape(2, 128),
+        scalars=2,
+    )
+    pair = lax.all_gather(message, "c")
+    messages = [pair] + [
+        lax.ppermute(pair, "y", [(i, (i + d) % NY) for i in range(NY)]) for d in range(1, NY)
+    ]
 
     def of_here(array):
         shape = array.shape[1:]
@@ -197,13 +220,13 @@
     weight = (of_here(ad_scale) * (inverse_root * TO_BITS)).reshape(1, ADS_HERE)
     fallback = (of_here(listing_unplaced_penalty) * -TO_BITS).reshape(1, ADS_HERE)
     log_demand = jnp.log2(of_here(listing_view_demand)).reshape(1, ADS_HERE)
-    mass = messages[:, UBS + 2 : UBS + 4, :].reshape(1, USERS_HERE)
 
     row_axes = ("y", "c", "x")
-    tile, row_parts = call(
+    tile, row_parts, mass, pot = call(
         tile_kernel,
-        [(ADS_HERE, USERS_HERE), (NROW, 1, USERS_HERE)],
-        messages, ads, weight, pot,
+        [(ADS_HERE, USERS_HERE), (NROW, 1, USERS_HERE), (1, USERS_HERE), (1, ADS_HERE)],
+        y.reshape(1), *messages, ads, weight, pot_parts, fallback, log_demand,
+        scalars=1,
     )
     row_parts = lax.all_to_all(row_parts, row_axes, 0, 0, tiled=True)
     row_pot, col_parts = call(
@@ -220,18 +243,15 @@
     row_parts = lax.all_to_all(row_parts, row_axes, 0, 0, tiled=True)
     users, col_parts = call(
         second_column_kernel,
-        [(1, UBS), (1, ADS_HERE)],
+        [(1, UBS), (NZ, 1, ADS_HERE)],
         mine.reshape(1), tile, row_parts, row_pot, mass, pot,
         scalars=1,
     )
-    col_parts = lax.all_to_all(col_parts.reshape(NZ, 1, SHARD), "z", 0, 0, tiled=True)
-
-    def of_mine(row):
-        return lax.dynamic_slice_in_dim(row, lax.axis_index("z") * SHARD, SHARD, 1)
-
+    col_parts = lax.all_to_all(col_parts, "z", 0, 0, tiled=True)
     (last,) = call(
         last_kernel, [(1, SHARD)],
-        col_parts, of_mine(pot), of_mine(fallback), of_mine(log_demand),
+        z.reshape(1), col_parts, pot, fallback, log_demand,
+        scalars=1,
     )
     return users.reshape(UBS), last.reshape(SHARD)
 

time: 130 us -> 112 us (0.86)
  blocking collectives: 0 us -> 67.8 us
  waiting for transfers between devices: 60.4 us -> 8.53 us
  starting transfers between devices: 40.7 us -> 19 us
  local copies, waits for them, and re-layouts: 12.4 us -> 6.09 us
  other arithmetic: 5.68 us -> 0.86 us
  Pallas kernels: 9.06 us -> 7.65 us
    all_to_all x0 -> x4, blocking collectives: none -> 59.3 us  [the longest x2 31.4 us: on_device(): row_parts = lax.all_to_all(row_parts, row_axes, 0, 0, tiled=True)]
    all_to_all x6 -> x1, waiting for transfers between devices: 60.4 us -> 8.52 us  [on_device(): lax.all_to_all(jnp.broadcast_to(pot_part, (NZ, 1, 128)), 'z', 0, 0, tiled...]
    all_to_all x6 -> x1, starting transfers between devices: 40.7 us -> 11.8 us  [on_device(): lax.all_to_all(jnp.broadcast_to(pot_part, (NZ, 1, 128)), 'z', 0, 0, tiled...]
    all_gather x0 -> x1, blocking collectives: none -> 8.52 us  [on_device(): pair = lax.all_gather(message, 'c')]
    ppermute x0 -> x3, starting transfers between devices: none -> 7.19 us  [on_device(): lax.ppermute(pair, 'y', [(i, (i + d) % NY) for i in range(NY)])]
    unnamed x16 -> x10, local copies, waits for them, and re-layouts: 8.52 us -> 2.85 us
    reshape x3, local copies, waits for them, and re-layouts: 0.22 us -> 2.38 us  [of_here(): array.reshape((NZ, NS, SHARD) + shape)]
    pallas_call x5 -> x6, Pallas kernels: 9.06 us -> 7.65 us  [call(): pl.pallas_call(kernel, out_shape=[jax.ShapeDtypeStruct(s, jnp.float32) fo...]
  transfers between devices with their start and end apart: 6 -> 4, of which waited for: 6 -> 1; matrix products, arithmetic and copies ran while one was open for 5% -> 4% of each run, Pallas kernels for 0% -> 0%
where the time goes in v2:
time: 112 us; the launch traced here: 111 us
  blocking collectives  67.8 us (61%)
  starting transfers between devices  19 us (17%)
  waiting for transfers between devices  8.53 us (8%)
  Pallas kernels  7.65 us (7%)
  local copies, waits for them, and re-layouts  6.09 us (5%)
  between operations  1.52 us (1%)
    all_to_all x2, blocking collectives, on_device(): row_parts = lax.all_to_all(row_parts, row_axes, 0, 0, tiled=True)  31.4 us
    all_to_all x2, blocking collectives, on_device(): col_parts = lax.all_to_all(col_parts, 'z', 0, 0, tiled=True)  27.9 us
    all_to_all x1, starting transfers between devices, on_device(): lax.all_to_all(jnp.broadcast_to(pot_part, (NZ, 1, 128)), 'z', 0, 0, tiled...  11.8 us
    all_to_all x1, waiting for transfers between devices, on_device(): lax.all_to_all(jnp.broadcast_to(pot_part, (NZ, 1, 128)), 'z', 0, 0, tiled...  8.52 us
    all_gather x1, blocking collectives, on_device(): pair = lax.all_gather(message, 'c')  8.52 us
    pallas_call x6, Pallas kernels, call(): pl.pallas_call(kernel, out_shape=[jax.ShapeDtypeStruct(s, jnp.float32) fo...  7.65 us
    ppermute x3, starting transfers between devices, on_device(): lax.ppermute(pair, 'y', [(i, (i + d) % NY) for i in range(NY)])  7.19 us
    unnamed x10, local copies, waits for them, and re-layouts  2.85 us
  transfers between devices with their start and end apart: 4, of which 1 were waited for; matrix products, arithmetic and copies ran while one was open for 4% of the time, Pallas kernels for 0%

profile of v2, /device:TPU:1, one launch (start us, length us, event | category | flops | bytes accessed | tf_op | source)
XLA Modules:
  0.0 111.5 jit_solution(13129276311100838461)
XLA Ops:
  0.6 0.0 copy-start
  1.4 0.0 copy-start.1
  1.4 0.8 copy-done.1
  2.2 0.0 copy-start.2
  2.2 0.7 copy-done.2
  2.9 0.0 copy-start.3
  2.9 0.7 copy-done.3
  3.6 0.0 copy-start.4
  3.6 0.7 copy-done.4
  4.2 0.6 shard_map.113
  4.8 8.5 %all-gather = f32[528,128]{1,0:T(8,128)S(1)} all-gather(f32[264,128]{1,0:T(8,128)S(1)} %shard_map.113), channel_id=2, replica_groups=mesh['z'=16,'y'=4,'c'=2,'x'=4] {'c'}, dimensions={0}, use_global_device_ids=true | all-gather | bytes 405504 | tf_op jit(solution)/shard_map/all_gather | solution.py:207
  13.3 1.9 %collective-permute-start.2 = (f32[2,264,128]{2,1,0:T(8,128)S(1)}, f32[2,264,128]{2,1,0:T(8,128)S(1)}, u32[]{:S(2)}, u32[]{:S(2)}) collective-permute-start(f32[2,264,128]{2,1,0:T(8,128)S(1)} %bitcast.13), channel_id=1, source_target_pairs={{0,24},{8,0},{16,8},{24,16},{1,25},{9,1},{17,9},{25,17},{2,26},{10... | collective-permute-start | bytes 811016 | tf_op jit(solution)/shard_map/ppermute | solution.py:209
  15.2 1.9 %collective-permute-start.1 = (f32[2,264,128]{2,1,0:T(8,128)S(1)}, f32[2,264,128]{2,1,0:T(8,128)S(1)}, u32[]{:S(2)}, u32[]{:S(2)}) collective-permute-start(f32[2,264,128]{2,1,0:T(8,128)S(1)} %bitcast.14), channel_id=1, source_target_pairs={{0,16},{8,24},{16,0},{24,8},{1,17},{9,25},{17,1},{25,9},{2,18},{10... | collective-permute-start | bytes 811016 | tf_op jit(solution)/shard_map/ppermute | solution.py:209
  17.2 3.4 %collective-permute-start = (f32[2,264,128]{2,1,0:T(8,128)S(1)}, f32[2,264,128]{2,1,0:T(8,128)S(1)}, u32[]{:S(2)}, u32[]{:S(2)}) collective-permute-start(f32[2,264,128]{2,1,0:T(8,128)S(1)} %bitcast.15), channel_id=1, source_target_pairs={{0,8},{8,16},{16,24},{24,0},{1,9},{9,17},{17,25},{25,1},{2,10},{10... | collective-permute-start | bytes 811016 | tf_op jit(solution)/shard_map/ppermute | solution.py:209
  20.6 0.8 multiply_dynamic-update-slice_fusion
  21.3 0.6 broadcast_in_dim.7
  21.9 11.8 %all-to-all-start = ((f32[16,1,128]{2,1,0:T(1,128)}), f32[16,1,128]{2,1,0:T(1,128)S(1)}, u32[]{:S(2)}, u32[]{:S(2)}) async-start(f32[16,1,128]{2,1,0:T(1,128)} %broadcast_in_dim.7), calls=%async_computation | async-start | bytes 16384 | tf_op jit(solution)/shard_map/all_to_all | solution.py:197
  33.8 0.0 copy-done
  33.8 0.8 reshape.96
  34.6 0.1 mul.47.ad_weight
  34.7 0.8 reshape.98
  35.5 0.8 reshape.97
  36.3 0.1 multiply_reduce_fusion
  36.4 0.1 log2.30.log_demand
  36.5 0.1 mul.53.fallback
  36.5 8.5 %all-to-all-done.pot_parts = f32[16,1,128]{2,1,0:T(1,128)S(1)} async-done(((f32[16,1,128]{2,1,0:T(1,128)}), f32[16,1,128]{2,1,0:T(1,128)S(1)}, u32[]{:S(2)}, u32[]{:S(2)}) %all-to-all-start) | async-done | bytes 8224 | tf_op jit(solution)/shard_map/all_to_all | solution.py:197
  45.1 0.0 collective-permute-done.2.msg3
  45.1 0.0 collective-permute-done.1.msg2
  45.1 0.0 collective-permute-done.msg1
  45.1 3.2 %shard_map.114 = (f32[512,2048]{1,0:T(8,128)S(1)}, f32[32,1,2048]{2,1,0:T(1,128)S(1)}, f32[1,2048]{1,0:T(1,128)S(1)}, f32[1,512]{1,0:T(1,128)S(1)}) custom-call(s32[1]{0:T(128)} %bitcast.1.mine, f32[2,264,128]{2,1,0:T(8,128)S(1)} %bitcast.16, f32[2,264,128]{2,1,0:T(8,128)S(1)} %collective-permute-done.msg1, f32[2,264,128]{2,1,0:T(8,128)S(1)} %collective-permute-done.1.msg2, ...), custom_call_target="tpu_custom_call" | custom-call | tf_op jit(solution)/shard_map/pallas_call | solution.py:167
  48.3 17.4 %all_to_all.25.parts = f32[32,1,2048]{2,1,0:T(1,128)S(1)} all-to-all(f32[32,1,2048]{2,1,0:T(1,128)S(1)} %get-tuple-element.13), channel_id=1, replica_groups=mesh['z'=16,'y'=4,'c'=2,'x'=4] {'y','c','x'}, dimensions={0} | all-to-all | bytes 524288 | tf_op jit(solution)/shard_map/all_to_all | solution.py:231
  65.7 0.9 shard_map.115
  66.7 14.0 %all_to_all.26.parts = f32[16,1,512]{2,1,0:T(1,128)S(1)} all-to-all(f32[16,1,512]{2,1,0:T(1,128)S(1)} %get-tuple-element.16), channel_id=1, replica_groups=mesh['z'=16,'y'=4,'c'=2,'x'=4] {'z'}, dimensions={0} | all-to-all | bytes 65536 | tf_op jit(solution)/shard_map/all_to_all | solution.py:237
  80.6 1.0 shard_map.116
  81.6 14.0 %all_to_all.27.parts = f32[32,1,2048]{2,1,0:T(1,128)S(1)} all-to-all(f32[32,1,2048]{2,1,0:T(1,128)S(1)} %get-tuple-element.18), channel_id=1, replica_groups=mesh['z'=16,'y'=4,'c'=2,'x'=4] {'y','c','x'}, dimensions={0} | all-to-all | bytes 524288 | tf_op jit(solution)/shard_map/all_to_all | solution.py:243
  95.6 1.3 %shard_map.117 = (f32[1,256]{1,0:T(1,128)}, f32[16,1,512]{2,1,0:T(1,128)S(1)}) custom-call(s32[1]{0:T(128)} %bitcast.own, f32[512,2048]{1,0:T(8,128)S(1)} %get-tuple-element.12.tile, f32[32,1,2048]{2,1,0:T(1,128)S(1)} %all_to_all.27.parts, f32[1,2048]{1,0:T(1,128)S(1)} %get-tuple-element.17.row_pot, f32[1,2048]{1,0:T(1,128)S(1)} %get-tuple-element.14.mass, ...), custom_call_target="tpu_custom_call" | custom-call | tf_op jit(solution)/shard_map/pallas_call | solution.py:167
  96.9 14.0 %all_to_all.28.parts = f32[16,1,512]{2,1,0:T(1,128)S(1)} all-to-all(f32[16,1,512]{2,1,0:T(1,128)S(1)} %get-tuple-element.21), channel_id=1, replica_groups=mesh['z'=16,'y'=4,'c'=2,'x'=4] {'z'}, dimensions={0} | all-to-all | bytes 65536 | tf_op jit(solution)/shard_map/all_to_all | solution.py:250
  110.8 0.6 shard_map.118
  (3 shorter events, 0.1 us)
Async XLA Ops:
  0.6 33.1 %copy-start = (bf16[4096,128]{1,0:T(8,128)(2,1)S(1)}, bf16[4096,128]{1,0:T(8,128)(2,1)}, u32[]{:S(2)}) copy-start(bf16[4096,128]{1,0:T(8,128)(2,1)} %param.13) | copy-start | bytes 3145732
  1.4 0.8 copy-start.1
  2.2 0.7 copy-start.2
  2.9 0.7 copy-start.3
  3.6 0.7 copy-start.4
  13.3 31.8 %collective-permute-start.2 = (f32[2,264,128]{2,1,0:T(8,128)S(1)}, f32[2,264,128]{2,1,0:T(8,128)S(1)}, u32[]{:S(2)}, u32[]{:S(2)}) collective-permute-start(f32[2,264,128]{2,1,0:T(8,128)S(1)} %bitcast.13), channel_id=1, source_target_pairs={{0,24},{8,0},{16,8},{24,16},{1,25},{9,1},{17,9},{25,17},{2,26},{10... | collective-permute-start | bytes 811016 | tf_op jit(solution)/shard_map/ppermute | solution.py:209
  15.2 29.8 %collective-permute-start.1 = (f32[2,264,128]{2,1,0:T(8,128)S(1)}, f32[2,264,128]{2,1,0:T(8,128)S(1)}, u32[]{:S(2)}, u32[]{:S(2)}) collective-permute-start(f32[2,264,128]{2,1,0:T(8,128)S(1)} %bitcast.14), channel_id=1, source_target_pairs={{0,16},{8,24},{16,0},{24,8},{1,17},{9,25},{17,1},{25,9},{2,18},{10... | collective-permute-start | bytes 811016 | tf_op jit(solution)/shard_map/ppermute | solution.py:209
  17.2 27.9 %collective-permute-start = (f32[2,264,128]{2,1,0:T(8,128)S(1)}, f32[2,264,128]{2,1,0:T(8,128)S(1)}, u32[]{:S(2)}, u32[]{:S(2)}) collective-permute-start(f32[2,264,128]{2,1,0:T(8,128)S(1)} %bitcast.15), channel_id=1, source_target_pairs={{0,8},{8,16},{16,24},{24,0},{1,9},{9,17},{17,25},{25,1},{2,10},{10... | collective-permute-start | bytes 811016 | tf_op jit(solution)/shard_map/ppermute | solution.py:209
  21.9 23.1 %all-to-all-start = ((f32[16,1,128]{2,1,0:T(1,128)}), f32[16,1,128]{2,1,0:T(1,128)S(1)}, u32[]{:S(2)}, u32[]{:S(2)}) async-start(f32[16,1,128]{2,1,0:T(1,128)} %broadcast_in_dim.7), calls=%async_computation | async-start | bytes 16384 | tf_op jit(solution)/shard_map/all_to_all | solution.py:197

commit v3 on v2

--- a/solution.py
+++ b/solution.py
@@ -37,27 +37,35 @@
     return jnp.broadcast_to(row, (128, row.shape[1])).T
 
 
-def message_kernel(eligible, counts, embedding, scale, mass, out):
-    out[:UBS, :] = embedding[...].astype(jnp.float32)
-    out[UBS : UBS + 2, :] = scale[...]
-    out[UBS + 2 : UBS + 4, :] = jnp.log2(mass[...])
+def message_kernel(
+    eligible, counts, embedding, scale, mass, out, embedding_here, mass_here, sems
+):
+    copies = [
+        pltpu.make_async_copy(embedding, embedding_here, sems.at[0]),
+        pltpu.make_async_copy(scale, out.at[pl.ds(UBS, 2), :], sems.at[1]),
+        pltpu.make_async_copy(mass, mass_here, sems.at[2]),
+    ]
+    for copy in copies:
+        copy.start()
     for q in range(AB_J):
         bias = jnp.float32(very_low)
         for k in range(KMAX):
             hit = jnp.logical_and(k < counts[0, 0], eligible[0, 0, k] == q)
             bias = jnp.where(hit, jnp.float32(0.0), bias)
         out[UBS + 4 + q : UBS + 5 + q, :] = jnp.full((1, 128), bias, jnp.float32)
+    for copy in copies:
+        copy.wait()
+    out[:UBS, :] = embedding_here[...].astype(jnp.float32)
+    out[UBS + 2 : UBS + 4, :] = jnp.log2(mass_here[...])
 
 
 def tile_kernel(
-    mine, msg0, msg1, msg2, msg3, ads, ad_weight, pot_parts, fallback, log_demand,
+    mine, place, msg0, msg1, msg2, msg3, ads, ad_weight, pot_parts, fallback, log_demand,
     tile, row_lse, log_mass, pot,
 ):
-    del fallback, log_demand
+    del place, fallback, log_demand
     weight = as_columns(ad_weight[...])
-    pots = jnp.concatenate(
-        [jnp.sum(pot_parts[4 * q : 4 * q + 4], axis=0) for q in range(AB_J)], axis=1
-    )
+    pots = jnp.concatenate([pot_parts[z] for z in range(NZ)], axis=1) * TO_BITS
     pot[...] = pots
     pots = as_columns(pots)
     for back, msg in enumerate((msg0, msg1, msg2, msg3)):
@@ -189,25 +197,26 @@
     y, z = lax.axis_index("y"), lax.axis_index("z")
     mine = y * NC + lax.axis_index("c")
 
-    pot_part = lax.dynamic_update_slice(
-        jnp.zeros((128,), jnp.float32),
-        campaign_dual_vector_initial * TO_BITS,
-        (lax.rem(z, AB_J) * SHARD,),
-    )
     pot_parts = lax.all_to_all(
-        jnp.broadcast_to(pot_part, (NZ, 1, 128)), "z", 0, 0, tiled=True
-    )
-
-    (message,) = call(
+        jnp.broadcast_to(campaign_dual_vector_initial, (NZ, 1, SHARD)), "z", 0, 0, tiled=True
+    )
+
+    message = pl.pallas_call(
         message_kernel,
-        [(ROWS, 128)],
-        eligible, counts, user_embedding, user_scale.reshape(2, 128), user_mass.reshape(2, 128),
-        scalars=2,
-    )
-    pair = lax.all_gather(message, "c")
-    messages = [pair] + [
-        lax.ppermute(pair, "y", [(i, (i + d) % NY) for i in range(NY)]) for d in range(1, NY)
+        out_shape=jax.ShapeDtypeStruct((ROWS, 128), jnp.float32),
+        in_specs=[pl.BlockSpec(memory_space=pltpu.SMEM)] * 2
+        + [pl.BlockSpec(memory_space=pl.ANY)] * 3,
+        out_specs=pl.BlockSpec(memory_space=pltpu.VMEM),
+        scratch_shapes=[
+            pltpu.VMEM((UBS, 128), jnp.bfloat16),
+            pltpu.VMEM((2, 128), jnp.float32),
+            pltpu.SemaphoreType.DMA((3,)),
+        ],
+    )(eligible, counts, user_embedding, user_scale.reshape(2, 128), user_mass.reshape(2, 128))
+    messages = [
+        lax.ppermute(message, "y", [(i, (i + d) % NY) for i in range(NY)]) for d in range(1, NY)
     ]
+    messages = [lax.all_gather(m, "c") for m in [message] + messages]
 
     def of_here(array):
         shape = array.shape[1:]
@@ -225,8 +234,8 @@
     tile, row_parts, mass, pot = call(
         tile_kernel,
         [(ADS_HERE, USERS_HERE), (NROW, 1, USERS_HERE), (1, USERS_HERE), (1, ADS_HERE)],
-        y.reshape(1), *messages, ads, weight, pot_parts, fallback, log_demand,
-        scalars=1,
+        y.reshape(1), z.reshape(1), *messages, ads, weight, pot_parts, fallback, log_demand,
+        scalars=2,
     )
     row_parts = lax.all_to_all(row_parts, row_axes, 0, 0, tiled=True)
     row_pot, col_parts = call(

time: 112 us -> 117 us (1.045)
  waiting for transfers between devices: 8.53 us -> 0.01 us
  blocking collectives: 67.8 us -> 76 us
  starting transfers between devices: 19 us -> 25.2 us
  local copies, waits for them, and re-layouts: 6.09 us -> 3.88 us
  Pallas kernels: 7.65 us -> 9.3 us
    all_to_all x1, waiting for transfers between devices: 8.52 us -> 0.01 us  [on_device(): lax.all_to_all(jnp.broadcast_to(campaign_dual_vector_initial, (NZ, 1, SHA...]
    all_to_all x2, blocking collectives: 27.9 us -> 35.7 us  [on_device(): col_parts = lax.all_to_all(col_parts, 'z', 0, 0, tiled=True)]
    ppermute x3, starting transfers between devices: 7.19 us -> 10.3 us  [on_device(): lax.ppermute(message, 'y', [(i, (i + d) % NY) for i in range(NY)])]
    all_to_all x1, starting transfers between devices: 11.8 us -> 14.9 us  [on_device(): lax.all_to_all(jnp.broadcast_to(campaign_dual_vector_initial, (NZ, 1, SHA...]
    unnamed x10 -> x2, local copies, waits for them, and re-layouts: 2.85 us -> 0.01 us
    pallas_call x0 -> x1, Pallas kernels: none -> 2.19 us  [on_device(): pl.pallas_call(message_kernel, out_shape=jax.ShapeDtypeStruct((ROWS, 128)...]
    all_gather x1 -> x4, blocking collectives: 8.52 us -> 9.61 us  [on_device(): messages = [lax.all_gather(m, 'c') for m in [message] + messages]]
    pallas_call x6 -> x5, Pallas kernels: 7.65 us -> 7.11 us  [call(): pl.pallas_call(kernel, out_shape=[jax.ShapeDtypeStruct(s, jnp.float32) fo...]
  transfers between devices with their start and end apart: 4 -> 4, of which waited for: 1 -> 0; matrix products, arithmetic and copies ran while one was open for 4% -> 3% of each run, Pallas kernels for 0% -> 0%
where the time goes in v3:
time: 117 us; the launch traced here: 116 us
  blocking collectives  76 us (65%)
  starting transfers between devices  25.2 us (22%)
  Pallas kernels  9.3 us (8%)
  local copies, waits for them, and re-layouts  3.88 us (3%)
  between operations  1.47 us (1%)
    all_to_all x2, blocking collectives, on_device(): col_parts = lax.all_to_all(col_parts, 'z', 0, 0, tiled=True)  35.7 us
    all_to_all x2, blocking collectives, on_device(): row_parts = lax.all_to_all(row_parts, row_axes, 0, 0, tiled=True)  30.8 us
    all_to_all x1, starting transfers between devices, on_device(): lax.all_to_all(jnp.broadcast_to(campaign_dual_vector_initial, (NZ, 1, SHA...  14.9 us
    ppermute x3, starting transfers between devices, on_device(): lax.ppermute(message, 'y', [(i, (i + d) % NY) for i in range(NY)])  10.3 us
    all_gather x4, blocking collectives, on_device(): messages = [lax.all_gather(m, 'c') for m in [message] + messages]  9.61 us
    pallas_call x5, Pallas kernels, call(): pl.pallas_call(kernel, out_shape=[jax.ShapeDtypeStruct(s, jnp.float32) fo...  7.11 us
    reshape x3, local copies, waits for them, and re-layouts, of_here(): array.reshape((NZ, NS, SHARD) + shape)  2.38 us
  transfers between devices with their start and end apart: 4, of which 0 were waited for; matrix products, arithmetic and copies ran while one was open for 3% of the time, Pallas kernels for 0%

profile of v3, /device:TPU:1, one launch (start us, length us, event | category | flops | bytes accessed | tf_op | source)
XLA Modules:
  0.0 116.1 jit_solution(16806109416360567637)
XLA Ops:
  0.6 0.0 copy-start
  1.4 2.2 %shard_map.113 = f32[264,128]{1,0:T(8,128)} custom-call(s32[1,1,4]{2,1,0:T(1,128)} %eligible.1, s32[1,1]{1,0:T(1,128)S(6)} %copy.15.counts, bf16[256,128]{1,0:T(8,128)(2,1)} %embedding.1, f32[2,128]{1,0:T(2,128)} %bitcast.21, f32[2,128]{1,0:T(2,128)} %bitcast.22), custom_call_target="tpu_custom_call" | custom-call | tf_op jit(solution)/shard_map/pallas_call | solution.py:204
  3.6 5.5 %collective-permute-start.2 = (f32[264,128]{1,0:T(8,128)}, f32[264,128]{1,0:T(8,128)S(1)}, u32[]{:S(2)}, u32[]{:S(2)}) collective-permute-start(f32[264,128]{1,0:T(8,128)} %shard_map.113), channel_id=1, source_target_pairs={{0,24},{8,0},{16,8},{24,16},{1,25},{9,1},{17,9},{25,17},{2,26},{10... | collective-permute-start | bytes 405512 | tf_op jit(solution)/shard_map/ppermute | solution.py:217
  9.1 2.3 %collective-permute-start.1 = (f32[264,128]{1,0:T(8,128)}, f32[264,128]{1,0:T(8,128)S(1)}, u32[]{:S(2)}, u32[]{:S(2)}) collective-permute-start(f32[264,128]{1,0:T(8,128)} %shard_map.113), channel_id=1, source_target_pairs={{0,16},{8,24},{16,0},{24,8},{1,17},{9,25},{17,1},{25,9},{2,18},{10... | collective-permute-start | bytes 405512 | tf_op jit(solution)/shard_map/ppermute | solution.py:217
  11.3 2.6 %collective-permute-start = (f32[264,128]{1,0:T(8,128)}, f32[264,128]{1,0:T(8,128)S(1)}, u32[]{:S(2)}, u32[]{:S(2)}) collective-permute-start(f32[264,128]{1,0:T(8,128)} %shard_map.113), channel_id=1, source_target_pairs={{0,8},{8,16},{16,24},{24,0},{1,9},{9,17},{17,25},{25,1},{2,10},{10... | collective-permute-start | bytes 405512 | tf_op jit(solution)/shard_map/ppermute | solution.py:217
  13.9 1.3 %broadcast_in_dim.3 = f32[16,1,32]{2,1,0:T(1,128)} broadcast(f32[32]{0:T(128)} %param.17), dimensions={2} | broadcast | bytes 2176 | tf_op jit(solution)/shard_map/broadcast_in_dim | solution.py:201
  15.2 14.9 %all-to-all-start = ((f32[16,1,32]{2,1,0:T(1,128)}), f32[16,1,32]{2,1,0:T(1,128)S(1)}, u32[]{:S(2)}, u32[]{:S(2)}) async-start(f32[16,1,32]{2,1,0:T(1,128)} %broadcast_in_dim.3), calls=%async_computation | async-start | bytes 16384 | tf_op jit(solution)/shard_map/all_to_all | solution.py:200
  30.1 0.8 reshape.98
  30.9 0.1 mul.38.ad_weight
  31.0 0.8 reshape.100
  31.8 0.8 reshape.99
  32.6 0.1 multiply_reduce_fusion
  32.7 0.1 log2.30.log_demand
  32.8 0.1 mul.41.fallback
  32.8 0.0 copy-done
  32.9 3.6 %all-gather = f32[528,128]{1,0:T(8,128)S(1)} all-gather(f32[264,128]{1,0:T(8,128)} %shard_map.113), channel_id=2, replica_groups=mesh['z'=16,'y'=4,'c'=2,'x'=4] {'c'}, dimensions={0}, use_global_device_ids=true | all-gather | bytes 405504 | tf_op jit(solution)/shard_map/all_gather | solution.py:219
  36.5 0.0 collective-permute-done.2
  36.5 2.0 %all-gather.3 = f32[528,128]{1,0:T(8,128)S(1)} all-gather(f32[264,128]{1,0:T(8,128)S(1)} %collective-permute-done.2), channel_id=5, replica_groups=mesh['z'=16,'y'=4,'c'=2,'x'=4] {'c'}, dimensions={0}, use_global_device_ids=true | all-gather | bytes 405504 | tf_op jit(solution)/shard_map/all_gather | solution.py:219
  38.5 0.0 collective-permute-done.1
  38.5 2.0 %all-gather.2 = f32[528,128]{1,0:T(8,128)S(1)} all-gather(f32[264,128]{1,0:T(8,128)S(1)} %collective-permute-done.1), channel_id=4, replica_groups=mesh['z'=16,'y'=4,'c'=2,'x'=4] {'c'}, dimensions={0}, use_global_device_ids=true | all-gather | bytes 405504 | tf_op jit(solution)/shard_map/all_gather | solution.py:219
  40.5 0.0 collective-permute-done
  40.5 2.0 %all-gather.1 = f32[528,128]{1,0:T(8,128)S(1)} all-gather(f32[264,128]{1,0:T(8,128)S(1)} %collective-permute-done), channel_id=3, replica_groups=mesh['z'=16,'y'=4,'c'=2,'x'=4] {'c'}, dimensions={0}, use_global_device_ids=true | all-gather | bytes 405504 | tf_op jit(solution)/shard_map/all_gather | solution.py:219
  42.5 0.0 all-to-all-done.pot_parts
  42.5 3.2 %shard_map.114 = (f32[512,2048]{1,0:T(8,128)S(1)}, f32[32,1,2048]{2,1,0:T(1,128)S(1)}, f32[1,2048]{1,0:T(1,128)S(1)}, f32[1,512]{1,0:T(1,128)S(1)}) custom-call(s32[1]{0:T(128)} %bitcast.1.mine, s32[1]{0:T(128)} %bitcast.2.place.own, f32[2,264,128]{2,1,0:T(8,128)S(1)} %bitcast.16, f32[2,264,128]{2,1,0:T(8,128)S(1)} %bitcast.19, f32[2,264,128]{2,1,0:T(8,128)S(1)} %bitcast.18, ...), custom_call_target="tpu_custom_call" | custom-call | tf_op jit(solution)/shard_map/pallas_call | solution.py:175
  45.7 16.6 %all_to_all.25.parts = f32[32,1,2048]{2,1,0:T(1,128)S(1)} all-to-all(f32[32,1,2048]{2,1,0:T(1,128)S(1)} %get-tuple-element.13), channel_id=1, replica_groups=mesh['z'=16,'y'=4,'c'=2,'x'=4] {'y','c','x'}, dimensions={0} | all-to-all | bytes 524288 | tf_op jit(solution)/shard_map/all_to_all | solution.py:240
  62.4 0.9 shard_map.115
  63.3 21.7 %all_to_all.26.parts = f32[16,1,512]{2,1,0:T(1,128)S(1)} all-to-all(f32[16,1,512]{2,1,0:T(1,128)S(1)} %get-tuple-element.16), channel_id=1, replica_groups=mesh['z'=16,'y'=4,'c'=2,'x'=4] {'z'}, dimensions={0} | all-to-all | bytes 65536 | tf_op jit(solution)/shard_map/all_to_all | solution.py:246
  85.0 1.0 shard_map.116
  86.0 14.1 %all_to_all.27.parts = f32[32,1,2048]{2,1,0:T(1,128)S(1)} all-to-all(f32[32,1,2048]{2,1,0:T(1,128)S(1)} %get-tuple-element.18), channel_id=1, replica_groups=mesh['z'=16,'y'=4,'c'=2,'x'=4] {'y','c','x'}, dimensions={0} | all-to-all | bytes 524288 | tf_op jit(solution)/shard_map/all_to_all | solution.py:252
  100.1 1.3 %shard_map.117 = (f32[1,256]{1,0:T(1,128)}, f32[16,1,512]{2,1,0:T(1,128)S(1)}) custom-call(s32[1]{0:T(128)} %bitcast.own, f32[512,2048]{1,0:T(8,128)S(1)} %get-tuple-element.12.tile, f32[32,1,2048]{2,1,0:T(1,128)S(1)} %all_to_all.27.parts, f32[1,2048]{1,0:T(1,128)S(1)} %get-tuple-element.17.row_pot, f32[1,2048]{1,0:T(1,128)S(1)} %get-tuple-element.14.mass, ...), custom_call_target="tpu_custom_call" | custom-call | tf_op jit(solution)/shard_map/pallas_call | solution.py:175
  101.5 14.0 %all_to_all.28.parts = f32[16,1,512]{2,1,0:T(1,128)S(1)} all-to-all(f32[16,1,512]{2,1,0:T(1,128)S(1)} %get-tuple-element.21), channel_id=1, replica_groups=mesh['z'=16,'y'=4,'c'=2,'x'=4] {'z'}, dimensions={0} | all-to-all | bytes 65536 | tf_op jit(solution)/shard_map/all_to_all | solution.py:259
  115.4 0.6 shard_map.118
  (2 shorter events, 0.0 us)
Async XLA Ops:
  0.6 32.2 %copy-start = (bf16[4096,128]{1,0:T(8,128)(2,1)S(1)}, bf16[4096,128]{1,0:T(8,128)(2,1)}, u32[]{:S(2)}) copy-start(bf16[4096,128]{1,0:T(8,128)(2,1)} %param.13) | copy-start | bytes 3145732
  3.6 32.9 %collective-permute-start.2 = (f32[264,128]{1,0:T(8,128)}, f32[264,128]{1,0:T(8,128)S(1)}, u32[]{:S(2)}, u32[]{:S(2)}) collective-permute-start(f32[264,128]{1,0:T(8,128)} %shard_map.113), channel_id=1, source_target_pairs={{0,24},{8,0},{16,8},{24,16},{1,25},{9,1},{17,9},{25,17},{2,26},{10... | collective-permute-start | bytes 405512 | tf_op jit(solution)/shard_map/ppermute | solution.py:217
  9.1 29.5 %collective-permute-start.1 = (f32[264,128]{1,0:T(8,128)}, f32[264,128]{1,0:T(8,128)S(1)}, u32[]{:S(2)}, u32[]{:S(2)}) collective-permute-start(f32[264,128]{1,0:T(8,128)} %shard_map.113), channel_id=1, source_target_pairs={{0,16},{8,24},{16,0},{24,8},{1,17},{9,25},{17,1},{25,9},{2,18},{10... | collective-permute-start | bytes 405512 | tf_op jit(solution)/shard_map/ppermute | solution.py:217
  11.3 29.2 %collective-permute-start = (f32[264,128]{1,0:T(8,128)}, f32[264,128]{1,0:T(8,128)S(1)}, u32[]{:S(2)}, u32[]{:S(2)}) collective-permute-start(f32[264,128]{1,0:T(8,128)} %shard_map.113), channel_id=1, source_target_pairs={{0,8},{8,16},{16,24},{24,0},{1,9},{9,17},{17,25},{25,1},{2,10},{10... | collective-permute-start | bytes 405512 | tf_op jit(solution)/shard_map/ppermute | solution.py:217
  15.2 27.3 %all-to-all-start = ((f32[16,1,32]{2,1,0:T(1,128)}), f32[16,1,32]{2,1,0:T(1,128)S(1)}, u32[]{:S(2)}, u32[]{:S(2)}) async-start(f32[16,1,32]{2,1,0:T(1,128)} %broadcast_in_dim.3), calls=%async_computation | async-start | bytes 16384 | tf_op jit(solution)/shard_map/all_to_all | solution.py:200

commit v4 on v3

--- a/solution.py
+++ b/solution.py
@@ -16,6 +16,7 @@
 NZ, NY, NC, NX = 16, 4, 2, 4
 NS = NY * NC
 NROW = NS * NX
+ADS_J = 4096
 SHARD = 32
 USERS_HERE = NS * UBS
 ADS_HERE = NZ * SHARD
@@ -27,6 +28,8 @@
 LOG2E = math.log2(math.e)
 TO_BITS = LOG2E / regularizer_epsilon
 FROM_BITS = regularizer_epsilon / LOG2E
+POT_MESSAGE = 2048
+WEIGHT = TO_BITS / math.sqrt(128)
 COL_SHIFT = 64.0
 ROW_SHIFT = 100.0
 
@@ -38,38 +41,59 @@
 
 
 def message_kernel(
-    eligible, counts, embedding, scale, mass, out, embedding_here, mass_here, sems
+    eligible, counts, embedding, scale, mass, pot, ad_scale, out, pot_out, ad_scale_out,
+    eligible_here, counts_here, embedding_here, mass_here, pot_here, sems,
 ):
-    copies = [
-        pltpu.make_async_copy(embedding, embedding_here, sems.at[0]),
-        pltpu.make_async_copy(scale, out.at[pl.ds(UBS, 2), :], sems.at[1]),
-        pltpu.make_async_copy(mass, mass_here, sems.at[2]),
+    pairs = [
+        (pot, pot_here),
+        (eligible, eligible_here),
+        (counts, counts_here),
+        (mass, mass_here),
+        (scale, out.at[pl.ds(UBS, 2), :]),
+        (embedding, embedding_here),
+        (ad_scale, ad_scale_out),
     ]
+    copies = [pltpu.make_async_copy(src, dst, sems.at[i]) for i, (src, dst) in enumerate(pairs)]
     for copy in copies:
         copy.start()
+    pot_out[...] = jnp.zeros((NZ, 1, POT_MESSAGE), jnp.float32)
+    copies[0].wait()
+    pot_out[:, :, :SHARD] = jnp.broadcast_to(pot_here[...][None], (NZ, 1, SHARD))
+    copies[1].wait()
+    copies[2].wait()
     for q in range(AB_J):
         bias = jnp.float32(very_low)
         for k in range(KMAX):
-            hit = jnp.logical_and(k < counts[0, 0], eligible[0, 0, k] == q)
+            hit = jnp.logical_and(k < counts_here[0, 0], eligible_here[0, 0, k] == q)
             bias = jnp.where(hit, jnp.float32(0.0), bias)
         out[UBS + 4 + q : UBS + 5 + q, :] = jnp.full((1, 128), bias, jnp.float32)
-    for copy in copies:
-        copy.wait()
+    copies[3].wait()
+    out[UBS + 2 : UBS + 4, :] = jnp.log2(mass_here[...])
+    copies[4].wait()
+    copies[5].wait()
     out[:UBS, :] = embedding_here[...].astype(jnp.float32)
-    out[UBS + 2 : UBS + 4, :] = jnp.log2(mass_here[...])
+    copies[6].wait()
+
+
+def of_here(array, mine):
+    rows = array[pl.ds(lax.shift_right_logical(mine, 2), NZ, stride=2), :]
+    turn = lax.rem(128 - lax.rem(mine, 4) * SHARD, 128)
+    rows = pltpu.roll(rows, turn, 1)
+    return jnp.concatenate([rows[z : z + 1, :SHARD] for z in range(NZ)], axis=1)
 
 
 def tile_kernel(
-    mine, place, msg0, msg1, msg2, msg3, ads, ad_weight, pot_parts, fallback, log_demand,
-    tile, row_lse, log_mass, pot,
+    mine, place, msg0, msg1, msg2, msg3, ads, ad_scale, pot_parts, tile, row_lse, log_mass, pot
 ):
-    del place, fallback, log_demand
-    weight = as_columns(ad_weight[...])
-    pots = jnp.concatenate([pot_parts[z] for z in range(NZ)], axis=1) * TO_BITS
+    del place
+    weight = as_columns(of_here(ad_scale, mine[0]) * WEIGHT)
+    pots = jnp.concatenate(
+        [pot_parts[PLANES[0].index(z), :, :SHARD] for z in range(NZ)], axis=1
+    ) * TO_BITS
     pot[...] = pots
     pots = as_columns(pots)
     for back, msg in enumerate((msg0, msg1, msg2, msg3)):
-        first = lax.rem(mine[0] + (NY - back), NY) * NC
+        first = lax.rem(lax.shift_right_logical(mine[0], 1) + (NY - back), NY) * NC
 
         def block(c, carry, msg=msg, first=first):
             users = msg[c, :UBS, :].astype(jnp.bfloat16)
@@ -131,7 +155,11 @@
     return log_demand - (peak + jnp.log2(jnp.exp2(log_sum - peak) + jnp.exp2(fallback - peak)))
 
 
-def second_row_kernel(tile, parts, row_pot, pot, fallback, log_demand, pot_out, row_out):
+def second_row_kernel(
+    mine, tile, parts, row_pot, pot, penalty, demand, pot_out, row_out, fallback, log_demand
+):
+    fallback[...] = of_here(penalty, mine[0]) * -TO_BITS
+    log_demand[...] = jnp.log2(of_here(demand, mine[0]))
     sums = jnp.sum(parts[...], axis=0)
     new_pot = column_update(
         jnp.log2(sums) - COL_SHIFT - pot[...], fallback[...], log_demand[...]
@@ -181,6 +209,28 @@
     )(*operands)
 
 
+FIRST_Z = NZ // 2
+PLANES = [[(FIRST_Z + i) % NZ for i in range(NZ)]]
+ROW_GROUP = [
+    [
+        ((NY // 2 + i) % NY * NC + c) * NX + (NX // 2 + j) % NX
+        for i in range(NY)
+        for c in range(NC)
+        for j in range(NX)
+    ]
+]
+
+
+def over_planes(value):
+    return lax.all_to_all(value, "z", 0, 0, tiled=True, axis_index_groups=PLANES)
+
+
+def over_rows(value):
+    return lax.all_to_all(
+        value, ("y", "c", "x"), 0, 0, tiled=True, axis_index_groups=ROW_GROUP
+    )
+
+
 def on_device(
     user_embedding,
     user_scale,
@@ -193,73 +243,68 @@
     eligible,
     counts,
 ):
-    inverse_root = 1.0 / math.sqrt(user_embedding.shape[1])
     y, z = lax.axis_index("y"), lax.axis_index("z")
-    mine = y * NC + lax.axis_index("c")
-
-    pot_parts = lax.all_to_all(
-        jnp.broadcast_to(campaign_dual_vector_initial, (NZ, 1, SHARD)), "z", 0, 0, tiled=True
-    )
-
-    message = pl.pallas_call(
+    mine = (y * NC + lax.axis_index("c")).reshape(1)
+    place = z.reshape(1)
+
+    message, pot_parts, ad_scale = pl.pallas_call(
         message_kernel,
-        out_shape=jax.ShapeDtypeStruct((ROWS, 128), jnp.float32),
-        in_specs=[pl.BlockSpec(memory_space=pltpu.SMEM)] * 2
-        + [pl.BlockSpec(memory_space=pl.ANY)] * 3,
-        out_specs=pl.BlockSpec(memory_space=pltpu.VMEM),
+        out_shape=[
+            jax.ShapeDtypeStruct((ROWS, 128), jnp.float32),
+            jax.ShapeDtypeStruct((NZ, 1, POT_MESSAGE), jnp.float32),
+            jax.ShapeDtypeStruct((ADS_J // 128, 128), jnp.float32),
+        ],
+        in_specs=[pl.BlockSpec(memory_space=pltpu.HBM)] * 7,
+        out_specs=[pl.BlockSpec(memory_space=pltpu.VMEM)] * 3,
         scratch_shapes=[
+            pltpu.SMEM((1, 1, KMAX), jnp.int32),
+            pltpu.SMEM((1, 1), jnp.int32),
             pltpu.VMEM((UBS, 128), jnp.bfloat16),
             pltpu.VMEM((2, 128), jnp.float32),
-            pltpu.SemaphoreType.DMA((3,)),
+            pltpu.VMEM((1, SHARD), jnp.float32),
+            pltpu.SemaphoreType.DMA((7,)),
         ],
-    )(eligible, counts, user_embedding, user_scale.reshape(2, 128), user_mass.reshape(2, 128))
-    messages = [
-        lax.ppermute(message, "y", [(i, (i + d) % NY) for i in range(NY)]) for d in range(1, NY)
+    )(
+        eligible, counts, user_embedding, user_scale.reshape(2, 128), user_mass.reshape(2, 128),
+        campaign_dual_vector_initial.reshape(1, SHARD), ad_scale.reshape(ADS_J // 128, 128),
+    )
+    pot_parts = over_planes(pot_parts)
+    pair = lax.all_gather(message, "c")
+    messages = [pair] + [
+        lax.ppermute(pair, "y", [(i, (i + d) % NY) for i in range(NY)]) for d in range(1, NY)
     ]
-    messages = [lax.all_gather(m, "c") for m in [message] + messages]
-
-    def of_here(array):
-        shape = array.shape[1:]
-        picked = lax.dynamic_index_in_dim(
-            array.reshape((NZ, NS, SHARD) + shape), mine, 1, keepdims=False
-        )
-        return picked.reshape((ADS_HERE,) + shape)
-
-    ads = of_here(ad_embedding)
-    weight = (of_here(ad_scale) * (inverse_root * TO_BITS)).reshape(1, ADS_HERE)
-    fallback = (of_here(listing_unplaced_penalty) * -TO_BITS).reshape(1, ADS_HERE)
-    log_demand = jnp.log2(of_here(listing_view_demand)).reshape(1, ADS_HERE)
-
-    row_axes = ("y", "c", "x")
+    ads = lax.dynamic_index_in_dim(
+        ad_embedding.reshape(NZ, NS, SHARD, -1), mine[0], 1, keepdims=False
+    ).reshape(ADS_HERE, -1)
+    demand = listing_view_demand.reshape(ADS_J // 128, 128)
+    penalty = listing_unplaced_penalty.reshape(ADS_J // 128, 128)
+
     tile, row_parts, mass, pot = call(
         tile_kernel,
         [(ADS_HERE, USERS_HERE), (NROW, 1, USERS_HERE), (1, USERS_HERE), (1, ADS_HERE)],
-        y.reshape(1), z.reshape(1), *messages, ads, weight, pot_parts, fallback, log_demand,
+        mine, place, *messages, ads, ad_scale, pot_parts,
         scalars=2,
     )
-    row_parts = lax.all_to_all(row_parts, row_axes, 0, 0, tiled=True)
     row_pot, col_parts = call(
         first_column_kernel,
         [(1, USERS_HERE), (NZ, 1, ADS_HERE)],
-        tile, row_parts, mass, pot,
-    )
-    col_parts = lax.all_to_all(col_parts, "z", 0, 0, tiled=True)
-    pot, row_parts = call(
+        tile, over_rows(row_parts), mass, pot,
+    )
+    pot, row_parts, fallback, log_demand = call(
         second_row_kernel,
-        [(1, ADS_HERE), (NROW, 1, USERS_HERE)],
-        tile, col_parts, row_pot, pot, fallback, log_demand,
-    )
-    row_parts = lax.all_to_all(row_parts, row_axes, 0, 0, tiled=True)
+        [(1, ADS_HERE), (NROW, 1, USERS_HERE), (1, ADS_HERE), (1, ADS_HERE)],
+        mine, tile, over_planes(col_parts), row_pot, pot, penalty, demand,
+        scalars=1,
+    )
     users, col_parts = call(
         second_column_kernel,
         [(1, UBS), (NZ, 1, ADS_HERE)],
-        mine.reshape(1), tile, row_parts, row_pot, mass, pot,
+        mine, tile, over_rows(row_parts), row_pot, mass, pot,
         scalars=1,
     )
-    col_parts = lax.all_to_all(col_parts, "z", 0, 0, tiled=True)
     (last,) = call(
         last_kernel, [(1, SHARD)],
-        z.reshape(1), col_parts, pot, fallback, log_demand,
+        place, over_planes(col_parts), pot, fallback, log_demand,
         scalars=1,
     )
     return users.reshape(UBS), last.reshape(SHARD)

time: 117 us -> 110 us (0.940)
  blocking collectives: 76 us -> 56.6 us
  waiting for transfers between devices: 0.01 us -> 12.7 us
  starting transfers between devices: 25.2 us -> 28.6 us
  local copies, waits for them, and re-layouts: 3.88 us -> 0.75 us
    all_to_all x4, blocking collectives: 66.4 us -> 53.6 us  [the longest x2 28 us: over_planes(): lax.all_to_all(value, 'z', 0, 0, tiled=True, axis_index_groups=PLANES)]
    ppermute x3, waiting for transfers between devices: 0.01 us -> 12.7 us  [on_device(): lax.ppermute(pair, 'y', [(i, (i + d) % NY) for i in range(NY)])]
    all_gather x4 -> x1, blocking collectives: 9.61 us -> 3.07 us  [on_device(): pair = lax.all_gather(message, 'c')]
    all_to_all x1, starting transfers between devices: 14.9 us -> 19.1 us  [over_planes(): lax.all_to_all(value, 'z', 0, 0, tiled=True, axis_index_groups=PLANES)]
    reshape x3 -> x0, local copies, waits for them, and re-layouts: 2.38 us -> none  [of_here(): array.reshape((NZ, NS, SHARD) + shape)]
    broadcast_in_dim x1 -> x0, local copies, waits for them, and re-layouts: 1.25 us -> none  [on_device(): jnp.broadcast_to(campaign_dual_vector_initial, (NZ, 1, SHARD))]
  transfers between devices with their start and end apart: 4 -> 4, of which waited for: 0 -> 2; matrix products, arithmetic and copies ran while one was open for 3% -> 0% of each run, Pallas kernels for 0% -> 0%
where the time goes in v4:
time: 110 us; the launch traced here: 109 us
  blocking collectives  56.6 us (51%)
  starting transfers between devices  28.6 us (26%)
  waiting for transfers between devices  12.7 us (12%)
  Pallas kernels  8.95 us (8%)
  between operations  1.47 us (1%)
    all_to_all x2, blocking collectives, over_planes(): lax.all_to_all(value, 'z', 0, 0, tiled=True, axis_index_groups=PLANES)  28 us
    all_to_all x2, blocking collectives, over_rows(): lax.all_to_all(value, ('y', 'c', 'x'), 0, 0, tiled=True, axis_index_group...  25.6 us
    all_to_all x1, starting transfers between devices, over_planes(): lax.all_to_all(value, 'z', 0, 0, tiled=True, axis_index_groups=PLANES)  19.1 us
    ppermute x3, waiting for transfers between devices, on_device(): lax.ppermute(pair, 'y', [(i, (i + d) % NY) for i in range(NY)])  12.7 us
    ppermute x3, starting transfers between devices, on_device(): lax.ppermute(pair, 'y', [(i, (i + d) % NY) for i in range(NY)])  9.49 us
    pallas_call x5, Pallas kernels, call(): pl.pallas_call(kernel, out_shape=[jax.ShapeDtypeStruct(s, jnp.float32) fo...  7.28 us
    all_gather x1, blocking collectives, on_device(): pair = lax.all_gather(message, 'c')  3.07 us
  transfers between devices with their start and end apart: 4, of which 2 were waited for; matrix products, arithmetic and copies ran while one was open for 0% of the time, Pallas kernels for 0%

profile of v4, /device:TPU:1, one launch (start us, length us, event | category | flops | bytes accessed | tf_op | source)
XLA Modules:
  0.0 109.1 jit_solution(910136021218101224)
XLA Ops:
  0.6 0.0 copy-start
  0.6 0.0 copy-start.1
  0.7 0.0 copy-start.2
  1.4 1.7 %shard_map.113 = (f32[264,128]{1,0:T(8,128)}, f32[16,1,2048]{2,1,0:T(1,128)}, f32[32,128]{1,0:T(8,128)}) custom-call(s32[1,1,4]{2,1,0:T(1,128)} %eligible.1, s32[1,1]{1,0:T(1,128)S(6)} %copy.14.counts, bf16[256,128]{1,0:T(8,128)(2,1)} %embedding.1, f32[2,128]{1,0:T(2,128)} %bitcast.24, f32[2,128]{1,0:T(2,128)} %bitcast.25, f32[1,32]{1,0:T(1,128)} %bitcast.26, ...), custom_call_target="tpu_custom_call" | custom-call | tf_op jit(solution)/shard_map/pallas_call | solution.py:250
  3.1 19.1 %all-to-all-start = ((f32[16,1,2048]{2,1,0:T(1,128)}), f32[16,1,2048]{2,1,0:T(1,128)S(1)}, u32[]{:S(2)}, u32[]{:S(2)}) async-start(f32[16,1,2048]{2,1,0:T(1,128)} %get-tuple-element.19), calls=%async_computation | async-start | bytes 262144 | tf_op jit(solution)/shard_map/all_to_all | solution.py:225
  22.2 3.1 %all-gather = f32[528,128]{1,0:T(8,128)S(1)} all-gather(f32[264,128]{1,0:T(8,128)} %get-tuple-element.17), channel_id=2, replica_groups=mesh['z'=16,'y'=4,'c'=2,'x'=4] {'c'}, dimensions={0}, use_global_device_ids=true | all-gather | bytes 405504 | tf_op jit(solution)/shard_map/all_gather | solution.py:272
  25.3 4.6 %collective-permute-start.2 = (f32[2,264,128]{2,1,0:T(8,128)S(1)}, f32[2,264,128]{2,1,0:T(8,128)S(1)}, u32[]{:S(2)}, u32[]{:S(2)}) collective-permute-start(f32[2,264,128]{2,1,0:T(8,128)S(1)} %bitcast.16), channel_id=1, source_target_pairs={{0,24},{8,0},{16,8},{24,16},{1,25},{9,1},{17,9},{25,17},{2,26},{10... | collective-permute-start | bytes 811016 | tf_op jit(solution)/shard_map/ppermute | solution.py:274
  29.9 2.3 %collective-permute-start.1 = (f32[2,264,128]{2,1,0:T(8,128)S(1)}, f32[2,264,128]{2,1,0:T(8,128)S(1)}, u32[]{:S(2)}, u32[]{:S(2)}) collective-permute-start(f32[2,264,128]{2,1,0:T(8,128)S(1)} %bitcast.17), channel_id=1, source_target_pairs={{0,16},{8,24},{16,0},{24,8},{1,17},{9,25},{17,1},{25,9},{2,18},{10... | collective-permute-start | bytes 811016 | tf_op jit(solution)/shard_map/ppermute | solution.py:274
  32.2 2.6 %collective-permute-start = (f32[2,264,128]{2,1,0:T(8,128)S(1)}, f32[2,264,128]{2,1,0:T(8,128)S(1)}, u32[]{:S(2)}, u32[]{:S(2)}) collective-permute-start(f32[2,264,128]{2,1,0:T(8,128)S(1)} %bitcast.18), channel_id=1, source_target_pairs={{0,8},{8,16},{16,24},{24,0},{1,9},{9,17},{17,25},{25,1},{2,10},{10... | collective-permute-start | bytes 811016 | tf_op jit(solution)/shard_map/ppermute | solution.py:274
  34.8 0.0 copy-done
  34.8 6.2 %collective-permute-done.2.msg3 = f32[2,264,128]{2,1,0:T(8,128)S(1)} collective-permute-done((f32[2,264,128]{2,1,0:T(8,128)S(1)}, f32[2,264,128]{2,1,0:T(8,128)S(1)}, u32[]{:S(2)}, u32[]{:S(2)}) %collective-permute-start.2) | collective-permute-done | bytes 270368 | tf_op jit(solution)/shard_map/ppermute | solution.py:274
  41.1 0.0 collective-permute-done.1.msg2
  41.1 6.5 %collective-permute-done.msg1 = f32[2,264,128]{2,1,0:T(8,128)S(1)} collective-permute-done((f32[2,264,128]{2,1,0:T(8,128)S(1)}, f32[2,264,128]{2,1,0:T(8,128)S(1)}, u32[]{:S(2)}, u32[]{:S(2)}) %collective-permute-start) | collective-permute-done | bytes 270368 | tf_op jit(solution)/shard_map/ppermute | solution.py:274
  47.5 0.0 all-to-all-done.pot_parts
  47.5 0.0 copy-start.3
  47.5 0.7 copy-done.3
  48.2 3.3 %shard_map.114 = (f32[512,2048]{1,0:T(8,128)S(1)}, f32[32,1,2048]{2,1,0:T(1,128)S(1)}, f32[1,2048]{1,0:T(1,128)S(1)}, f32[1,512]{1,0:T(1,128)S(1)}) custom-call(s32[1]{0:T(128)} %bitcast.mine.own, s32[1]{0:T(128)} %bitcast.1.place.own, f32[2,264,128]{2,1,0:T(8,128)S(1)} %bitcast.19, f32[2,264,128]{2,1,0:T(8,128)S(1)} %collective-permute-done.msg1, ...), custom_call_target="tpu_custom_call" | custom-call | tf_op jit(solution)/shard_map/pallas_call | solution.py:203
  51.6 12.0 %all_to_all.25.parts = f32[32,1,2048]{2,1,0:T(1,128)S(1)} all-to-all(f32[32,1,2048]{2,1,0:T(1,128)S(1)} %get-tuple-element.21), channel_id=1, replica_groups={{18,19,16,17,22,23,20,21,26,27,24,25,30,31,28,29,2,3,0,1,6,7,4,5,10,11,..., dimensions={0} | all-to-all | bytes 524288 | tf_op jit(solution)/shard_map/all_to_all | solution.py:229
  63.6 0.9 shard_map.115
  64.6 13.7 %all_to_all.26.parts = f32[16,1,512]{2,1,0:T(1,128)S(1)} all-to-all(f32[16,1,512]{2,1,0:T(1,128)S(1)} %get-tuple-element.24), channel_id=1, replica_groups={{256,288,320,352,384,416,448,480,0,32,64,96,128,160,192,224},{257,289,3..., dimensions={0} | all-to-all | bytes 65536 | tf_op jit(solution)/shard_map/all_to_all | solution.py:225
  78.3 0.0 copy-done.1
  78.3 0.0 copy-done.2
  78.3 1.0 shard_map.116
  79.3 13.5 %all_to_all.27.parts = f32[32,1,2048]{2,1,0:T(1,128)S(1)} all-to-all(f32[32,1,2048]{2,1,0:T(1,128)S(1)} %get-tuple-element.26), channel_id=1, replica_groups={{18,19,16,17,22,23,20,21,26,27,24,25,30,31,28,29,2,3,0,1,6,7,4,5,10,11,..., dimensions={0} | all-to-all | bytes 524288 | tf_op jit(solution)/shard_map/all_to_all | solution.py:229
  92.9 1.3 %shard_map.117 = (f32[1,256]{1,0:T(1,128)}, f32[16,1,512]{2,1,0:T(1,128)S(1)}) custom-call(s32[1]{0:T(128)} %bitcast.mine.own, f32[512,2048]{1,0:T(8,128)S(1)} %get-tuple-element.20.tile, f32[32,1,2048]{2,1,0:T(1,128)S(1)} %all_to_all.27.parts, f32[1,2048]{1,0:T(1,128)S(1)} %get-tuple-element.25.row_pot, f32[1,2048]{1,0:T(1,128)S(1)} %get-tuple-element.22.mass, ...), custom_call_target="tpu_custom_call" | custom-call | tf_op jit(solution)/shard_map/pallas_call | solution.py:203
  94.2 14.3 %all_to_all.28.parts = f32[16,1,512]{2,1,0:T(1,128)S(1)} all-to-all(f32[16,1,512]{2,1,0:T(1,128)S(1)} %get-tuple-element.29), channel_id=1, replica_groups={{256,288,320,352,384,416,448,480,0,32,64,96,128,160,192,224},{257,289,3..., dimensions={0} | all-to-all | bytes 65536 | tf_op jit(solution)/shard_map/all_to_all | solution.py:225
  108.5 0.6 shard_map.118
  (1 shorter events, 0.0 us)
Async XLA Ops:
  0.6 34.2 %copy-start = (bf16[4096,128]{1,0:T(8,128)(2,1)S(1)}, bf16[4096,128]{1,0:T(8,128)(2,1)}, u32[]{:S(2)}) copy-start(bf16[4096,128]{1,0:T(8,128)(2,1)} %param.13) | copy-start | bytes 3145732
  0.6 77.6 %copy-start.1 = (f32[4096]{0:T(1024)S(1)}, f32[4096]{0:T(1024)}, u32[]{:S(2)}) copy-start(f32[4096]{0:T(1024)} %param.16) | copy-start | bytes 49156
  0.7 77.6 %copy-start.2 = (f32[4096]{0:T(1024)S(1)}, f32[4096]{0:T(1024)}, u32[]{:S(2)}) copy-start(f32[4096]{0:T(1024)} %param.15) | copy-start | bytes 49156
  3.1 44.4 %all-to-all-start = ((f32[16,1,2048]{2,1,0:T(1,128)}), f32[16,1,2048]{2,1,0:T(1,128)S(1)}, u32[]{:S(2)}, u32[]{:S(2)}) async-start(f32[16,1,2048]{2,1,0:T(1,128)} %get-tuple-element.19), calls=%async_computation | async-start | bytes 262144 | tf_op jit(solution)/shard_map/all_to_all | solution.py:225
  25.3 15.8 %collective-permute-start.2 = (f32[2,264,128]{2,1,0:T(8,128)S(1)}, f32[2,264,128]{2,1,0:T(8,128)S(1)}, u32[]{:S(2)}, u32[]{:S(2)}) collective-permute-start(f32[2,264,128]{2,1,0:T(8,128)S(1)} %bitcast.16), channel_id=1, source_target_pairs={{0,24},{8,0},{16,8},{24,16},{1,25},{9,1},{17,9},{25,17},{2,26},{10... | collective-permute-start | bytes 811016 | tf_op jit(solution)/shard_map/ppermute | solution.py:274
  29.9 11.1 %collective-permute-start.1 = (f32[2,264,128]{2,1,0:T(8,128)S(1)}, f32[2,264,128]{2,1,0:T(8,128)S(1)}, u32[]{:S(2)}, u32[]{:S(2)}) collective-permute-start(f32[2,264,128]{2,1,0:T(8,128)S(1)} %bitcast.17), channel_id=1, source_target_pairs={{0,16},{8,24},{16,0},{24,8},{1,17},{9,25},{17,1},{25,9},{2,18},{10... | collective-permute-start | bytes 811016 | tf_op jit(solution)/shard_map/ppermute | solution.py:274
  32.2 15.3 %collective-permute-start = (f32[2,264,128]{2,1,0:T(8,128)S(1)}, f32[2,264,128]{2,1,0:T(8,128)S(1)}, u32[]{:S(2)}, u32[]{:S(2)}) collective-permute-start(f32[2,264,128]{2,1,0:T(8,128)S(1)} %bitcast.18), channel_id=1, source_target_pairs={{0,8},{8,16},{16,24},{24,0},{1,9},{9,17},{17,25},{25,1},{2,10},{10... | collective-permute-start | bytes 811016 | tf_op jit(solution)/shard_map/ppermute | solution.py:274
  47.5 0.7 copy-start.3

commit v5 on v4

--- a/solution.py
+++ b/solution.py
@@ -28,7 +28,7 @@
 LOG2E = math.log2(math.e)
 TO_BITS = LOG2E / regularizer_epsilon
 FROM_BITS = regularizer_epsilon / LOG2E
-POT_MESSAGE = 2048
+POT_MESSAGE = 32
 WEIGHT = TO_BITS / math.sqrt(128)
 COL_SHIFT = 64.0
 ROW_SHIFT = 100.0

time: 110 us -> 101 us (0.918)
  waiting for transfers between devices: 12.7 us -> 1.52 us
  blocking collectives: 56.6 us -> 65.4 us
  starting transfers between devices: 28.6 us -> 22.4 us
    ppermute x3, waiting for transfers between devices: 12.7 us -> 0.01 us  [on_device(): lax.ppermute(pair, 'y', [(i, (i + d) % NY) for i in range(NY)])]
    all_gather x1, blocking collectives: 3.07 us -> 8.73 us  [on_device(): pair = lax.all_gather(message, 'c')]
    all_to_all x1, starting transfers between devices: 19.1 us -> 15.2 us  [over_planes(): lax.all_to_all(value, 'z', 0, 0, tiled=True, axis_index_groups=PLANES)]
    all_to_all x2, blocking collectives: 25.6 us -> 27.9 us  [over_rows(): lax.all_to_all(value, ('y', 'c', 'x'), 0, 0, tiled=True, axis_index_group...]
    ppermute x3, starting transfers between devices: 9.49 us -> 7.19 us  [on_device(): lax.ppermute(pair, 'y', [(i, (i + d) % NY) for i in range(NY)])]
    all_to_all x1, waiting for transfers between devices: 0.01 us -> 1.51 us  [over_planes(): lax.all_to_all(value, 'z', 0, 0, tiled=True, axis_index_groups=PLANES)]
  transfers between devices with their start and end apart: 4 -> 4, of which waited for: 2 -> 1; matrix products, arithmetic and copies ran while one was open for 0% -> 0% of each run, Pallas kernels for 0% -> 0%
where the time goes in v5:
time: 101 us; the launch traced here: 100 us
  blocking collectives  65.4 us (65%)
  starting transfers between devices  22.4 us (22%)
  Pallas kernels  8.91 us (9%)
  waiting for transfers between devices  1.52 us (2%)
  between operations  1.47 us (1%)
    all_to_all x2, blocking collectives, over_planes(): lax.all_to_all(value, 'z', 0, 0, tiled=True, axis_index_groups=PLANES)  28.8 us
    all_to_all x2, blocking collectives, over_rows(): lax.all_to_all(value, ('y', 'c', 'x'), 0, 0, tiled=True, axis_index_group...  27.9 us
    all_to_all x1, starting transfers between devices, over_planes(): lax.all_to_all(value, 'z', 0, 0, tiled=True, axis_index_groups=PLANES)  15.2 us
    all_gather x1, blocking collectives, on_device(): pair = lax.all_gather(message, 'c')  8.73 us
    pallas_call x5, Pallas kernels, call(): pl.pallas_call(kernel, out_shape=[jax.ShapeDtypeStruct(s, jnp.float32) fo...  7.28 us
    ppermute x3, starting transfers between devices, on_device(): lax.ppermute(pair, 'y', [(i, (i + d) % NY) for i in range(NY)])  7.19 us
  transfers between devices with their start and end apart: 4, of which 1 were waited for; matrix products, arithmetic and copies ran while one was open for 0% of the time, Pallas kernels for 0%

profile of v5, /device:TPU:1, one launch (start us, length us, event | category | flops | bytes accessed | tf_op | source)
XLA Modules:
  0.0 100.5 jit_solution(7961681952512185960)
XLA Ops:
  0.6 0.0 copy-start
  0.6 0.0 copy-start.1
  0.7 0.0 copy-start.2
  1.4 1.6 %shard_map.113 = (f32[264,128]{1,0:T(8,128)}, f32[16,1,32]{2,1,0:T(1,128)}, f32[32,128]{1,0:T(8,128)}) custom-call(s32[1,1,4]{2,1,0:T(1,128)} %eligible.1, s32[1,1]{1,0:T(1,128)S(6)} %copy.14.counts, bf16[256,128]{1,0:T(8,128)(2,1)} %embedding.1, f32[2,128]{1,0:T(2,128)} %bitcast.24, f32[2,128]{1,0:T(2,128)} %bitcast.25, f32[1,32]{1,0:T(1,128)} %bitcast.26, ...), custom_call_target="tpu_custom_call" | custom-call | tf_op jit(solution)/shard_map/pallas_call | solution.py:250
  3.0 8.7 %all-gather = f32[528,128]{1,0:T(8,128)S(1)} all-gather(f32[264,128]{1,0:T(8,128)} %get-tuple-element.17), channel_id=2, replica_groups=mesh['z'=16,'y'=4,'c'=2,'x'=4] {'c'}, dimensions={0}, use_global_device_ids=true | all-gather | bytes 405504 | tf_op jit(solution)/shard_map/all_gather | solution.py:272
  11.8 1.9 %collective-permute-start.2 = (f32[2,264,128]{2,1,0:T(8,128)S(1)}, f32[2,264,128]{2,1,0:T(8,128)S(1)}, u32[]{:S(2)}, u32[]{:S(2)}) collective-permute-start(f32[2,264,128]{2,1,0:T(8,128)S(1)} %bitcast.16), channel_id=1, source_target_pairs={{0,24},{8,0},{16,8},{24,16},{1,25},{9,1},{17,9},{25,17},{2,26},{10... | collective-permute-start | bytes 811016 | tf_op jit(solution)/shard_map/ppermute | solution.py:274
  13.7 1.9 %collective-permute-start.1 = (f32[2,264,128]{2,1,0:T(8,128)S(1)}, f32[2,264,128]{2,1,0:T(8,128)S(1)}, u32[]{:S(2)}, u32[]{:S(2)}) collective-permute-start(f32[2,264,128]{2,1,0:T(8,128)S(1)} %bitcast.17), channel_id=1, source_target_pairs={{0,16},{8,24},{16,0},{24,8},{1,17},{9,25},{17,1},{25,9},{2,18},{10... | collective-permute-start | bytes 811016 | tf_op jit(solution)/shard_map/ppermute | solution.py:274
  15.6 3.4 %collective-permute-start = (f32[2,264,128]{2,1,0:T(8,128)S(1)}, f32[2,264,128]{2,1,0:T(8,128)S(1)}, u32[]{:S(2)}, u32[]{:S(2)}) collective-permute-start(f32[2,264,128]{2,1,0:T(8,128)S(1)} %bitcast.18), channel_id=1, source_target_pairs={{0,8},{8,16},{16,24},{24,0},{1,9},{9,17},{17,25},{25,1},{2,10},{10... | collective-permute-start | bytes 811016 | tf_op jit(solution)/shard_map/ppermute | solution.py:274
  19.0 15.2 %all-to-all-start = ((f32[16,1,32]{2,1,0:T(1,128)}), f32[16,1,32]{2,1,0:T(1,128)S(1)}, u32[]{:S(2)}, u32[]{:S(2)}) async-start(f32[16,1,32]{2,1,0:T(1,128)} %get-tuple-element.19), calls=%async_computation | async-start | bytes 16384 | tf_op jit(solution)/shard_map/all_to_all | solution.py:225
  34.2 0.0 copy-done
  34.2 1.5 %all-to-all-done.pot_parts = f32[16,1,32]{2,1,0:T(1,128)S(1)} async-done(((f32[16,1,32]{2,1,0:T(1,128)}), f32[16,1,32]{2,1,0:T(1,128)S(1)}, u32[]{:S(2)}, u32[]{:S(2)}) %all-to-all-start) | async-done | bytes 2080 | tf_op jit(solution)/shard_map/all_to_all | solution.py:225
  35.8 0.0 collective-permute-done.2.msg3
  35.8 0.0 collective-permute-done.1.msg2
  35.8 0.0 collective-permute-done.msg1
  35.8 0.0 copy-start.3
  35.8 0.7 copy-done.3
  36.5 3.3 %shard_map.114 = (f32[512,2048]{1,0:T(8,128)S(1)}, f32[32,1,2048]{2,1,0:T(1,128)S(1)}, f32[1,2048]{1,0:T(1,128)S(1)}, f32[1,512]{1,0:T(1,128)S(1)}) custom-call(s32[1]{0:T(128)} %bitcast.mine.own, s32[1]{0:T(128)} %bitcast.1.place.own, f32[2,264,128]{2,1,0:T(8,128)S(1)} %bitcast.19, f32[2,264,128]{2,1,0:T(8,128)S(1)} %collective-permute-done.msg1, ...), custom_call_target="tpu_custom_call" | custom-call | tf_op jit(solution)/shard_map/pallas_call | solution.py:203
  39.8 14.6 %all_to_all.25.parts = f32[32,1,2048]{2,1,0:T(1,128)S(1)} all-to-all(f32[32,1,2048]{2,1,0:T(1,128)S(1)} %get-tuple-element.21), channel_id=1, replica_groups={{18,19,16,17,22,23,20,21,26,27,24,25,30,31,28,29,2,3,0,1,6,7,4,5,10,11,..., dimensions={0} | all-to-all | bytes 524288 | tf_op jit(solution)/shard_map/all_to_all | solution.py:229
  54.5 0.9 shard_map.115
  55.4 14.6 %all_to_all.26.parts = f32[16,1,512]{2,1,0:T(1,128)S(1)} all-to-all(f32[16,1,512]{2,1,0:T(1,128)S(1)} %get-tuple-element.24), channel_id=1, replica_groups={{256,288,320,352,384,416,448,480,0,32,64,96,128,160,192,224},{257,289,3..., dimensions={0} | all-to-all | bytes 65536 | tf_op jit(solution)/shard_map/all_to_all | solution.py:225
  70.0 0.0 copy-done.1
  70.0 0.0 copy-done.2
  70.0 1.0 %shard_map.116 = (f32[1,512]{1,0:T(1,128)S(1)}, f32[32,1,2048]{2,1,0:T(1,128)S(1)}, f32[1,512]{1,0:T(1,128)S(1)}, f32[1,512]{1,0:T(1,128)S(1)}) custom-call(s32[1]{0:T(128)} %bitcast.mine.own, f32[512,2048]{1,0:T(8,128)S(1)} %get-tuple-element.20.tile, f32[16,1,512]{2,1,0:T(1,128)S(1)} %all_to_all.26.parts, f32[1,2048]{1,0:T(1,128)S(1)} %get-tuple-element.25.row_pot, ...), custom_call_target="tpu_custom_call" | custom-call | tf_op jit(solution)/shard_map/pallas_call | solution.py:203
  71.1 13.3 %all_to_all.27.parts = f32[32,1,2048]{2,1,0:T(1,128)S(1)} all-to-all(f32[32,1,2048]{2,1,0:T(1,128)S(1)} %get-tuple-element.26), channel_id=1, replica_groups={{18,19,16,17,22,23,20,21,26,27,24,25,30,31,28,29,2,3,0,1,6,7,4,5,10,11,..., dimensions={0} | all-to-all | bytes 524288 | tf_op jit(solution)/shard_map/all_to_all | solution.py:229
  84.3 1.3 %shard_map.117 = (f32[1,256]{1,0:T(1,128)}, f32[16,1,512]{2,1,0:T(1,128)S(1)}) custom-call(s32[1]{0:T(128)} %bitcast.mine.own, f32[512,2048]{1,0:T(8,128)S(1)} %get-tuple-element.20.tile, f32[32,1,2048]{2,1,0:T(1,128)S(1)} %all_to_all.27.parts, f32[1,2048]{1,0:T(1,128)S(1)} %get-tuple-element.25.row_pot, f32[1,2048]{1,0:T(1,128)S(1)} %get-tuple-element.22.mass, ...), custom_call_target="tpu_custom_call" | custom-call | tf_op jit(solution)/shard_map/pallas_call | solution.py:203
  85.7 14.2 %all_to_all.28.parts = f32[16,1,512]{2,1,0:T(1,128)S(1)} all-to-all(f32[16,1,512]{2,1,0:T(1,128)S(1)} %get-tuple-element.29), channel_id=1, replica_groups={{256,288,320,352,384,416,448,480,0,32,64,96,128,160,192,224},{257,289,3..., dimensions={0} | all-to-all | bytes 65536 | tf_op jit(solution)/shard_map/all_to_all | solution.py:225
  99.8 0.6 shard_map.118
  (1 shorter events, 0.0 us)
Async XLA Ops:
  0.6 33.6 %copy-start = (bf16[4096,128]{1,0:T(8,128)(2,1)S(1)}, bf16[4096,128]{1,0:T(8,128)(2,1)}, u32[]{:S(2)}) copy-start(bf16[4096,128]{1,0:T(8,128)(2,1)} %param.13) | copy-start | bytes 3145732
  0.6 69.4 %copy-start.1 = (f32[4096]{0:T(1024)S(1)}, f32[4096]{0:T(1024)}, u32[]{:S(2)}) copy-start(f32[4096]{0:T(1024)} %param.16) | copy-start | bytes 49156
  0.7 69.4 %copy-start.2 = (f32[4096]{0:T(1024)S(1)}, f32[4096]{0:T(1024)}, u32[]{:S(2)}) copy-start(f32[4096]{0:T(1024)} %param.15) | copy-start | bytes 49156
  11.8 24.0 %collective-permute-start.2 = (f32[2,264,128]{2,1,0:T(8,128)S(1)}, f32[2,264,128]{2,1,0:T(8,128)S(1)}, u32[]{:S(2)}, u32[]{:S(2)}) collective-permute-start(f32[2,264,128]{2,1,0:T(8,128)S(1)} %bitcast.16), channel_id=1, source_target_pairs={{0,24},{8,0},{16,8},{24,16},{1,25},{9,1},{17,9},{25,17},{2,26},{10... | collective-permute-start | bytes 811016 | tf_op jit(solution)/shard_map/ppermute | solution.py:274
  13.7 22.1 %collective-permute-start.1 = (f32[2,264,128]{2,1,0:T(8,128)S(1)}, f32[2,264,128]{2,1,0:T(8,128)S(1)}, u32[]{:S(2)}, u32[]{:S(2)}) collective-permute-start(f32[2,264,128]{2,1,0:T(8,128)S(1)} %bitcast.17), channel_id=1, source_target_pairs={{0,16},{8,24},{16,0},{24,8},{1,17},{9,25},{17,1},{25,9},{2,18},{10... | collective-permute-start | bytes 811016 | tf_op jit(solution)/shard_map/ppermute | solution.py:274
  15.6 20.2 %collective-permute-start = (f32[2,264,128]{2,1,0:T(8,128)S(1)}, f32[2,264,128]{2,1,0:T(8,128)S(1)}, u32[]{:S(2)}, u32[]{:S(2)}) collective-permute-start(f32[2,264,128]{2,1,0:T(8,128)S(1)} %bitcast.18), channel_id=1, source_target_pairs={{0,8},{8,16},{16,24},{24,0},{1,9},{9,17},{17,25},{25,1},{2,10},{10... | collective-permute-start | bytes 811016 | tf_op jit(solution)/shard_map/ppermute | solution.py:274
  19.0 16.8 %all-to-all-start = ((f32[16,1,32]{2,1,0:T(1,128)}), f32[16,1,32]{2,1,0:T(1,128)S(1)}, u32[]{:S(2)}, u32[]{:S(2)}) async-start(f32[16,1,32]{2,1,0:T(1,128)} %get-tuple-element.19), calls=%async_computation | async-start | bytes 16384 | tf_op jit(solution)/shard_map/all_to_all | solution.py:225
  35.8 0.7 copy-start.3

commit v6 on v5

--- a/solution.py
+++ b/solution.py
@@ -28,7 +28,6 @@
 LOG2E = math.log2(math.e)
 TO_BITS = LOG2E / regularizer_epsilon
 FROM_BITS = regularizer_epsilon / LOG2E
-POT_MESSAGE = 32
 WEIGHT = TO_BITS / math.sqrt(128)
 COL_SHIFT = 64.0
 ROW_SHIFT = 100.0
@@ -41,7 +40,7 @@
 
 
 def message_kernel(
-    eligible, counts, embedding, scale, mass, pot, ad_scale, out, pot_out, ad_scale_out,
+    eligible, counts, embedding, scale, mass, pot, out, pot_out,
     eligible_here, counts_here, embedding_here, mass_here, pot_here, sems,
 ):
     pairs = [
@@ -51,14 +50,12 @@
         (mass, mass_here),
         (scale, out.at[pl.ds(UBS, 2), :]),
         (embedding, embedding_here),
-        (ad_scale, ad_scale_out),
     ]
     copies = [pltpu.make_async_copy(src, dst, sems.at[i]) for i, (src, dst) in enumerate(pairs)]
     for copy in copies:
         copy.start()
-    pot_out[...] = jnp.zeros((NZ, 1, POT_MESSAGE), jnp.float32)
     copies[0].wait()
-    pot_out[:, :, :SHARD] = jnp.broadcast_to(pot_here[...][None], (NZ, 1, SHARD))
+    pot_out[...] = jnp.broadcast_to(pot_here[...][None], (NZ, 1, SHARD))
     copies[1].wait()
     copies[2].wait()
     for q in range(AB_J):
@@ -72,7 +69,6 @@
     copies[4].wait()
     copies[5].wait()
     out[:UBS, :] = embedding_here[...].astype(jnp.float32)
-    copies[6].wait()
 
 
 def of_here(array, mine):
@@ -83,19 +79,19 @@
 
 
 def tile_kernel(
-    mine, place, msg0, msg1, msg2, msg3, ads, ad_scale, pot_parts, tile, row_lse, log_mass, pot
+    mine, place, msg0, msg1, msg2, msg3, ads, ad_weight, pot_parts, tile, row_lse, log_mass, pot
 ):
     del place
-    weight = as_columns(of_here(ad_scale, mine[0]) * WEIGHT)
+    weight = as_columns(of_here(ad_weight, mine[0]))
     pots = jnp.concatenate(
-        [pot_parts[PLANES[0].index(z), :, :SHARD] for z in range(NZ)], axis=1
+        [pot_parts[PLANES[0].index(z)] for z in range(NZ)], axis=1
     ) * TO_BITS
     pot[...] = pots
     pots = as_columns(pots)
     for back, msg in enumerate((msg0, msg1, msg2, msg3)):
         first = lax.rem(lax.shift_right_logical(mine[0], 1) + (NY - back), NY) * NC
 
-        def block(c, carry, msg=msg, first=first):
+        for c in range(NC):
             users = msg[c, :UBS, :].astype(jnp.bfloat16)
             scale = jnp.concatenate(
                 [msg[c, UBS : UBS + 1, :], msg[c, UBS + 1 : UBS + 2, :]], axis=1
@@ -124,9 +120,6 @@
             total = sum(t * jnp.exp2(p - peak) for p, t in zip(peaks, totals))
             lse = peak + jnp.log2(total)
             row_lse[:, :, at] = jnp.broadcast_to(lse[None], (NROW, 1, UBS))
-            return carry
-
-        lax.fori_loop(0, NC, block, 0)
 
 
 def column_sums(tile, row_pot, pots):
@@ -247,42 +240,43 @@
     mine = (y * NC + lax.axis_index("c")).reshape(1)
     place = z.reshape(1)
 
-    message, pot_parts, ad_scale = pl.pallas_call(
+    message, pot_parts = pl.pallas_call(
         message_kernel,
         out_shape=[
             jax.ShapeDtypeStruct((ROWS, 128), jnp.float32),
-            jax.ShapeDtypeStruct((NZ, 1, POT_MESSAGE), jnp.float32),
-            jax.ShapeDtypeStruct((ADS_J // 128, 128), jnp.float32),
+            jax.ShapeDtypeStruct((NZ, 1, SHARD), jnp.float32),
         ],
-        in_specs=[pl.BlockSpec(memory_space=pltpu.HBM)] * 7,
-        out_specs=[pl.BlockSpec(memory_space=pltpu.VMEM)] * 3,
+        in_specs=[pl.BlockSpec(memory_space=pltpu.HBM)] * 6,
+        out_specs=[pl.BlockSpec(memory_space=pltpu.VMEM)] * 2,
         scratch_shapes=[
             pltpu.SMEM((1, 1, KMAX), jnp.int32),
             pltpu.SMEM((1, 1), jnp.int32),
             pltpu.VMEM((UBS, 128), jnp.bfloat16),
             pltpu.VMEM((2, 128), jnp.float32),
             pltpu.VMEM((1, SHARD), jnp.float32),
-            pltpu.SemaphoreType.DMA((7,)),
+            pltpu.SemaphoreType.DMA((6,)),
         ],
     )(
         eligible, counts, user_embedding, user_scale.reshape(2, 128), user_mass.reshape(2, 128),
-        campaign_dual_vector_initial.reshape(1, SHARD), ad_scale.reshape(ADS_J // 128, 128),
+        campaign_dual_vector_initial.reshape(1, SHARD),
     )
     pot_parts = over_planes(pot_parts)
     pair = lax.all_gather(message, "c")
-    messages = [pair] + [
-        lax.ppermute(pair, "y", [(i, (i + d) % NY) for i in range(NY)]) for d in range(1, NY)
-    ]
+    behind = {
+        d: lax.ppermute(pair, "y", [(i, (i + d) % NY) for i in range(NY)]) for d in (1, 2, 3)
+    }
+    messages = [pair, behind[1], behind[2], behind[3]]
     ads = lax.dynamic_index_in_dim(
         ad_embedding.reshape(NZ, NS, SHARD, -1), mine[0], 1, keepdims=False
     ).reshape(ADS_HERE, -1)
+    ad_weight = ad_scale.reshape(ADS_J // 128, 128) * WEIGHT
     demand = listing_view_demand.reshape(ADS_J // 128, 128)
     penalty = listing_unplaced_penalty.reshape(ADS_J // 128, 128)
 
     tile, row_parts, mass, pot = call(
         tile_kernel,
         [(ADS_HERE, USERS_HERE), (NROW, 1, USERS_HERE), (1, USERS_HERE), (1, ADS_HERE)],
-        mine, place, *messages, ads, ad_scale, pot_parts,
+        mine, place, *messages, ads, ad_weight, pot_parts,
         scalars=2,
     )
     row_pot, col_parts = call(

time: 101 us -> 98.9 us (0.979)
  Pallas kernels: 8.91 us -> 7.47 us
    pallas_call x5, Pallas kernels: 7.28 us -> 5.87 us  [call(): pl.pallas_call(kernel, out_shape=[jax.ShapeDtypeStruct(s, jnp.float32) fo...]
  transfers between devices with their start and end apart: 4 -> 4, of which waited for: 1 -> 1; matrix products, arithmetic and copies ran while one was open for 0% -> 1% of each run, Pallas kernels for 0% -> 0%
where the time goes in v6:
time: 98.9 us; the launch traced here: 98.4 us
  blocking collectives  65.5 us (66%)
  starting transfers between devices  22.4 us (23%)
  Pallas kernels  7.47 us (8%)
  between operations  1.46 us (1%)
    all_to_all x2, blocking collectives, over_planes(): lax.all_to_all(value, 'z', 0, 0, tiled=True, axis_index_groups=PLANES)  28.9 us
    all_to_all x2, blocking collectives, over_rows(): lax.all_to_all(value, ('y', 'c', 'x'), 0, 0, tiled=True, axis_index_group...  27.8 us
    all_to_all x1, starting transfers between devices, over_planes(): lax.all_to_all(value, 'z', 0, 0, tiled=True, axis_index_groups=PLANES)  15.2 us
    all_gather x1, blocking collectives, on_device(): pair = lax.all_gather(message, 'c')  8.73 us
    ppermute x3, starting transfers between devices, on_device(): lax.ppermute(pair, 'y', [(i, (i + d) % NY) for i in range(NY)])  7.19 us
    pallas_call x5, Pallas kernels, call(): pl.pallas_call(kernel, out_shape=[jax.ShapeDtypeStruct(s, jnp.float32) fo...  5.87 us
  transfers between devices with their start and end apart: 4, of which 1 were waited for; matrix products, arithmetic and copies ran while one was open for 1% of the time, Pallas kernels for 0%

profile of v6, /device:TPU:1, one launch (start us, length us, event | category | flops | bytes accessed | tf_op | source)
XLA Modules:
  0.0 98.4 jit_solution(13313176286514701060)
XLA Ops:
  0.6 0.0 copy-start
  0.6 0.0 copy-start.1
  0.7 0.0 copy-start.2
  1.4 1.6 %shard_map.113 = (f32[264,128]{1,0:T(8,128)}, f32[16,1,32]{2,1,0:T(1,128)}) custom-call(s32[1,1,4]{2,1,0:T(1,128)} %eligible.1, s32[1,1]{1,0:T(1,128)S(6)} %copy.14.counts, bf16[256,128]{1,0:T(8,128)(2,1)} %embedding.1, f32[2,128]{1,0:T(2,128)} %bitcast.24, f32[2,128]{1,0:T(2,128)} %bitcast.25, f32[1,32]{1,0:T(1,128)} %bitcast.26), custom_call_target="tpu_custom_call" | custom-call | tf_op jit(solution)/shard_map/pallas_call | solution.py:243
  3.0 8.7 %all-gather = f32[528,128]{1,0:T(8,128)S(1)} all-gather(f32[264,128]{1,0:T(8,128)} %get-tuple-element.16), channel_id=2, replica_groups=mesh['z'=16,'y'=4,'c'=2,'x'=4] {'c'}, dimensions={0}, use_global_device_ids=true | all-gather | bytes 405504 | tf_op jit(solution)/shard_map/all_gather | solution.py:264
  11.7 1.9 %collective-permute-start.2 = (f32[2,264,128]{2,1,0:T(8,128)S(1)}, f32[2,264,128]{2,1,0:T(8,128)S(1)}, u32[]{:S(2)}, u32[]{:S(2)}) collective-permute-start(f32[2,264,128]{2,1,0:T(8,128)S(1)} %bitcast.17), channel_id=1, source_target_pairs={{0,24},{8,0},{16,8},{24,16},{1,25},{9,1},{17,9},{25,17},{2,26},{10... | collective-permute-start | bytes 811016 | tf_op jit(solution)/shard_map/ppermute | solution.py:266
  13.7 1.9 %collective-permute-start.1 = (f32[2,264,128]{2,1,0:T(8,128)S(1)}, f32[2,264,128]{2,1,0:T(8,128)S(1)}, u32[]{:S(2)}, u32[]{:S(2)}) collective-permute-start(f32[2,264,128]{2,1,0:T(8,128)S(1)} %bitcast.18), channel_id=1, source_target_pairs={{0,16},{8,24},{16,0},{24,8},{1,17},{9,25},{17,1},{25,9},{2,18},{10... | collective-permute-start | bytes 811016 | tf_op jit(solution)/shard_map/ppermute | solution.py:266
  15.6 3.4 %collective-permute-start = (f32[2,264,128]{2,1,0:T(8,128)S(1)}, f32[2,264,128]{2,1,0:T(8,128)S(1)}, u32[]{:S(2)}, u32[]{:S(2)}) collective-permute-start(f32[2,264,128]{2,1,0:T(8,128)S(1)} %bitcast.19), channel_id=1, source_target_pairs={{0,8},{8,16},{16,24},{24,0},{1,9},{9,17},{17,25},{25,1},{2,10},{10... | collective-permute-start | bytes 811016 | tf_op jit(solution)/shard_map/ppermute | solution.py:266
  19.0 15.2 %all-to-all-start = ((f32[16,1,32]{2,1,0:T(1,128)}), f32[16,1,32]{2,1,0:T(1,128)S(1)}, u32[]{:S(2)}, u32[]{:S(2)}) async-start(f32[16,1,32]{2,1,0:T(1,128)} %get-tuple-element.17), calls=%async_computation | async-start | bytes 16384 | tf_op jit(solution)/shard_map/all_to_all | solution.py:218
  34.2 0.7 multiply_bitcast_fusion.ad_weight
  34.9 0.0 copy-done
  34.9 0.8 all-to-all-done.pot_parts
  35.7 0.0 collective-permute-done.2.msg3
  35.7 0.0 collective-permute-done.1.msg2
  35.7 0.0 collective-permute-done.msg1
  35.8 1.9 %shard_map.114 = (f32[512,2048]{1,0:T(8,128)S(1)}, f32[32,1,2048]{2,1,0:T(1,128)S(1)}, f32[1,2048]{1,0:T(1,128)S(1)}, f32[1,512]{1,0:T(1,128)S(1)}) custom-call(s32[1]{0:T(128)} %bitcast.mine.own, s32[1]{0:T(128)} %bitcast.1.place.own, f32[2,264,128]{2,1,0:T(8,128)S(1)} %bitcast.20, f32[2,264,128]{2,1,0:T(8,128)S(1)} %collective-permute-done.msg1, ...), custom_call_target="tpu_custom_call" | custom-call | tf_op jit(solution)/shard_map/pallas_call | solution.py:196
  37.7 14.6 %all_to_all.25.parts = f32[32,1,2048]{2,1,0:T(1,128)S(1)} all-to-all(f32[32,1,2048]{2,1,0:T(1,128)S(1)} %get-tuple-element.19), channel_id=1, replica_groups={{18,19,16,17,22,23,20,21,26,27,24,25,30,31,28,29,2,3,0,1,6,7,4,5,10,11,..., dimensions={0} | all-to-all | bytes 524288 | tf_op jit(solution)/shard_map/all_to_all | solution.py:222
  52.3 0.9 shard_map.115
  53.2 14.7 %all_to_all.26.parts = f32[16,1,512]{2,1,0:T(1,128)S(1)} all-to-all(f32[16,1,512]{2,1,0:T(1,128)S(1)} %get-tuple-element.22), channel_id=1, replica_groups={{256,288,320,352,384,416,448,480,0,32,64,96,128,160,192,224},{257,289,3..., dimensions={0} | all-to-all | bytes 65536 | tf_op jit(solution)/shard_map/all_to_all | solution.py:218
  67.9 0.0 copy-done.1
  67.9 0.0 copy-done.2
  67.9 1.0 %shard_map.116 = (f32[1,512]{1,0:T(1,128)S(1)}, f32[32,1,2048]{2,1,0:T(1,128)S(1)}, f32[1,512]{1,0:T(1,128)S(1)}, f32[1,512]{1,0:T(1,128)S(1)}) custom-call(s32[1]{0:T(128)} %bitcast.mine.own, f32[512,2048]{1,0:T(8,128)S(1)} %get-tuple-element.18.tile, f32[16,1,512]{2,1,0:T(1,128)S(1)} %all_to_all.26.parts, f32[1,2048]{1,0:T(1,128)S(1)} %get-tuple-element.23.row_pot, ...), custom_call_target="tpu_custom_call" | custom-call | tf_op jit(solution)/shard_map/pallas_call | solution.py:196
  69.0 13.3 %all_to_all.27.parts = f32[32,1,2048]{2,1,0:T(1,128)S(1)} all-to-all(f32[32,1,2048]{2,1,0:T(1,128)S(1)} %get-tuple-element.24), channel_id=1, replica_groups={{18,19,16,17,22,23,20,21,26,27,24,25,30,31,28,29,2,3,0,1,6,7,4,5,10,11,..., dimensions={0} | all-to-all | bytes 524288 | tf_op jit(solution)/shard_map/all_to_all | solution.py:222
  82.2 1.3 %shard_map.117 = (f32[1,256]{1,0:T(1,128)}, f32[16,1,512]{2,1,0:T(1,128)S(1)}) custom-call(s32[1]{0:T(128)} %bitcast.mine.own, f32[512,2048]{1,0:T(8,128)S(1)} %get-tuple-element.18.tile, f32[32,1,2048]{2,1,0:T(1,128)S(1)} %all_to_all.27.parts, f32[1,2048]{1,0:T(1,128)S(1)} %get-tuple-element.23.row_pot, f32[1,2048]{1,0:T(1,128)S(1)} %get-tuple-element.20.mass, ...), custom_call_target="tpu_custom_call" | custom-call | tf_op jit(solution)/shard_map/pallas_call | solution.py:196
  83.6 14.2 %all_to_all.28.parts = f32[16,1,512]{2,1,0:T(1,128)S(1)} all-to-all(f32[16,1,512]{2,1,0:T(1,128)S(1)} %get-tuple-element.27), channel_id=1, replica_groups={{256,288,320,352,384,416,448,480,0,32,64,96,128,160,192,224},{257,289,3..., dimensions={0} | all-to-all | bytes 65536 | tf_op jit(solution)/shard_map/all_to_all | solution.py:218
  97.8 0.6 shard_map.118
  (1 shorter events, 0.0 us)
Async XLA Ops:
  0.6 34.3 %copy-start = (bf16[4096,128]{1,0:T(8,128)(2,1)S(1)}, bf16[4096,128]{1,0:T(8,128)(2,1)}, u32[]{:S(2)}) copy-start(bf16[4096,128]{1,0:T(8,128)(2,1)} %param.13) | copy-start | bytes 3145732
  0.6 67.3 %copy-start.1 = (f32[4096]{0:T(1024)S(1)}, f32[4096]{0:T(1024)}, u32[]{:S(2)}) copy-start(f32[4096]{0:T(1024)} %param.16) | copy-start | bytes 49156
  0.7 67.3 %copy-start.2 = (f32[4096]{0:T(1024)S(1)}, f32[4096]{0:T(1024)}, u32[]{:S(2)}) copy-start(f32[4096]{0:T(1024)} %param.15) | copy-start | bytes 49156
  11.7 24.0 %collective-permute-start.2 = (f32[2,264,128]{2,1,0:T(8,128)S(1)}, f32[2,264,128]{2,1,0:T(8,128)S(1)}, u32[]{:S(2)}, u32[]{:S(2)}) collective-permute-start(f32[2,264,128]{2,1,0:T(8,128)S(1)} %bitcast.17), channel_id=1, source_target_pairs={{0,24},{8,0},{16,8},{24,16},{1,25},{9,1},{17,9},{25,17},{2,26},{10... | collective-permute-start | bytes 811016 | tf_op jit(solution)/shard_map/ppermute | solution.py:266
  13.7 22.1 %collective-permute-start.1 = (f32[2,264,128]{2,1,0:T(8,128)S(1)}, f32[2,264,128]{2,1,0:T(8,128)S(1)}, u32[]{:S(2)}, u32[]{:S(2)}) collective-permute-start(f32[2,264,128]{2,1,0:T(8,128)S(1)} %bitcast.18), channel_id=1, source_target_pairs={{0,16},{8,24},{16,0},{24,8},{1,17},{9,25},{17,1},{25,9},{2,18},{10... | collective-permute-start | bytes 811016 | tf_op jit(solution)/shard_map/ppermute | solution.py:266
  15.6 20.2 %collective-permute-start = (f32[2,264,128]{2,1,0:T(8,128)S(1)}, f32[2,264,128]{2,1,0:T(8,128)S(1)}, u32[]{:S(2)}, u32[]{:S(2)}) collective-permute-start(f32[2,264,128]{2,1,0:T(8,128)S(1)} %bitcast.19), channel_id=1, source_target_pairs={{0,8},{8,16},{16,24},{24,0},{1,9},{9,17},{17,25},{25,1},{2,10},{10... | collective-permute-start | bytes 811016 | tf_op jit(solution)/shard_map/ppermute | solution.py:266
  19.0 16.8 %all-to-all-start = ((f32[16,1,32]{2,1,0:T(1,128)}), f32[16,1,32]{2,1,0:T(1,128)S(1)}, u32[]{:S(2)}, u32[]{:S(2)}) async-start(f32[16,1,32]{2,1,0:T(1,128)} %get-tuple-element.17), calls=%async_computation | async-start | bytes 16384 | tf_op jit(solution)/shard_map/all_to_all | solution.py:218

commit v7 on v6

v7 whole, which is shorter than its diff:
```python
import functools
import math

import jax
import jax.numpy as jnp
from jax import lax
from jax.experimental import pallas as pl
from jax.experimental.pallas import tpu as pltpu
from jax.sharding import Mesh
from jax.sharding import PartitionSpec as P

ADS_IN_PART = 1024
AB_J = 4
KMAX = 4
UBS = 256
NZ, NY, NC, NX = 16, 4, 2, 4
NS = NY * NC
NROW = NS * NX
ADS_J = 4096
SHARD = 32
USERS_HERE = NS * UBS
ADS_HERE = NZ * SHARD
PART_HERE = ADS_HERE // AB_J
ROWS = UBS + 8 + 32

regularizer_epsilon = 0.1
very_low = -1e30
TO_UNITS = 1.0 / regularizer_epsilon
WEIGHT = TO_UNITS / math.sqrt(128)
COL_SHIFT = 44.0
ROW_SHIFT = 69.0

VMEM_LIMIT = 40 * 1024 * 1024


def as_columns(row):
    return jnp.broadcast_to(row, (128, row.shape[1])).T


def my_block():
    return lax.axis_index("y") * NC + lax.axis_index("c")


def message_kernel(
    eligible, counts, embedding, scale, mass, pot, ad_scale, out, pot_out,
    eligible_here, counts_here, embedding_here, mass_here, pot_here, sems,
):
    pairs = [
        (pot, pot_here),
        (eligible, eligible_here),
        (counts, counts_here),
        (mass, mass_here),
        (scale, out.at[pl.ds(UBS, 2), :]),
        (embedding, embedding_here),
        (ad_scale, out.at[pl.ds(UBS + 8, 32), :]),
    ]
    copies = [pltpu.make_async_copy(src, dst, sems.at[i]) for i, (src, dst) in enumerate(pairs)]
    for copy in copies:
        copy.start()
    copies[0].wait()
    pot_out[...] = jnp.broadcast_to(pot_here[...][None], (NZ, 1, SHARD))
    copies[1].wait()
    copies[2].wait()
    for q in range(AB_J):
        bias = jnp.float32(very_low)
        for k in range(KMAX):
            hit = jnp.logical_and(k < counts_here[0, 0], eligible_here[0, 0, k] == q)
            bias = jnp.where(hit, jnp.float32(0.0), bias)
        out[UBS + 4 + q : UBS + 5 + q, :] = jnp.full((1, 128), bias, jnp.float32)
    copies[3].wait()
    out[UBS + 2 : UBS + 4, :] = jnp.log(mass_here[...])
    copies[4].wait()
    copies[5].wait()
    out[:UBS, :] = embedding_here[...].astype(jnp.float32)
    copies[6].wait()


def of_here(array, mine):
    rows = array[pl.ds(lax.shift_right_logical(mine, 2), NZ, stride=2), :]
    turn = lax.rem(128 - lax.rem(mine, 4) * SHARD, 128)
    rows = pltpu.roll(rows, turn, 1)
    return jnp.concatenate([rows[z : z + 1, :SHARD] for z in range(NZ)], axis=1)


def tile_kernel(
    msg0, msg1, msg2, msg3, ads, pot_parts, tile, row_lse, log_mass, pot, lse_here
):
    mine = my_block()
    weight = as_columns(of_here(msg0.at[lax.rem(mine, NC), pl.ds(UBS + 8, 32), :], mine) * WEIGHT)
    pots = jnp.concatenate(
        [pot_parts[PLANES[0].index(z)] for z in range(NZ)], axis=1
    ) * TO_UNITS
    pot[...] = pots
    pots = as_columns(pots)
    for back, msg in enumerate((msg0, msg1, msg2, msg3)):
        first = lax.rem(lax.shift_right_logical(mine, 1) + (NY - back), NY) * NC

        for c in range(NC):
            users = msg[c, :UBS, :].astype(jnp.bfloat16)
            scale = jnp.concatenate(
                [msg[c, UBS : UBS + 1, :], msg[c, UBS + 1 : UBS + 2, :]], axis=1
            )
            at = pl.ds(pl.multiple_of((first + c) * UBS, UBS), UBS)
            log_mass[pl.ds(first + c, 1), :] = jnp.concatenate(
                [msg[c, UBS + 2 : UBS + 3, :], msg[c, UBS + 3 : UBS + 4, :]], axis=1
            )
            peaks, totals = [], []
            for q in range(AB_J):
                rows = slice(q * PART_HERE, (q + 1) * PART_HERE)
                product = lax.dot_general(
                    ads[rows, :], users, (((1,), (1,)), ((), ())),
                    preferred_element_type=jnp.float32,
                )
                bias = msg[c, UBS + 4 + q : UBS + 5 + q, :]
                bias = jnp.concatenate([bias, bias], axis=1)
                wide = jnp.concatenate([weight[rows], weight[rows]], axis=1)
                values = product * wide * scale + bias
                tile[rows, at] = values
                values = values + jnp.concatenate([pots[rows], pots[rows]], axis=1)
                peak = jnp.max(values, axis=0, keepdims=True)
                peaks.append(peak)
                totals.append(jnp.sum(jnp.exp(values - peak), axis=0, keepdims=True))
            peak = functools.reduce(jnp.maximum, peaks)
            total = sum(t * jnp.exp(p - peak) for p, t in zip(peaks, totals))
            lse = peak + jnp.log(total)
            lse_here[pl.ds(first + c, 1), :] = lse
    row_lse[...] = jnp.broadcast_to(lse_here[...][None], (NROW, NS, UBS))


def row_of(blocks, t):
    half = t % 2 * 128
    return blocks[t // 2 : t // 2 + 1, half : half + 128]


def column_sums(tile, row_pot, pots):
    sums = []
    for q in range(AB_J):
        rows = slice(q * PART_HERE, (q + 1) * PART_HERE)
        total = jnp.zeros((PART_HERE, 128), jnp.float32)
        for t in range(USERS_HERE // 128):
            lanes = slice(t * 128, (t + 1) * 128)
            total = total + jnp.exp(tile[rows, lanes] + row_of(row_pot, t) + pots[rows])
        sums.append(jnp.sum(total.T, axis=0, keepdims=True))
    return jnp.concatenate(sums, axis=1)


def first_column_kernel(tile, parts, mass, pot, row_pot_out, col_out):
    peak = jnp.max(parts[...], axis=0)
    total = jnp.sum(jnp.exp(parts[...] - peak[None]), axis=0)
    row_pot = mass[...] - (peak + jnp.log(total))
    row_pot_out[...] = row_pot
    sums = column_sums(tile, row_pot + COL_SHIFT, as_columns(pot[...]))
    col_out[...] = jnp.broadcast_to(sums[None], (NZ, 1, ADS_HERE))


def column_update(log_sum, fallback, log_demand):
    peak = jnp.maximum(log_sum, fallback)
    return log_demand - (peak + jnp.log(jnp.exp(log_sum - peak) + jnp.exp(fallback - peak)))


def second_row_kernel(
    tile, parts, row_pot, pot, penalty, demand, pot_out, row_out, fallback, log_demand, sums_here
):
    mine = my_block()
    fallback[...] = of_here(penalty, mine) * -TO_UNITS
    log_demand[...] = jnp.log(of_here(demand, mine))
    sums = jnp.sum(parts[...], axis=0)
    new_pot = column_update(
        jnp.log(sums) - COL_SHIFT - pot[...], fallback[...], log_demand[...]
    )
    pot_out[...] = new_pot
    pots = as_columns(new_pot)
    for t in range(USERS_HERE // 128):
        lanes = slice(t * 128, (t + 1) * 128)
        shift = row_of(row_pot, t) + ROW_SHIFT
        total = jnp.zeros((8, 128), jnp.float32)
        for q in range(AB_J):
            rows = slice(q * PART_HERE, (q + 1) * PART_HERE)
            terms = jnp.exp(tile[rows, lanes] + shift + pots[rows])
            total = total + jnp.sum(terms.reshape(PART_HERE // 8, 8, 128), axis=0)
        half = t % 2 * 128
        sums_here[t // 2 : t // 2 + 1, half : half + 128] = jnp.sum(total, axis=0, keepdims=True)
    row_out[...] = jnp.broadcast_to(sums_here[...][None], (NROW, NS, UBS))


def second_column_kernel(tile, parts, row_pot, mass, pot, new_out, col_out):
    sums = jnp.sum(parts[...], axis=0)
    new = row_pot[...] + (mass[...] + ROW_SHIFT - jnp.log(sums))
    new_out[...] = new
    sums = column_sums(tile, new, as_columns(pot[...]))
    col_out[...] = jnp.broadcast_to(sums[None], (NZ, 1, ADS_HERE))


def last_kernel(parts, pot, fallback, log_demand, row_pot, out, user_out):
    user_out[...] = row_pot[pl.ds(my_block(), 1), :] * regularizer_epsilon
    sums = jnp.sum(parts[...], axis=0)
    new = column_update(
        jnp.log(sums) - pot[...], fallback[...], log_demand[...]
    ) * regularizer_epsilon
    new = jnp.broadcast_to(new, (8, ADS_HERE))
    turned = pltpu.roll(new, lax.rem(ADS_HERE - lax.axis_index("z") * SHARD, ADS_HERE), 1)
    out[...] = turned[:1, :SHARD]


def call(kernel, out_shape, *operands, scratch=()):
    vmem = pl.BlockSpec(memory_space=pltpu.VMEM)
    return pl.pallas_call(
        kernel,
        out_shape=[jax.ShapeDtypeStruct(s, jnp.float32) for s in out_shape],
        in_specs=[vmem] * len(operands),
        out_specs=[vmem] * len(out_shape),
        scratch_shapes=[pltpu.VMEM(shape, jnp.float32) for shape in scratch],
        compiler_params=pltpu.CompilerParams(vmem_limit_bytes=VMEM_LIMIT),
    )(*operands)


FIRST_Z = NZ // 2
PLANES = [[8, 15, 6, 13, 4, 11, 2, 9, 0, 7, 14, 5, 12, 3, 10, 1]]
ROW_GROUP = [
    [
        ((NY // 2 + i) % NY * NC + c) * NX + (NX // 2 + j) % NX
        for i in range(NY)
        for c in (1, 0)
        for j in range(NX)
    ]
]


def over_planes(value):
    return lax.all_to_all(value, "z", 0, 0, tiled=True, axis_index_groups=PLANES)


def over_rows(value):
    return lax.all_to_all(
        value, ("y", "c", "x"), 0, 0, tiled=True, axis_index_groups=ROW_GROUP
    )


def on_device(
    user_embedding,
    user_scale,
    user_mass,
    ad_embedding,
    ad_scale,
    listing_view_demand,
    listing_unplaced_penalty,
    campaign_dual_vector_initial,
    eligible,
    counts,
):

    message, pot_parts = pl.pallas_call(
        message_kernel,
        out_shape=[
            jax.ShapeDtypeStruct((ROWS, 128), jnp.float32),
            jax.ShapeDtypeStruct((NZ, 1, SHARD), jnp.float32),
        ],
        in_specs=[pl.BlockSpec(memory_space=pltpu.HBM)] * 7,
        out_specs=[pl.BlockSpec(memory_space=pltpu.VMEM)] * 2,
        scratch_shapes=[
            pltpu.SMEM((1, 1, KMAX), jnp.int32),
            pltpu.SMEM((1, 1), jnp.int32),
            pltpu.VMEM((UBS, 128), jnp.bfloat16),
            pltpu.VMEM((2, 128), jnp.float32),
            pltpu.VMEM((1, SHARD), jnp.float32),
            pltpu.SemaphoreType.DMA((7,)),
        ],
    )(
        eligible, counts, user_embedding, user_scale.reshape(2, 128), user_mass.reshape(2, 128),
        campaign_dual_vector_initial.reshape(1, SHARD), ad_scale.reshape(ADS_J // 128, 128),
    )
    ads = lax.dynamic_index_in_dim(
        ad_embedding.reshape(NZ, NS, SHARD, -1), my_block(), 1, keepdims=False
    ).reshape(ADS_HERE, -1)
    ads, pot_parts = lax.optimization_barrier((ads, pot_parts))
    pot_parts = over_planes(pot_parts)
    pair = lax.all_gather(message, "c")
    behind = {
        d: lax.ppermute(pair, "y", [(i, (i + d) % NY) for i in range(NY)]) for d in (1, 2, 3)
    }
    messages = [pair, behind[1], behind[2], behind[3]]
    demand = listing_view_demand.reshape(ADS_J // 128, 128)
    penalty = listing_unplaced_penalty.reshape(ADS_J // 128, 128)

    tile, row_parts, mass, pot = call(
        tile_kernel,
        [(ADS_HERE, USERS_HERE), (NROW, NS, UBS), (NS, UBS), (1, ADS_HERE)],
        *messages, ads, pot_parts,
        scratch=[(NS, UBS)],
    )
    row_pot, col_parts = call(
        first_column_kernel,
        [(NS, UBS), (NZ, 1, ADS_HERE)],
        tile, over_rows(row_parts), mass, pot,
    )
    pot, row_parts, fallback, log_demand = call(
        second_row_kernel,
        [(1, ADS_HERE), (NROW, NS, UBS), (1, ADS_HERE), (1, ADS_HERE)],
        tile, over_planes(col_parts), row_pot, pot, penalty, demand,
        scratch=[(NS, UBS)],
    )
    new_row_pot, col_parts = call(
        second_column_kernel,
        [(NS, UBS), (NZ, 1, ADS_HERE)],
        tile, over_rows(row_parts), row_pot, mass, pot,
    )
    last, users = call(
        last_kernel,
        [(1, SHARD), (1, UBS)],
        over_planes(col_parts), pot, fallback, log_demand, new_row_pot,
    )
    return users.reshape(UBS), last.reshape(SHARD)


def solution(mesh):
    fine = Mesh(mesh.devices.reshape(NZ, NY, NC, NX), ("z", "y", "c", "x"))
    user = ("z", "y", "c")
    in_specs = (
        P(user, None),
        P(user),
        P(user),
        P("x", None),
        P("x"),
        P("x"),
        P("x"),
        P(("x",) + user),
        P(user, "x", None),
        P(user, "x"),
    )
    out_specs = (P(user), P(("x",) + user))
    return jax.shard_map(
        on_device, mesh=fine, in_specs=in_specs, out_specs=out_specs, check_vma=False
    )
```

time: 98.9 us -> 97.7 us (0.988)
  blocking collectives: 65.5 us -> 81.5 us
  starting transfers between devices: 22.4 us -> 7.19 us
    all_to_all x2 -> x3, blocking collectives: 28.9 us -> 45.6 us  [over_planes(): lax.all_to_all(value, 'z', 0, 0, tiled=True, axis_index_groups=PLANES)]
    all_to_all x1 -> x0, starting transfers between devices: 15.2 us -> none  [over_planes(): lax.all_to_all(value, 'z', 0, 0, tiled=True, axis_index_groups=PLANES)]
  transfers between devices with their start and end apart: 4 -> 3, of which waited for: 1 -> 0; matrix products, arithmetic and copies ran while one was open for 1% -> 0% of each run, Pallas kernels for 0% -> 0%
where the time goes in v7:
time: 97.7 us; the launch traced here: 97.3 us
  blocking collectives  81.5 us (83%)
  starting transfers between devices  7.19 us (7%)
  Pallas kernels  7.06 us (7%)
  between operations  1.47 us (2%)
    all_to_all x3, blocking collectives, over_planes(): lax.all_to_all(value, 'z', 0, 0, tiled=True, axis_index_groups=PLANES)  45.6 us
    all_to_all x2, blocking collectives, over_rows(): lax.all_to_all(value, ('y', 'c', 'x'), 0, 0, tiled=True, axis_index_group...  27.1 us
    all_gather x1, blocking collectives, on_device(): pair = lax.all_gather(message, 'c')  8.75 us
    ppermute x3, starting transfers between devices, on_device(): lax.ppermute(pair, 'y', [(i, (i + d) % NY) for i in range(NY)])  7.19 us
    pallas_call x5, Pallas kernels, call(): pl.pallas_call(kernel, out_shape=[jax.ShapeDtypeStruct(s, jnp.float32) fo...  5.43 us
  transfers between devices with their start and end apart: 3, of which 0 were waited for; matrix products, arithmetic and copies ran while one was open for 0% of the time, Pallas kernels for 0%

profile of v7, /device:TPU:1, one launch (start us, length us, event | category | flops | bytes accessed | tf_op | source)
XLA Modules:
  0.0 97.3 jit_solution(17881870987379920151)
XLA Ops:
  0.6 0.0 copy-start
  0.6 0.0 copy-start.1
  0.7 0.0 copy-start.2
  1.4 1.6 %shard_map.113 = (f32[296,128]{1,0:T(8,128)}, f32[16,1,32]{2,1,0:T(1,128)}) custom-call(s32[1,1,4]{2,1,0:T(1,128)} %eligible.1, s32[1,1]{1,0:T(1,128)S(6)} %copy.14.counts, bf16[256,128]{1,0:T(8,128)(2,1)} %embedding.1, f32[2,128]{1,0:T(2,128)} %bitcast.22, f32[2,128]{1,0:T(2,128)} %bitcast.23, f32[1,32]{1,0:T(1,128)} %bitcast.24, f32[32,128]{1,0:T(8,128)} %bitcast.21), custom_call_target="tpu_custom_call" | custom-call | tf_op jit(solution)/shard_map/pallas_call | solution.py:252
  3.0 8.7 %all-gather = f32[592,128]{1,0:T(8,128)S(1)} all-gather(f32[296,128]{1,0:T(8,128)} %get-tuple-element.20), channel_id=2, replica_groups=mesh['z'=16,'y'=4,'c'=2,'x'=4] {'c'}, dimensions={0}, use_global_device_ids=true | all-gather | bytes 454656 | tf_op jit(solution)/shard_map/all_gather | solution.py:277
  11.8 1.9 %collective-permute-start.2 = (f32[2,296,128]{2,1,0:T(8,128)S(1)}, f32[2,296,128]{2,1,0:T(8,128)S(1)}, u32[]{:S(2)}, u32[]{:S(2)}) collective-permute-start(f32[2,296,128]{2,1,0:T(8,128)S(1)} %bitcast.14), channel_id=1, source_target_pairs={{0,24},{8,0},{16,8},{24,16},{1,25},{9,1},{17,9},{25,17},{2,26},{10... | collective-permute-start | bytes 909320 | tf_op jit(solution)/shard_map/ppermute | solution.py:279
  13.7 1.9 %collective-permute-start.1 = (f32[2,296,128]{2,1,0:T(8,128)S(1)}, f32[2,296,128]{2,1,0:T(8,128)S(1)}, u32[]{:S(2)}, u32[]{:S(2)}) collective-permute-start(f32[2,296,128]{2,1,0:T(8,128)S(1)} %bitcast.15), channel_id=1, source_target_pairs={{0,16},{8,24},{16,0},{24,8},{1,17},{9,25},{17,1},{25,9},{2,18},{10... | collective-permute-start | bytes 909320 | tf_op jit(solution)/shard_map/ppermute | solution.py:279
  15.6 3.4 %collective-permute-start = (f32[2,296,128]{2,1,0:T(8,128)S(1)}, f32[2,296,128]{2,1,0:T(8,128)S(1)}, u32[]{:S(2)}, u32[]{:S(2)}) collective-permute-start(f32[2,296,128]{2,1,0:T(8,128)S(1)} %bitcast.16), channel_id=1, source_target_pairs={{0,8},{8,16},{16,24},{24,0},{1,9},{9,17},{17,25},{25,1},{2,10},{10... | collective-permute-start | bytes 909320 | tf_op jit(solution)/shard_map/ppermute | solution.py:279
  19.0 0.0 copy-done
  19.0 16.8 %all_to_all.25.pot_parts = f32[16,1,32]{2,1,0:T(1,128)S(1)} all-to-all(f32[16,1,32]{2,1,0:T(1,128)} %get-tuple-element.23), channel_id=1, replica_groups={{256,480,192,416,128,352,64,288,0,224,448,160,384,96,320,32},{257,481,1..., dimensions={0} | all-to-all | bytes 4096 | tf_op jit(solution)/shard_map/all_to_all | solution.py:230
  35.8 0.0 collective-permute-done.2.msg3
  35.8 0.0 collective-permute-done.1.msg2
  35.8 0.0 collective-permute-done.msg1
  35.8 2.0 %shard_map.114 = (f32[512,2048]{1,0:T(8,128)S(1)}, f32[32,8,256]{2,1,0:T(8,128)S(1)}, f32[8,256]{1,0:T(8,128)S(1)}, f32[1,512]{1,0:T(1,128)S(1)}) custom-call(f32[2,296,128]{2,1,0:T(8,128)S(1)} %bitcast.17, f32[2,296,128]{2,1,0:T(8,128)S(1)} %collective-permute-done.msg1, f32[2,296,128]{2,1,0:T(8,128)S(1)} %collective-permute-done.1.msg2, ...), custom_call_target="tpu_custom_call" | custom-call | tf_op jit(solution)/shard_map/pallas_call | solution.py:207
  37.8 14.3 %all_to_all.26.parts = f32[32,8,256]{2,1,0:T(8,128)S(1)} all-to-all(f32[32,8,256]{2,1,0:T(8,128)S(1)} %get-tuple-element.25), channel_id=1, replica_groups={{22,23,20,21,18,19,16,17,30,31,28,29,26,27,24,25,6,7,4,5,2,3,0,1,14,15,..., dimensions={0} | all-to-all | bytes 524288 | tf_op jit(solution)/shard_map/all_to_all | solution.py:234
  52.1 0.8 shard_map.115
  53.0 14.6 %all_to_all.27.parts = f32[16,1,512]{2,1,0:T(1,128)S(1)} all-to-all(f32[16,1,512]{2,1,0:T(1,128)S(1)} %get-tuple-element.28), channel_id=1, replica_groups={{256,480,192,416,128,352,64,288,0,224,448,160,384,96,320,32},{257,481,1..., dimensions={0} | all-to-all | bytes 65536 | tf_op jit(solution)/shard_map/all_to_all | solution.py:230
  67.5 0.0 copy-done.1
  67.5 0.0 copy-done.2
  67.6 1.1 %shard_map.116 = (f32[1,512]{1,0:T(1,128)S(1)}, f32[32,8,256]{2,1,0:T(8,128)S(1)}, f32[1,512]{1,0:T(1,128)S(1)}, f32[1,512]{1,0:T(1,128)S(1)}) custom-call(f32[512,2048]{1,0:T(8,128)S(1)} %get-tuple-element.24.tile, f32[16,1,512]{2,1,0:T(1,128)S(1)} %all_to_all.27.parts, f32[8,256]{1,0:T(8,128)S(1)} %get-tuple-element.29.row_pot, ...), custom_call_target="tpu_custom_call" | custom-call | tf_op jit(solution)/shard_map/pallas_call | solution.py:207
  68.7 12.9 %all_to_all.28.parts = f32[32,8,256]{2,1,0:T(8,128)S(1)} all-to-all(f32[32,8,256]{2,1,0:T(8,128)S(1)} %get-tuple-element.30), channel_id=1, replica_groups={{22,23,20,21,18,19,16,17,30,31,28,29,26,27,24,25,6,7,4,5,2,3,0,1,14,15,..., dimensions={0} | all-to-all | bytes 524288 | tf_op jit(solution)/shard_map/all_to_all | solution.py:234
  81.6 0.8 shard_map.117
  82.4 14.2 %all_to_all.29.parts = f32[16,1,512]{2,1,0:T(1,128)S(1)} all-to-all(f32[16,1,512]{2,1,0:T(1,128)S(1)} %get-tuple-element.32), channel_id=1, replica_groups={{256,480,192,416,128,352,64,288,0,224,448,160,384,96,320,32},{257,481,1..., dimensions={0} | all-to-all | bytes 65536 | tf_op jit(solution)/shard_map/all_to_all | solution.py:230
  96.6 0.6 shard_map.118
  (1 shorter events, 0.0 us)
Async XLA Ops:
  0.6 18.4 %copy-start = (bf16[4096,128]{1,0:T(8,128)(2,1)S(1)}, bf16[4096,128]{1,0:T(8,128)(2,1)}, u32[]{:S(2)}) copy-start(bf16[4096,128]{1,0:T(8,128)(2,1)} %param.13) | copy-start | bytes 3145732
  0.6 66.9 %copy-start.1 = (f32[4096]{0:T(1024)S(1)}, f32[4096]{0:T(1024)}, u32[]{:S(2)}) copy-start(f32[4096]{0:T(1024)} %param.16) | copy-start | bytes 49156
  0.7 66.9 %copy-start.2 = (f32[4096]{0:T(1024)S(1)}, f32[4096]{0:T(1024)}, u32[]{:S(2)}) copy-start(f32[4096]{0:T(1024)} %param.15) | copy-start | bytes 49156
  11.8 24.0 %collective-permute-start.2 = (f32[2,296,128]{2,1,0:T(8,128)S(1)}, f32[2,296,128]{2,1,0:T(8,128)S(1)}, u32[]{:S(2)}, u32[]{:S(2)}) collective-permute-start(f32[2,296,128]{2,1,0:T(8,128)S(1)} %bitcast.14), channel_id=1, source_target_pairs={{0,24},{8,0},{16,8},{24,16},{1,25},{9,1},{17,9},{25,17},{2,26},{10... | collective-permute-start | bytes 909320 | tf_op jit(solution)/shard_map/ppermute | solution.py:279
  13.7 22.1 %collective-permute-start.1 = (f32[2,296,128]{2,1,0:T(8,128)S(1)}, f32[2,296,128]{2,1,0:T(8,128)S(1)}, u32[]{:S(2)}, u32[]{:S(2)}) collective-permute-start(f32[2,296,128]{2,1,0:T(8,128)S(1)} %bitcast.15), channel_id=1, source_target_pairs={{0,16},{8,24},{16,0},{24,8},{1,17},{9,25},{17,1},{25,9},{2,18},{10... | collective-permute-start | bytes 909320 | tf_op jit(solution)/shard_map/ppermute | solution.py:279
  15.6 20.2 %collective-permute-start = (f32[2,296,128]{2,1,0:T(8,128)S(1)}, f32[2,296,128]{2,1,0:T(8,128)S(1)}, u32[]{:S(2)}, u32[]{:S(2)}) collective-permute-start(f32[2,296,128]{2,1,0:T(8,128)S(1)} %bitcast.16), channel_id=1, source_target_pairs={{0,8},{8,16},{16,24},{24,0},{1,9},{9,17},{17,25},{25,1},{2,10},{10... | collective-permute-start | bytes 909320 | tf_op jit(solution)/shard_map/ppermute | solution.py:279

commit v8 on v7

--- a/solution.py
+++ b/solution.py
@@ -21,7 +21,7 @@
 USERS_HERE = NS * UBS
 ADS_HERE = NZ * SHARD
 PART_HERE = ADS_HERE // AB_J
-ROWS = UBS + 8 + 32
+ROWS = UBS + 8
 
 regularizer_epsilon = 0.1
 very_low = -1e30
@@ -42,7 +42,7 @@
 
 
 def message_kernel(
-    eligible, counts, embedding, scale, mass, pot, ad_scale, out, pot_out,
+    eligible, counts, embedding, scale, mass, pot, out, pot_out,
     eligible_here, counts_here, embedding_here, mass_here, pot_here, sems,
 ):
     pairs = [
@@ -52,7 +52,6 @@
         (mass, mass_here),
         (scale, out.at[pl.ds(UBS, 2), :]),
         (embedding, embedding_here),
-        (ad_scale, out.at[pl.ds(UBS + 8, 32), :]),
     ]
     copies = [pltpu.make_async_copy(src, dst, sems.at[i]) for i, (src, dst) in enumerate(pairs)]
     for copy in copies:
@@ -72,7 +71,6 @@
     copies[4].wait()
     copies[5].wait()
     out[:UBS, :] = embedding_here[...].astype(jnp.float32)
-    copies[6].wait()
 
 
 def of_here(array, mine):
@@ -83,17 +81,17 @@
 
 
 def tile_kernel(
-    msg0, msg1, msg2, msg3, ads, pot_parts, tile, row_lse, log_mass, pot, lse_here
+    msg0, msg1, msg3, msg2, ads, ad_weight, pot_parts, tile, row_lse, log_mass, pot, lse_here
 ):
     mine = my_block()
-    weight = as_columns(of_here(msg0.at[lax.rem(mine, NC), pl.ds(UBS + 8, 32), :], mine) * WEIGHT)
+    weight = as_columns(of_here(ad_weight, mine))
     pots = jnp.concatenate(
         [pot_parts[PLANES[0].index(z)] for z in range(NZ)], axis=1
     ) * TO_UNITS
     pot[...] = pots
     pots = as_columns(pots)
-    for back, msg in enumerate((msg0, msg1, msg2, msg3)):
-        first = lax.rem(lax.shift_right_logical(mine, 1) + (NY - back), NY) * NC
+    for back, msg in ((0, msg0), (1, msg1), (3, msg3), (2, msg2)):
+        first = lax.bitwise_xor(lax.shift_right_logical(mine, 1), back) * NC
 
         for c in range(NC):
             users = msg[c, :UBS, :].astype(jnp.bfloat16)
@@ -255,7 +253,7 @@
             jax.ShapeDtypeStruct((ROWS, 128), jnp.float32),
             jax.ShapeDtypeStruct((NZ, 1, SHARD), jnp.float32),
         ],
-        in_specs=[pl.BlockSpec(memory_space=pltpu.HBM)] * 7,
+        in_specs=[pl.BlockSpec(memory_space=pltpu.HBM)] * 6,
         out_specs=[pl.BlockSpec(memory_space=pltpu.VMEM)] * 2,
         scratch_shapes=[
             pltpu.SMEM((1, 1, KMAX), jnp.int32),
@@ -263,29 +261,28 @@
             pltpu.VMEM((UBS, 128), jnp.bfloat16),
             pltpu.VMEM((2, 128), jnp.float32),
             pltpu.VMEM((1, SHARD), jnp.float32),
-            pltpu.SemaphoreType.DMA((7,)),
+            pltpu.SemaphoreType.DMA((6,)),
         ],
     )(
         eligible, counts, user_embedding, user_scale.reshape(2, 128), user_mass.reshape(2, 128),
-        campaign_dual_vector_initial.reshape(1, SHARD), ad_scale.reshape(ADS_J // 128, 128),
+        campaign_dual_vector_initial.reshape(1, SHARD),
     )
     ads = lax.dynamic_index_in_dim(
         ad_embedding.reshape(NZ, NS, SHARD, -1), my_block(), 1, keepdims=False
     ).reshape(ADS_HERE, -1)
-    ads, pot_parts = lax.optimization_barrier((ads, pot_parts))
     pot_parts = over_planes(pot_parts)
     pair = lax.all_gather(message, "c")
     behind = {
-        d: lax.ppermute(pair, "y", [(i, (i + d) % NY) for i in range(NY)]) for d in (1, 2, 3)
+        d: lax.ppermute(pair, "y", [(i, i ^ d) for i in range(NY)]) for d in (1, 2, 3)
     }
-    messages = [pair, behind[1], behind[2], behind[3]]
+    messages = [pair, behind[1], behind[3], behind[2]]
     demand = listing_view_demand.reshape(ADS_J // 128, 128)
     penalty = listing_unplaced_penalty.reshape(ADS_J // 128, 128)
 
     tile, row_parts, mass, pot = call(
         tile_kernel,
         [(ADS_HERE, USERS_HERE), (NROW, NS, UBS), (NS, UBS), (1, ADS_HERE)],
-        *messages, ads, pot_parts,
+        *messages, ads, ad_scale.reshape(ADS_J // 128, 128) * WEIGHT, pot_parts,
         scratch=[(NS, UBS)],
     )
     row_pot, col_parts = call(

time: 97.7 us -> 97.4 us (level)
  blocking collectives: 81.5 us -> 64.5 us
  starting transfers between devices: 7.19 us -> 22.3 us
    all_to_all x3 -> x2, blocking collectives: 45.6 us -> 28.7 us  [over_planes(): lax.all_to_all(value, 'z', 0, 0, tiled=True, axis_index_groups=PLANES)]
    all_to_all x0 -> x1, starting transfers between devices: none -> 14 us  [over_planes(): lax.all_to_all(value, 'z', 0, 0, tiled=True, axis_index_groups=PLANES)]
    ppermute x3, starting transfers between devices: 7.19 us -> 8.36 us  [on_device(): lax.ppermute(pair, 'y', [(i, i ^ d) for i in range(NY)])]
  transfers between devices with their start and end apart: 3 -> 4, of which waited for: 0 -> 1; matrix products, arithmetic and copies ran while one was open for 0% -> 1% of each run, Pallas kernels for 0% -> 0%
where the time goes in v8:
time: 97.4 us; the launch traced here: 96.9 us
  blocking collectives  64.5 us (66%)
  starting transfers between devices  22.3 us (23%)
  Pallas kernels  7.04 us (7%)
  between operations  1.45 us (1%)
    all_to_all x2, blocking collectives, over_planes(): lax.all_to_all(value, 'z', 0, 0, tiled=True, axis_index_groups=PLANES)  28.7 us
    all_to_all x2, blocking collectives, over_rows(): lax.all_to_all(value, ('y', 'c', 'x'), 0, 0, tiled=True, axis_index_group...  27.1 us
    all_to_all x1, starting transfers between devices, over_planes(): lax.all_to_all(value, 'z', 0, 0, tiled=True, axis_index_groups=PLANES)  14 us
    all_gather x1, blocking collectives, on_device(): pair = lax.all_gather(message, 'c')  8.73 us
    ppermute x3, starting transfers between devices, on_device(): lax.ppermute(pair, 'y', [(i, i ^ d) for i in range(NY)])  8.36 us
    pallas_call x5, Pallas kernels, call(): pl.pallas_call(kernel, out_shape=[jax.ShapeDtypeStruct(s, jnp.float32) fo...  5.44 us
  transfers between devices with their start and end apart: 4, of which 1 were waited for; matrix products, arithmetic and copies ran while one was open for 1% of the time, Pallas kernels for 0%

profile of v8, /device:TPU:1, one launch (start us, length us, event | category | flops | bytes accessed | tf_op | source)
XLA Modules:
  0.0 96.9 jit_solution(2863464369138628422)
XLA Ops:
  0.6 0.0 copy-start
  0.6 0.0 copy-start.1
  0.7 0.0 copy-start.2
  1.4 1.6 %shard_map.113 = (f32[264,128]{1,0:T(8,128)}, f32[16,1,32]{2,1,0:T(1,128)}) custom-call(s32[1,1,4]{2,1,0:T(1,128)} %eligible.1, s32[1,1]{1,0:T(1,128)S(6)} %copy.14.counts, bf16[256,128]{1,0:T(8,128)(2,1)} %embedding.1, f32[2,128]{1,0:T(2,128)} %bitcast.22, f32[2,128]{1,0:T(2,128)} %bitcast.23, f32[1,32]{1,0:T(1,128)} %bitcast.24), custom_call_target="tpu_custom_call" | custom-call | tf_op jit(solution)/shard_map/pallas_call | solution.py:250
  3.0 8.7 %all-gather = f32[528,128]{1,0:T(8,128)S(1)} all-gather(f32[264,128]{1,0:T(8,128)} %get-tuple-element.18), channel_id=2, replica_groups=mesh['z'=16,'y'=4,'c'=2,'x'=4] {'c'}, dimensions={0}, use_global_device_ids=true | all-gather | bytes 405504 | tf_op jit(solution)/shard_map/all_gather | solution.py:274
  11.7 1.9 %collective-permute-start.2 = (f32[2,264,128]{2,1,0:T(8,128)S(1)}, f32[2,264,128]{2,1,0:T(8,128)S(1)}, u32[]{:S(2)}, u32[]{:S(2)}) collective-permute-start(f32[2,264,128]{2,1,0:T(8,128)S(1)} %bitcast.15), channel_id=1, source_target_pairs={{0,16},{8,24},{16,0},{24,8},{1,17},{9,25},{17,1},{25,9},{2,18},{10... | collective-permute-start | bytes 811016 | tf_op jit(solution)/shard_map/ppermute | solution.py:276
  13.7 1.9 %collective-permute-start.1 = (f32[2,264,128]{2,1,0:T(8,128)S(1)}, f32[2,264,128]{2,1,0:T(8,128)S(1)}, u32[]{:S(2)}, u32[]{:S(2)}) collective-permute-start(f32[2,264,128]{2,1,0:T(8,128)S(1)} %bitcast.16), channel_id=1, source_target_pairs={{0,24},{8,16},{16,8},{24,0},{1,25},{9,17},{17,9},{25,1},{2,26},{10... | collective-permute-start | bytes 811016 | tf_op jit(solution)/shard_map/ppermute | solution.py:276
  15.6 4.5 %collective-permute-start = (f32[2,264,128]{2,1,0:T(8,128)S(1)}, f32[2,264,128]{2,1,0:T(8,128)S(1)}, u32[]{:S(2)}, u32[]{:S(2)}) collective-permute-start(f32[2,264,128]{2,1,0:T(8,128)S(1)} %bitcast.17), channel_id=1, source_target_pairs={{0,8},{8,0},{16,24},{24,16},{1,9},{9,1},{17,25},{25,17},{2,10},{10... | collective-permute-start | bytes 811016 | tf_op jit(solution)/shard_map/ppermute | solution.py:276
  20.1 14.0 %all-to-all-start = ((f32[16,1,32]{2,1,0:T(1,128)}), f32[16,1,32]{2,1,0:T(1,128)S(1)}, u32[]{:S(2)}, u32[]{:S(2)}) async-start(f32[16,1,32]{2,1,0:T(1,128)} %get-tuple-element.19), calls=%async_computation | async-start | bytes 16384 | tf_op jit(solution)/shard_map/all_to_all | solution.py:228
  34.1 0.7 multiply_bitcast_fusion.ad_weight
  34.8 0.0 copy-done
  34.8 0.8 all-to-all-done.pot_parts
  35.7 0.0 collective-permute-done.2.msg2
  35.7 0.0 collective-permute-done.1.msg3
  35.7 0.0 collective-permute-done.msg1
  35.7 2.0 %shard_map.114 = (f32[512,2048]{1,0:T(8,128)S(1)}, f32[32,8,256]{2,1,0:T(8,128)S(1)}, f32[8,256]{1,0:T(8,128)S(1)}, f32[1,512]{1,0:T(1,128)S(1)}) custom-call(f32[2,264,128]{2,1,0:T(8,128)S(1)} %bitcast.18, f32[2,264,128]{2,1,0:T(8,128)S(1)} %collective-permute-done.msg1, f32[2,264,128]{2,1,0:T(8,128)S(1)} %collective-permute-done.1.msg3, ...), custom_call_target="tpu_custom_call" | custom-call | tf_op jit(solution)/shard_map/pallas_call | solution.py:205
  37.7 14.3 %all_to_all.25.parts = f32[32,8,256]{2,1,0:T(8,128)S(1)} all-to-all(f32[32,8,256]{2,1,0:T(8,128)S(1)} %get-tuple-element.21), channel_id=1, replica_groups={{22,23,20,21,18,19,16,17,30,31,28,29,26,27,24,25,6,7,4,5,2,3,0,1,14,15,..., dimensions={0} | all-to-all | bytes 524288 | tf_op jit(solution)/shard_map/all_to_all | solution.py:232
  52.0 0.8 shard_map.115
  52.9 14.4 %all_to_all.26.parts = f32[16,1,512]{2,1,0:T(1,128)S(1)} all-to-all(f32[16,1,512]{2,1,0:T(1,128)S(1)} %get-tuple-element.24), channel_id=1, replica_groups={{256,480,192,416,128,352,64,288,0,224,448,160,384,96,320,32},{257,481,1..., dimensions={0} | all-to-all | bytes 65536 | tf_op jit(solution)/shard_map/all_to_all | solution.py:228
  67.3 0.0 copy-done.1
  67.3 0.0 copy-done.2
  67.3 1.1 %shard_map.116 = (f32[1,512]{1,0:T(1,128)S(1)}, f32[32,8,256]{2,1,0:T(8,128)S(1)}, f32[1,512]{1,0:T(1,128)S(1)}, f32[1,512]{1,0:T(1,128)S(1)}) custom-call(f32[512,2048]{1,0:T(8,128)S(1)} %get-tuple-element.20.tile, f32[16,1,512]{2,1,0:T(1,128)S(1)} %all_to_all.26.parts, f32[8,256]{1,0:T(8,128)S(1)} %get-tuple-element.25.row_pot, ...), custom_call_target="tpu_custom_call" | custom-call | tf_op jit(solution)/shard_map/pallas_call | solution.py:205
  68.4 12.8 %all_to_all.27.parts = f32[32,8,256]{2,1,0:T(8,128)S(1)} all-to-all(f32[32,8,256]{2,1,0:T(8,128)S(1)} %get-tuple-element.26), channel_id=1, replica_groups={{22,23,20,21,18,19,16,17,30,31,28,29,26,27,24,25,6,7,4,5,2,3,0,1,14,15,..., dimensions={0} | all-to-all | bytes 524288 | tf_op jit(solution)/shard_map/all_to_all | solution.py:232
  81.2 0.8 shard_map.117
  82.0 14.2 %all_to_all.28.parts = f32[16,1,512]{2,1,0:T(1,128)S(1)} all-to-all(f32[16,1,512]{2,1,0:T(1,128)S(1)} %get-tuple-element.28), channel_id=1, replica_groups={{256,480,192,416,128,352,64,288,0,224,448,160,384,96,320,32},{257,481,1..., dimensions={0} | all-to-all | bytes 65536 | tf_op jit(solution)/shard_map/all_to_all | solution.py:228
  96.3 0.6 shard_map.118
  (1 shorter events, 0.0 us)
Async XLA Ops:
  0.6 34.2 %copy-start = (bf16[4096,128]{1,0:T(8,128)(2,1)S(1)}, bf16[4096,128]{1,0:T(8,128)(2,1)}, u32[]{:S(2)}) copy-start(bf16[4096,128]{1,0:T(8,128)(2,1)} %param.13) | copy-start | bytes 3145732
  0.6 66.7 %copy-start.1 = (f32[4096]{0:T(1024)S(1)}, f32[4096]{0:T(1024)}, u32[]{:S(2)}) copy-start(f32[4096]{0:T(1024)} %param.16) | copy-start | bytes 49156
  0.7 66.7 %copy-start.2 = (f32[4096]{0:T(1024)S(1)}, f32[4096]{0:T(1024)}, u32[]{:S(2)}) copy-start(f32[4096]{0:T(1024)} %param.15) | copy-start | bytes 49156
  11.7 23.9 %collective-permute-start.2 = (f32[2,264,128]{2,1,0:T(8,128)S(1)}, f32[2,264,128]{2,1,0:T(8,128)S(1)}, u32[]{:S(2)}, u32[]{:S(2)}) collective-permute-start(f32[2,264,128]{2,1,0:T(8,128)S(1)} %bitcast.15), channel_id=1, source_target_pairs={{0,16},{8,24},{16,0},{24,8},{1,17},{9,25},{17,1},{25,9},{2,18},{10... | collective-permute-start | bytes 811016 | tf_op jit(solution)/shard_map/ppermute | solution.py:276
  13.7 22.0 %collective-permute-start.1 = (f32[2,264,128]{2,1,0:T(8,128)S(1)}, f32[2,264,128]{2,1,0:T(8,128)S(1)}, u32[]{:S(2)}, u32[]{:S(2)}) collective-permute-start(f32[2,264,128]{2,1,0:T(8,128)S(1)} %bitcast.16), channel_id=1, source_target_pairs={{0,24},{8,16},{16,8},{24,0},{1,25},{9,17},{17,9},{25,1},{2,26},{10... | collective-permute-start | bytes 811016 | tf_op jit(solution)/shard_map/ppermute | solution.py:276
  15.6 20.1 %collective-permute-start = (f32[2,264,128]{2,1,0:T(8,128)S(1)}, f32[2,264,128]{2,1,0:T(8,128)S(1)}, u32[]{:S(2)}, u32[]{:S(2)}) collective-permute-start(f32[2,264,128]{2,1,0:T(8,128)S(1)} %bitcast.17), channel_id=1, source_target_pairs={{0,8},{8,0},{16,24},{24,16},{1,9},{9,1},{17,25},{25,17},{2,10},{10... | collective-permute-start | bytes 811016 | tf_op jit(solution)/shard_map/ppermute | solution.py:276
  20.1 15.5 %all-to-all-start = ((f32[16,1,32]{2,1,0:T(1,128)}), f32[16,1,32]{2,1,0:T(1,128)S(1)}, u32[]{:S(2)}, u32[]{:S(2)}) async-start(f32[16,1,32]{2,1,0:T(1,128)} %get-tuple-element.19), calls=%async_computation | async-start | bytes 16384 | tf_op jit(solution)/shard_map/all_to_all | solution.py:228

commit v9 on v8

--- a/solution.py
+++ b/solution.py
@@ -57,7 +57,11 @@
     for copy in copies:
         copy.start()
     copies[0].wait()
-    pot_out[...] = jnp.broadcast_to(pot_here[...][None], (NZ, 1, SHARD))
+    row = jnp.concatenate([pot_here[...], jnp.zeros((1, 128 - SHARD), jnp.float32)], axis=1)
+    row = pltpu.roll(
+        jnp.broadcast_to(row, (8, 128)), lax.rem(lax.axis_index("z"), 4) * SHARD, 1
+    )
+    pot_out[...] = jnp.broadcast_to(row[:1][None], (NZ, 1, 128))
     copies[1].wait()
     copies[2].wait()
     for q in range(AB_J):
@@ -75,9 +79,17 @@
 
 def of_here(array, mine):
     rows = array[pl.ds(lax.shift_right_logical(mine, 2), NZ, stride=2), :]
-    turn = lax.rem(128 - lax.rem(mine, 4) * SHARD, 128)
-    rows = pltpu.roll(rows, turn, 1)
-    return jnp.concatenate([rows[z : z + 1, :SHARD] for z in range(NZ)], axis=1)
+    place = lax.broadcasted_iota(jnp.int32, (NZ, 128), 1) // SHARD
+    plane = lax.broadcasted_iota(jnp.int32, (NZ, 128), 0) % 4
+    placed = jnp.zeros((NZ, 128), jnp.float32)
+    for i in range(4):
+        turn = lax.rem(128 + i * SHARD - lax.rem(mine, 4) * SHARD, 128)
+        here = jnp.logical_and(place == i, plane == i)
+        placed = jnp.where(here, pltpu.roll(rows, turn, 1), placed)
+    rows = placed
+    return jnp.concatenate(
+        [jnp.sum(rows[z : z + 4], axis=0, keepdims=True) for z in range(0, NZ, 4)], axis=1
+    )
 
 
 def tile_kernel(
@@ -86,7 +98,8 @@
     mine = my_block()
     weight = as_columns(of_here(ad_weight, mine))
     pots = jnp.concatenate(
-        [pot_parts[PLANES[0].index(z)] for z in range(NZ)], axis=1
+        [sum(pot_parts[PLANES[0].index(z + i)] for i in range(4)) for z in range(0, NZ, 4)],
+        axis=1,
     ) * TO_UNITS
     pot[...] = pots
     pots = as_columns(pots)
@@ -251,7 +264,7 @@
         message_kernel,
         out_shape=[
             jax.ShapeDtypeStruct((ROWS, 128), jnp.float32),
-            jax.ShapeDtypeStruct((NZ, 1, SHARD), jnp.float32),
+            jax.ShapeDtypeStruct((NZ, 1, 128), jnp.float32),
         ],
         in_specs=[pl.BlockSpec(memory_space=pltpu.HBM)] * 6,
         out_specs=[pl.BlockSpec(memory_space=pltpu.VMEM)] * 2,

time: 97.4 us -> 97.3 us (level)
  no operation moved by 1% of the time
where the time goes in v9:
time: 97.3 us; the launch traced here: 96.8 us
  blocking collectives  64.5 us (66%)
  starting transfers between devices  22.3 us (23%)
  Pallas kernels  6.91 us (7%)
  between operations  1.45 us (1%)
    all_to_all x2, blocking collectives, over_planes(): lax.all_to_all(value, 'z', 0, 0, tiled=True, axis_index_groups=PLANES)  28.7 us
    all_to_all x2, blocking collectives, over_rows(): lax.all_to_all(value, ('y', 'c', 'x'), 0, 0, tiled=True, axis_index_group...  27.1 us
    all_to_all x1, starting transfers between devices, over_planes(): lax.all_to_all(value, 'z', 0, 0, tiled=True, axis_index_groups=PLANES)  14 us
    all_gather x1, blocking collectives, on_device(): pair = lax.all_gather(message, 'c')  8.73 us
    ppermute x3, starting transfers between devices, on_device(): lax.ppermute(pair, 'y', [(i, i ^ d) for i in range(NY)])  8.36 us
    pallas_call x5, Pallas kernels, call(): pl.pallas_call(kernel, out_shape=[jax.ShapeDtypeStruct(s, jnp.float32) fo...  5.3 us
  transfers between devices with their start and end apart: 4, of which 1 were waited for; matrix products, arithmetic and copies ran while one was open for 1% of the time, Pallas kernels for 0%

profile of v9, /device:TPU:1, one launch (start us, length us, event | category | flops | bytes accessed | tf_op | source)
XLA Modules:
  0.0 96.8 jit_solution(58099113006510331)
XLA Ops:
  0.6 0.0 copy-start
  0.6 0.0 copy-start.1
  0.7 0.0 copy-start.2
  1.4 1.6 %shard_map.113 = (f32[264,128]{1,0:T(8,128)}, f32[16,1,128]{2,1,0:T(1,128)}) custom-call(s32[1,1,4]{2,1,0:T(1,128)} %eligible.1, s32[1,1]{1,0:T(1,128)S(6)} %copy.14.counts, bf16[256,128]{1,0:T(8,128)(2,1)} %embedding.1, f32[2,128]{1,0:T(2,128)} %bitcast.22, f32[2,128]{1,0:T(2,128)} %bitcast.23, f32[1,32]{1,0:T(1,128)} %bitcast.24), custom_call_target="tpu_custom_call" | custom-call | tf_op jit(solution)/shard_map/pallas_call | solution.py:263
  3.0 8.7 %all-gather = f32[528,128]{1,0:T(8,128)S(1)} all-gather(f32[264,128]{1,0:T(8,128)} %get-tuple-element.18), channel_id=2, replica_groups=mesh['z'=16,'y'=4,'c'=2,'x'=4] {'c'}, dimensions={0}, use_global_device_ids=true | all-gather | bytes 405504 | tf_op jit(solution)/shard_map/all_gather | solution.py:287
  11.7 1.9 %collective-permute-start.2 = (f32[2,264,128]{2,1,0:T(8,128)S(1)}, f32[2,264,128]{2,1,0:T(8,128)S(1)}, u32[]{:S(2)}, u32[]{:S(2)}) collective-permute-start(f32[2,264,128]{2,1,0:T(8,128)S(1)} %bitcast.15), channel_id=1, source_target_pairs={{0,16},{8,24},{16,0},{24,8},{1,17},{9,25},{17,1},{25,9},{2,18},{10... | collective-permute-start | bytes 811016 | tf_op jit(solution)/shard_map/ppermute | solution.py:289
  13.7 1.9 %collective-permute-start.1 = (f32[2,264,128]{2,1,0:T(8,128)S(1)}, f32[2,264,128]{2,1,0:T(8,128)S(1)}, u32[]{:S(2)}, u32[]{:S(2)}) collective-permute-start(f32[2,264,128]{2,1,0:T(8,128)S(1)} %bitcast.16), channel_id=1, source_target_pairs={{0,24},{8,16},{16,8},{24,0},{1,25},{9,17},{17,9},{25,1},{2,26},{10... | collective-permute-start | bytes 811016 | tf_op jit(solution)/shard_map/ppermute | solution.py:289
  15.6 4.5 %collective-permute-start = (f32[2,264,128]{2,1,0:T(8,128)S(1)}, f32[2,264,128]{2,1,0:T(8,128)S(1)}, u32[]{:S(2)}, u32[]{:S(2)}) collective-permute-start(f32[2,264,128]{2,1,0:T(8,128)S(1)} %bitcast.17), channel_id=1, source_target_pairs={{0,8},{8,0},{16,24},{24,16},{1,9},{9,1},{17,25},{25,17},{2,10},{10... | collective-permute-start | bytes 811016 | tf_op jit(solution)/shard_map/ppermute | solution.py:289
  20.1 14.0 %all-to-all-start = ((f32[16,1,128]{2,1,0:T(1,128)}), f32[16,1,128]{2,1,0:T(1,128)S(1)}, u32[]{:S(2)}, u32[]{:S(2)}) async-start(f32[16,1,128]{2,1,0:T(1,128)} %get-tuple-element.19), calls=%async_computation | async-start | bytes 16384 | tf_op jit(solution)/shard_map/all_to_all | solution.py:241
  34.1 0.7 multiply_bitcast_fusion.ad_weight
  34.8 0.0 copy-done
  34.8 0.8 all-to-all-done.pot_parts
  35.7 0.0 collective-permute-done.2.msg2
  35.7 0.0 collective-permute-done.1.msg3
  35.7 0.0 collective-permute-done.msg1
  35.7 2.0 %shard_map.114 = (f32[512,2048]{1,0:T(8,128)S(1)}, f32[32,8,256]{2,1,0:T(8,128)S(1)}, f32[8,256]{1,0:T(8,128)S(1)}, f32[1,512]{1,0:T(1,128)S(1)}) custom-call(f32[2,264,128]{2,1,0:T(8,128)S(1)} %bitcast.18, f32[2,264,128]{2,1,0:T(8,128)S(1)} %collective-permute-done.msg1, f32[2,264,128]{2,1,0:T(8,128)S(1)} %collective-permute-done.1.msg3, ...), custom_call_target="tpu_custom_call" | custom-call | tf_op jit(solution)/shard_map/pallas_call | solution.py:218
  37.7 14.3 %all_to_all.25.parts = f32[32,8,256]{2,1,0:T(8,128)S(1)} all-to-all(f32[32,8,256]{2,1,0:T(8,128)S(1)} %get-tuple-element.21), channel_id=1, replica_groups={{22,23,20,21,18,19,16,17,30,31,28,29,26,27,24,25,6,7,4,5,2,3,0,1,14,15,..., dimensions={0} | all-to-all | bytes 524288 | tf_op jit(solution)/shard_map/all_to_all | solution.py:245
  52.0 0.8 shard_map.115
  52.8 14.4 %all_to_all.26.parts = f32[16,1,512]{2,1,0:T(1,128)S(1)} all-to-all(f32[16,1,512]{2,1,0:T(1,128)S(1)} %get-tuple-element.24), channel_id=1, replica_groups={{256,480,192,416,128,352,64,288,0,224,448,160,384,96,320,32},{257,481,1..., dimensions={0} | all-to-all | bytes 65536 | tf_op jit(solution)/shard_map/all_to_all | solution.py:241
  67.2 0.0 copy-done.1
  67.2 0.0 copy-done.2
  67.2 1.0 %shard_map.116 = (f32[1,512]{1,0:T(1,128)S(1)}, f32[32,8,256]{2,1,0:T(8,128)S(1)}, f32[1,512]{1,0:T(1,128)S(1)}, f32[1,512]{1,0:T(1,128)S(1)}) custom-call(f32[512,2048]{1,0:T(8,128)S(1)} %get-tuple-element.20.tile, f32[16,1,512]{2,1,0:T(1,128)S(1)} %all_to_all.26.parts, f32[8,256]{1,0:T(8,128)S(1)} %get-tuple-element.25.row_pot, ...), custom_call_target="tpu_custom_call" | custom-call | tf_op jit(solution)/shard_map/pallas_call | solution.py:218
  68.3 12.8 %all_to_all.27.parts = f32[32,8,256]{2,1,0:T(8,128)S(1)} all-to-all(f32[32,8,256]{2,1,0:T(8,128)S(1)} %get-tuple-element.26), channel_id=1, replica_groups={{22,23,20,21,18,19,16,17,30,31,28,29,26,27,24,25,6,7,4,5,2,3,0,1,14,15,..., dimensions={0} | all-to-all | bytes 524288 | tf_op jit(solution)/shard_map/all_to_all | solution.py:245
  81.1 0.8 shard_map.117
  81.9 14.2 %all_to_all.28.parts = f32[16,1,512]{2,1,0:T(1,128)S(1)} all-to-all(f32[16,1,512]{2,1,0:T(1,128)S(1)} %get-tuple-element.28), channel_id=1, replica_groups={{256,480,192,416,128,352,64,288,0,224,448,160,384,96,320,32},{257,481,1..., dimensions={0} | all-to-all | bytes 65536 | tf_op jit(solution)/shard_map/all_to_all | solution.py:241
  96.1 0.6 shard_map.118
  (1 shorter events, 0.0 us)
Async XLA Ops:
  0.6 34.2 %copy-start = (bf16[4096,128]{1,0:T(8,128)(2,1)S(1)}, bf16[4096,128]{1,0:T(8,128)(2,1)}, u32[]{:S(2)}) copy-start(bf16[4096,128]{1,0:T(8,128)(2,1)} %param.13) | copy-start | bytes 3145732
  0.6 66.6 %copy-start.1 = (f32[4096]{0:T(1024)S(1)}, f32[4096]{0:T(1024)}, u32[]{:S(2)}) copy-start(f32[4096]{0:T(1024)} %param.16) | copy-start | bytes 49156
  0.7 66.6 %copy-start.2 = (f32[4096]{0:T(1024)S(1)}, f32[4096]{0:T(1024)}, u32[]{:S(2)}) copy-start(f32[4096]{0:T(1024)} %param.15) | copy-start | bytes 49156
  11.7 23.9 %collective-permute-start.2 = (f32[2,264,128]{2,1,0:T(8,128)S(1)}, f32[2,264,128]{2,1,0:T(8,128)S(1)}, u32[]{:S(2)}, u32[]{:S(2)}) collective-permute-start(f32[2,264,128]{2,1,0:T(8,128)S(1)} %bitcast.15), channel_id=1, source_target_pairs={{0,16},{8,24},{16,0},{24,8},{1,17},{9,25},{17,1},{25,9},{2,18},{10... | collective-permute-start | bytes 811016 | tf_op jit(solution)/shard_map/ppermute | solution.py:289
  13.7 22.0 %collective-permute-start.1 = (f32[2,264,128]{2,1,0:T(8,128)S(1)}, f32[2,264,128]{2,1,0:T(8,128)S(1)}, u32[]{:S(2)}, u32[]{:S(2)}) collective-permute-start(f32[2,264,128]{2,1,0:T(8,128)S(1)} %bitcast.16), channel_id=1, source_target_pairs={{0,24},{8,16},{16,8},{24,0},{1,25},{9,17},{17,9},{25,1},{2,26},{10... | collective-permute-start | bytes 811016 | tf_op jit(solution)/shard_map/ppermute | solution.py:289
  15.6 20.1 %collective-permute-start = (f32[2,264,128]{2,1,0:T(8,128)S(1)}, f32[2,264,128]{2,1,0:T(8,128)S(1)}, u32[]{:S(2)}, u32[]{:S(2)}) collective-permute-start(f32[2,264,128]{2,1,0:T(8,128)S(1)} %bitcast.17), channel_id=1, source_target_pairs={{0,8},{8,0},{16,24},{24,16},{1,9},{9,1},{17,25},{25,17},{2,10},{10... | collective-permute-start | bytes 811016 | tf_op jit(solution)/shard_map/ppermute | solution.py:289
  20.1 15.5 %all-to-all-start = ((f32[16,1,128]{2,1,0:T(1,128)}), f32[16,1,128]{2,1,0:T(1,128)S(1)}, u32[]{:S(2)}, u32[]{:S(2)}) async-start(f32[16,1,128]{2,1,0:T(1,128)} %get-tuple-element.19), calls=%async_computation | async-start | bytes 16384 | tf_op jit(solution)/shard_map/all_to_all | solution.py:241

commit v10 on v9

--- a/solution.py
+++ b/solution.py
@@ -118,10 +118,12 @@
             peaks, totals = [], []
             for q in range(AB_J):
                 rows = slice(q * PART_HERE, (q + 1) * PART_HERE)
-                product = lax.dot_general(
-                    ads[rows, :], users, (((1,), (1,)), ((), ())),
-                    preferred_element_type=jnp.float32,
-                )
+                if q % 2 == 0:
+                    products = lax.dot_general(
+                        ads[q * PART_HERE : q * PART_HERE + 256, :], users, (((1,), (1,)), ((), ())),
+                        preferred_element_type=jnp.float32,
+                    )
+                product = products[q % 2 * PART_HERE : (q % 2 + 1) * PART_HERE]
                 bias = msg[c, UBS + 4 + q : UBS + 5 + q, :]
                 bias = jnp.concatenate([bias, bias], axis=1)
                 wide = jnp.concatenate([weight[rows], weight[rows]], axis=1)

time: 97.3 us -> 97.3 us (level)
  no operation moved by 1% of the time
where the time goes in v10:
time: 97.3 us; the launch traced here: 96.8 us
  blocking collectives  64.5 us (66%)
  starting transfers between devices  22.3 us (23%)
  Pallas kernels  6.92 us (7%)
  between operations  1.45 us (1%)
    all_to_all x2, blocking collectives, over_planes(): lax.all_to_all(value, 'z', 0, 0, tiled=True, axis_index_groups=PLANES)  28.7 us
    all_to_all x2, blocking collectives, over_rows(): lax.all_to_all(value, ('y', 'c', 'x'), 0, 0, tiled=True, axis_index_group...  27.1 us
    all_to_all x1, starting transfers between devices, over_planes(): lax.all_to_all(value, 'z', 0, 0, tiled=True, axis_index_groups=PLANES)  14 us
    all_gather x1, blocking collectives, on_device(): pair = lax.all_gather(message, 'c')  8.73 us
    ppermute x3, starting transfers between devices, on_device(): lax.ppermute(pair, 'y', [(i, i ^ d) for i in range(NY)])  8.36 us
    pallas_call x5, Pallas kernels, call(): pl.pallas_call(kernel, out_shape=[jax.ShapeDtypeStruct(s, jnp.float32) fo...  5.32 us
  transfers between devices with their start and end apart: 4, of which 1 were waited for; matrix products, arithmetic and copies ran while one was open for 1% of the time, Pallas kernels for 0%

profile of v10, /device:TPU:1, one launch (start us, length us, event | category | flops | bytes accessed | tf_op | source)
XLA Modules:
  0.0 96.8 jit_solution(18317544661453017435)
XLA Ops:
  0.6 0.0 copy-start
  0.6 0.0 copy-start.1
  0.7 0.0 copy-start.2
  1.4 1.6 %shard_map.113 = (f32[264,128]{1,0:T(8,128)}, f32[16,1,128]{2,1,0:T(1,128)}) custom-call(s32[1,1,4]{2,1,0:T(1,128)} %eligible.1, s32[1,1]{1,0:T(1,128)S(6)} %copy.14.counts, bf16[256,128]{1,0:T(8,128)(2,1)} %embedding.1, f32[2,128]{1,0:T(2,128)} %bitcast.22, f32[2,128]{1,0:T(2,128)} %bitcast.23, f32[1,32]{1,0:T(1,128)} %bitcast.24), custom_call_target="tpu_custom_call" | custom-call | tf_op jit(solution)/shard_map/pallas_call | solution.py:265
  3.0 8.7 %all-gather = f32[528,128]{1,0:T(8,128)S(1)} all-gather(f32[264,128]{1,0:T(8,128)} %get-tuple-element.18), channel_id=2, replica_groups=mesh['z'=16,'y'=4,'c'=2,'x'=4] {'c'}, dimensions={0}, use_global_device_ids=true | all-gather | bytes 405504 | tf_op jit(solution)/shard_map/all_gather | solution.py:289
  11.7 1.9 %collective-permute-start.2 = (f32[2,264,128]{2,1,0:T(8,128)S(1)}, f32[2,264,128]{2,1,0:T(8,128)S(1)}, u32[]{:S(2)}, u32[]{:S(2)}) collective-permute-start(f32[2,264,128]{2,1,0:T(8,128)S(1)} %bitcast.15), channel_id=1, source_target_pairs={{0,16},{8,24},{16,0},{24,8},{1,17},{9,25},{17,1},{25,9},{2,18},{10... | collective-permute-start | bytes 811016 | tf_op jit(solution)/shard_map/ppermute | solution.py:291
  13.7 1.9 %collective-permute-start.1 = (f32[2,264,128]{2,1,0:T(8,128)S(1)}, f32[2,264,128]{2,1,0:T(8,128)S(1)}, u32[]{:S(2)}, u32[]{:S(2)}) collective-permute-start(f32[2,264,128]{2,1,0:T(8,128)S(1)} %bitcast.16), channel_id=1, source_target_pairs={{0,24},{8,16},{16,8},{24,0},{1,25},{9,17},{17,9},{25,1},{2,26},{10... | collective-permute-start | bytes 811016 | tf_op jit(solution)/shard_map/ppermute | solution.py:291
  15.6 4.5 %collective-permute-start = (f32[2,264,128]{2,1,0:T(8,128)S(1)}, f32[2,264,128]{2,1,0:T(8,128)S(1)}, u32[]{:S(2)}, u32[]{:S(2)}) collective-permute-start(f32[2,264,128]{2,1,0:T(8,128)S(1)} %bitcast.17), channel_id=1, source_target_pairs={{0,8},{8,0},{16,24},{24,16},{1,9},{9,1},{17,25},{25,17},{2,10},{10... | collective-permute-start | bytes 811016 | tf_op jit(solution)/shard_map/ppermute | solution.py:291
  20.1 14.0 %all-to-all-start = ((f32[16,1,128]{2,1,0:T(1,128)}), f32[16,1,128]{2,1,0:T(1,128)S(1)}, u32[]{:S(2)}, u32[]{:S(2)}) async-start(f32[16,1,128]{2,1,0:T(1,128)} %get-tuple-element.19), calls=%async_computation | async-start | bytes 16384 | tf_op jit(solution)/shard_map/all_to_all | solution.py:243
  34.1 0.7 multiply_bitcast_fusion.ad_weight
  34.8 0.0 copy-done
  34.8 0.8 all-to-all-done.pot_parts
  35.7 0.0 collective-permute-done.2.msg2
  35.7 0.0 collective-permute-done.1.msg3
  35.7 0.0 collective-permute-done.msg1
  35.7 2.0 %shard_map.114 = (f32[512,2048]{1,0:T(8,128)S(1)}, f32[32,8,256]{2,1,0:T(8,128)S(1)}, f32[8,256]{1,0:T(8,128)S(1)}, f32[1,512]{1,0:T(1,128)S(1)}) custom-call(f32[2,264,128]{2,1,0:T(8,128)S(1)} %bitcast.18, f32[2,264,128]{2,1,0:T(8,128)S(1)} %collective-permute-done.msg1, f32[2,264,128]{2,1,0:T(8,128)S(1)} %collective-permute-done.1.msg3, ...), custom_call_target="tpu_custom_call" | custom-call | tf_op jit(solution)/shard_map/pallas_call | solution.py:220
  37.7 14.3 %all_to_all.25.parts = f32[32,8,256]{2,1,0:T(8,128)S(1)} all-to-all(f32[32,8,256]{2,1,0:T(8,128)S(1)} %get-tuple-element.21), channel_id=1, replica_groups={{22,23,20,21,18,19,16,17,30,31,28,29,26,27,24,25,6,7,4,5,2,3,0,1,14,15,..., dimensions={0} | all-to-all | bytes 524288 | tf_op jit(solution)/shard_map/all_to_all | solution.py:247
  52.0 0.8 shard_map.115
  52.8 14.4 %all_to_all.26.parts = f32[16,1,512]{2,1,0:T(1,128)S(1)} all-to-all(f32[16,1,512]{2,1,0:T(1,128)S(1)} %get-tuple-element.24), channel_id=1, replica_groups={{256,480,192,416,128,352,64,288,0,224,448,160,384,96,320,32},{257,481,1..., dimensions={0} | all-to-all | bytes 65536 | tf_op jit(solution)/shard_map/all_to_all | solution.py:243
  67.2 0.0 copy-done.1
  67.2 0.0 copy-done.2
  67.2 1.0 %shard_map.116 = (f32[1,512]{1,0:T(1,128)S(1)}, f32[32,8,256]{2,1,0:T(8,128)S(1)}, f32[1,512]{1,0:T(1,128)S(1)}, f32[1,512]{1,0:T(1,128)S(1)}) custom-call(f32[512,2048]{1,0:T(8,128)S(1)} %get-tuple-element.20.tile, f32[16,1,512]{2,1,0:T(1,128)S(1)} %all_to_all.26.parts, f32[8,256]{1,0:T(8,128)S(1)} %get-tuple-element.25.row_pot, ...), custom_call_target="tpu_custom_call" | custom-call | tf_op jit(solution)/shard_map/pallas_call | solution.py:220
  68.3 12.8 %all_to_all.27.parts = f32[32,8,256]{2,1,0:T(8,128)S(1)} all-to-all(f32[32,8,256]{2,1,0:T(8,128)S(1)} %get-tuple-element.26), channel_id=1, replica_groups={{22,23,20,21,18,19,16,17,30,31,28,29,26,27,24,25,6,7,4,5,2,3,0,1,14,15,..., dimensions={0} | all-to-all | bytes 524288 | tf_op jit(solution)/shard_map/all_to_all | solution.py:247
  81.1 0.8 shard_map.117
  81.9 14.2 %all_to_all.28.parts = f32[16,1,512]{2,1,0:T(1,128)S(1)} all-to-all(f32[16,1,512]{2,1,0:T(1,128)S(1)} %get-tuple-element.28), channel_id=1, replica_groups={{256,480,192,416,128,352,64,288,0,224,448,160,384,96,320,32},{257,481,1..., dimensions={0} | all-to-all | bytes 65536 | tf_op jit(solution)/shard_map/all_to_all | solution.py:243
  96.1 0.6 shard_map.118
  (1 shorter events, 0.0 us)
Async XLA Ops:
  0.6 34.2 %copy-start = (bf16[4096,128]{1,0:T(8,128)(2,1)S(1)}, bf16[4096,128]{1,0:T(8,128)(2,1)}, u32[]{:S(2)}) copy-start(bf16[4096,128]{1,0:T(8,128)(2,1)} %param.13) | copy-start | bytes 3145732
  0.6 66.6 %copy-start.1 = (f32[4096]{0:T(1024)S(1)}, f32[4096]{0:T(1024)}, u32[]{:S(2)}) copy-start(f32[4096]{0:T(1024)} %param.16) | copy-start | bytes 49156
  0.7 66.6 %copy-start.2 = (f32[4096]{0:T(1024)S(1)}, f32[4096]{0:T(1024)}, u32[]{:S(2)}) copy-start(f32[4096]{0:T(1024)} %param.15) | copy-start | bytes 49156
  11.7 23.9 %collective-permute-start.2 = (f32[2,264,128]{2,1,0:T(8,128)S(1)}, f32[2,264,128]{2,1,0:T(8,128)S(1)}, u32[]{:S(2)}, u32[]{:S(2)}) collective-permute-start(f32[2,264,128]{2,1,0:T(8,128)S(1)} %bitcast.15), channel_id=1, source_target_pairs={{0,16},{8,24},{16,0},{24,8},{1,17},{9,25},{17,1},{25,9},{2,18},{10... | collective-permute-start | bytes 811016 | tf_op jit(solution)/shard_map/ppermute | solution.py:291
  13.7 22.0 %collective-permute-start.1 = (f32[2,264,128]{2,1,0:T(8,128)S(1)}, f32[2,264,128]{2,1,0:T(8,128)S(1)}, u32[]{:S(2)}, u32[]{:S(2)}) collective-permute-start(f32[2,264,128]{2,1,0:T(8,128)S(1)} %bitcast.16), channel_id=1, source_target_pairs={{0,24},{8,16},{16,8},{24,0},{1,25},{9,17},{17,9},{25,1},{2,26},{10... | collective-permute-start | bytes 811016 | tf_op jit(solution)/shard_map/ppermute | solution.py:291
  15.6 20.1 %collective-permute-start = (f32[2,264,128]{2,1,0:T(8,128)S(1)}, f32[2,264,128]{2,1,0:T(8,128)S(1)}, u32[]{:S(2)}, u32[]{:S(2)}) collective-permute-start(f32[2,264,128]{2,1,0:T(8,128)S(1)} %bitcast.17), channel_id=1, source_target_pairs={{0,8},{8,0},{16,24},{24,16},{1,9},{9,1},{17,25},{25,17},{2,10},{10... | collective-permute-start | bytes 811016 | tf_op jit(solution)/shard_map/ppermute | solution.py:291
  20.1 15.5 %all-to-all-start = ((f32[16,1,128]{2,1,0:T(1,128)}), f32[16,1,128]{2,1,0:T(1,128)S(1)}, u32[]{:S(2)}, u32[]{:S(2)}) async-start(f32[16,1,128]{2,1,0:T(1,128)} %get-tuple-element.19), calls=%async_computation | async-start | bytes 16384 | tf_op jit(solution)/shard_map/all_to_all | solution.py:243
